TPU v7x, 256 devices: a whole 4x4x8 slice. The times are simulated.
256 devices in a mesh: patch: 16 (over x, y_lo, core), var: 16 (over z, y_hi).
Axes of the slice: x: 4, y: 4 (y_hi: 2, y_lo: 2; y = y_hi * 2 + y_lo), z: 8, core: 2. Of those that a mesh axis runs over, the one named last changes fastest.
Arguments:
- fields: bfloat16 [32, 48, 4, 1024], P(None, 'var', None, 'patch'), may hold values from -8 to 8
- var_ids: int32 [48], replicated, may hold values from 0 to 47, each once
- lead_index: int32 [32], P('var'), may hold values from 0 to 15
- embed_weight: bfloat16 [48, 4, 1024], replicated, may hold values from -3 to 3
- var_embed: bfloat16 [48, 1024], replicated, may hold values from -3 to 3
- agg_query: bfloat16 [1024], replicated, may hold values from -28 to 28
- agg_key: bfloat16 [1024, 1024], replicated, may hold values from -0.1875 to 0.1875
- agg_value: bfloat16 [1024, 1024], replicated, may hold values from -0.1875 to 0.1875
- agg_out: bfloat16 [1024, 1024], replicated, may hold values from -0.1875 to 0.1875
- pos_embed: bfloat16 [1024, 1024], P('patch'), may hold values from -3 to 6
- lead_table: bfloat16 [16, 1024], replicated, may hold values from -3 to 3
- norm_gain: bfloat16 [1024], replicated, may hold values from 0.099609375 to 1.8984375
- qkv_weight: bfloat16 [3, 1024, 1024], P(None, None, 'patch'), may hold values from -0.5 to 0.5
- out_weight: bfloat16 [1024, 1024], replicated, may hold values from -0.1875 to 0.1875
- cotangent: bfloat16 [32, 1024, 1024], P('var', 'patch'), may hold values from -0.3125 to 0.3125
Outputs:
- layer_out: bfloat16 [32, 1024, 1024], P('var', 'patch')
- grad_qkv: float32 [3, 1024, 1024], P(None, 'var', 'patch')
Inputs may be any that keep to these rules, and one draw needn't show every extreme that they name: `var_ids`: each variable id stands in exactly one slot.
All inputs are finite; a program needn't handle non-finite values.
Results may differ from a plain program's by a relative error of at most 0.015.
The roundings to bfloat16 on the way count: a program that leaves them out, or rounds other values in their place, can miss the bound.
Values may be sent and summed in bfloat16 or wider, within the bound.
No kernel may reach another device: no remote copies, remote signals or barrier semaphores. Data moves between devices by JAX's collectives and lax.ppermute only.
A program may use at most 128 MiB of HBM per device.

v0:
```python
import jax
import jax.numpy as jnp
from jax import lax
from jax.sharding import PartitionSpec as P

H = 16
HD = 64


def layer_norm(tokens, norm_gain):
    center = tokens - jnp.mean(tokens, axis=-1, keepdims=True)
    spread = jnp.mean(center * center, axis=-1, keepdims=True)
    return (center * lax.rsqrt(spread + 1e-05) * norm_gain.astype(jnp.float32)).astype(jnp.bfloat16)


def on_device(
    fields,
    var_ids,
    lead_index,
    embed_weight,
    var_embed,
    agg_query,
    agg_key,
    agg_value,
    agg_out,
    pos_embed,
    lead_table,
    norm_gain,
    qkv_weight,
    out_weight,
    cotangent,
):
    highest = lax.Precision.HIGHEST
    scaling = HD ** (-0.5)
    owned = lax.all_to_all(fields, "var", split_axis=0, concat_axis=1, tiled=True)
    samples, slots, pixels, patches = owned.shape
    width = agg_out.shape[0]
    onehot = (var_ids[:, None] == jnp.arange(slots)[None, :]).astype(jnp.float32)
    table = jnp.concatenate(
        [embed_weight.astype(jnp.float32), var_embed.astype(jnp.float32)[:, None, :]], axis=1
    )
    table = jnp.einsum("vn,nkd->vkd", onehot, table, precision=highest)
    query_heads = agg_query.astype(jnp.float32).reshape(H, HD) * scaling
    key_query = jnp.einsum(
        "dhe,he->dh",
        agg_key.astype(jnp.float32).reshape(width, H, HD),
        query_heads,
        precision=highest,
    )
    score_table = jnp.einsum("vkd,dh->vkh", table, key_query, precision=highest)
    value_table = jnp.einsum(
        "vkd,de->vke", table, agg_value.astype(jnp.float32), precision=highest
    ).reshape(slots, pixels + 1, H, HD)
    padded = jnp.concatenate(
        [owned.astype(jnp.float32), jnp.ones((samples, slots, 1, patches), jnp.float32)], axis=2
    )
    agg_scores = jnp.einsum("bvkp,vkh->bvhp", padded, score_table, precision=highest)
    agg_probs = jax.nn.softmax(agg_scores, axis=1)
    mixing = agg_probs[:, :, None, :, :] * padded[:, :, :, None, :]
    pooled = (
        jnp.einsum("bvkhp,vkhe->bphe", mixing, value_table, precision=highest)
        .reshape(samples, patches, width)
        .astype(jnp.bfloat16)
    )
    lead_hot = (lead_index[:, None] == jnp.arange(lead_table.shape[0])[None, :]).astype(jnp.float32)
    lead_rows = jnp.dot(lead_hot, lead_table.astype(jnp.float32), precision=highest)
    tokens = jnp.einsum("bpd,de->bpe", pooled, agg_out, preferred_element_type=jnp.float32)
    tokens = tokens + pos_embed.astype(jnp.float32)[None] + lead_rows[:, None, :]
    normed = layer_norm(tokens, norm_gain)
    columns = qkv_weight.shape[2]
    head_count = columns // HD
    everyone = lax.all_gather(normed, "patch", axis=1, tiled=True)
    head_qkv = jnp.einsum(
        "bpd,ide->ibpe", everyone, qkv_weight, preferred_element_type=jnp.float32
    ).astype(jnp.bfloat16)
    length = head_qkv.shape[2]
    queries = head_qkv[0].reshape(samples, length, head_count, HD)
    key_rows = head_qkv[1].reshape(samples, length, head_count, HD)
    value_rows = head_qkv[2].reshape(samples, length, head_count, HD)
    scores = (
        jnp.einsum("bqhe,bkhe->bhqk", queries, key_rows, preferred_element_type=jnp.float32)
        * scaling
    )
    att_probs = jax.nn.softmax(scores, axis=-1)
    probs_low = att_probs.astype(jnp.bfloat16)
    context = jnp.einsum(
        "bhqk,bkhe->bqhe", probs_low, value_rows, preferred_element_type=jnp.float32
    ).astype(jnp.bfloat16)
    merged = lax.all_to_all(
        context.reshape(samples, length, columns), "patch", split_axis=1, concat_axis=2, tiled=True
    )
    layer_out = (
        tokens + jnp.einsum("bpd,de->bpe", merged, out_weight, preferred_element_type=jnp.float32)
    ).astype(jnp.bfloat16)
    grad_context = jnp.einsum(
        "bpe,de->bpd", cotangent, out_weight, preferred_element_type=jnp.float32
    ).astype(jnp.bfloat16)
    grad_heads = lax.all_to_all(
        grad_context, "patch", split_axis=2, concat_axis=1, tiled=True
    ).reshape(samples, length, head_count, HD)
    grad_probs = jnp.einsum(
        "bqhe,bkhe->bhqk", grad_heads, value_rows, preferred_element_type=jnp.float32
    )
    grad_values = jnp.einsum(
        "bhqk,bqhe->bkhe", probs_low, grad_heads, preferred_element_type=jnp.float32
    ).astype(jnp.bfloat16)
    grad_scores = (
        att_probs * (grad_probs - jnp.sum(att_probs * grad_probs, axis=-1, keepdims=True)) * scaling
    ).astype(jnp.bfloat16)
    grad_queries = jnp.einsum(
        "bhqk,bkhe->bqhe", grad_scores, key_rows, preferred_element_type=jnp.float32
    ).astype(jnp.bfloat16)
    grad_keys = jnp.einsum(
        "bhqk,bqhe->bkhe", grad_scores, queries, preferred_element_type=jnp.float32
    ).astype(jnp.bfloat16)
    stacked = jnp.stack([grad_queries, grad_keys, grad_values]).reshape(3, samples, length, columns)
    partial_grad = jnp.einsum(
        "bpd,ibpe->ide", everyone, stacked, preferred_element_type=jnp.float32
    )
    grad_qkv = lax.psum_scatter(partial_grad, "var", scatter_dimension=1, tiled=True)
    return (layer_out, grad_qkv)


def solution(mesh):
    in_specs = (
        P(None, "var", None, "patch"),
        P(),
        P("var"),
        P(),
        P(),
        P(),
        P(),
        P(),
        P(),
        P("patch", None),
        P(),
        P(),
        P(None, None, "patch"),
        P(),
        P("var", "patch", None),
    )
    out_specs = (P("var", "patch", None), P(None, "var", "patch"))
    return jax.shard_map(
        on_device, mesh=mesh, in_specs=in_specs, out_specs=out_specs, check_vma=False
    )
```

profile of v0, /device:TPU:1, one launch (start us, length us, event | category | flops | bytes accessed | tf_op | source)
XLA Modules:
  0.0 358.5 jit_solution(16505109508012951951)
XLA Ops:
  7.2 1.8 reshape.139
  9.0 11.7 %all-to-all-start = ((bf16[16,2,768]{2,1,0:T(2,128)(2,1)}), bf16[16,2,768]{2,1,0:T(2,128)(2,1)S(1)}, u32[]{:S(2)}, u32[]{:S(2)}) async-start(bf16[16,2,768]{2,1,0:T(2,128)(2,1)} %reshape.139), calls=%async_computation | async-start | bytes 98304 | tf_op jit(solution)/shard_map/all_to_all | solution.py:35
  20.8 1.6 convert_element_type.101
  24.3 4.0 %copy.78 = bf16[1024,1024]{0,1:T(8,128)(2,1)} copy(bf16[1024,1024]{1,0:T(8,128)(2,1)} %param.21) | data formatting | bytes 4194304 | tf_op args[6]
  29.2 2.5 fusion.135
  31.7 1.2 fusion.107
  33.0 4.3 %fusion.27 = f32[48,5,1024]{2,0,1:T(8,128)} fusion(f32[48,5,1024]{2,0,1:T(8,128)S(1)} %fusion.107, bf16[1024,1024]{1,0:T(8,128)(2,1)} %param.22), kind=kOutput, calls=%fused_computation.24 | convolution fusion | flops 3019898880 | bytes 4063232 | tf_op jit(solution)/shard_map/vkd,de->vke/dot_general | solution.py:51
  37.2 1.4 convolution_bitcast_fusion.1
  38.8 2.8 reshape.115
  43.1 5.6 %fusion.55 = bf16[2,64,16,64]{1,3,0,2:T(8,128)(2,1)S(1)} fusion(f32[2,48,5,64]{3,1,2,0:T(8,128)S(1)} %get-tuple-element.13, f32[2,48,16,64]{3,1,0,2:T(8,128)S(1)} %copy.83, f32[48,5,16,64,1]{3,2,0,1,4:T(8,128)} %bitcast.167), kind=kOutput, calls=%fused_computation.39 | convolution fusion | flops 378109952 | bytes 1761280 | tf_op jit(solution)/shard_map/bvkhp,vkhe->bphe/dot_general | solution.py:61
  49.6 2.1 fusion.133
  53.0 1.8 fusion.81
  55.6 12.7 %all_to_all.42 = bf16[16,2,4096]{2,1,0:T(2,128)(2,1)} all-to-all(bf16[16,2,4096]{2,1,0:T(2,128)(2,1)S(1)} %reshape.143), channel_id=1, replica_groups=mesh['patch'=16,'var'=16] {'patch'}, dimensions={0} | all-to-all | bytes 524288 | tf_op jit(solution)/shard_map/all_to_all | solution.py:98
  68.3 1.3 reshape.144
  69.6 1.1 copy.131
  70.8 1.5 reshape.121
  72.2 22.6 %all-gather.2.cloned.1.call-done = bf16[2,1024,1024]{2,1,0:T(8,128)(2,1)} async-done(((bf16[2,64,1024]{2,1,0:T(8,128)(2,1)}), bf16[2,1024,1024]{2,1,0:T(8,128)(2,1)}) %all-gather.2.cloned.1.call-update) | async-done | bytes 4194320 | tf_op jit(solution)/shard_map/all_gather | solution.py:72
  94.9 4.7 %fusion.49 = bf16[3,2,1024,64]{2,3,0,1:T(8,128)(2,1)} fusion(bf16[2,1024,1024]{2,1,0:T(8,128)(2,1)} %all-gather.2.cloned.1.call-done, bf16[3,1024,64]{1,2,0:T(8,128)(2,1)} %param.27), kind=kOutput, calls=%fused_computation.36 | convolution fusion | flops 805699584 | bytes 5373952 | tf_op jit(solution)/shard_map/bpd,ide->ibpe/dot_general | solution.py:73
  99.5 6.9 %fusion.134 = (f32[2,1024]{1,0:T(2,128)S(1)}, f32[2,1024,1024]{1,2,0:T(8,128)}) fusion(bf16[3,2,1024,64]{2,3,0,1:T(8,128)(2,1)} %fusion.49), kind=kOutput, calls=%fused_computation.101 | convolution fusion | flops 274727936 | bytes 8921088 | tf_op jit(solution)/shard_map/sub | solution.py:84
  106.5 5.6 %fusion.112 = f32[2,1024,1024]{1,2,0:T(8,128)} fusion(bf16[2,1024,64]{1,2,0:T(8,128)(2,1)S(1)} %reshape.121, bf16[3,2,1024,64]{2,3,0,1:T(8,128)(2,1)} %fusion.49), kind=kOutput, calls=%fused_computation.75 | convolution fusion | flops 268435456 | bytes 8912896 | tf_op jit(solution)/shard_map/bqhe,bkhe->bhqk/dot_general | solution.py:101
  112.1 2.1 fusion.87
  114.2 14.4 %fusion.93 = bf16[1,2,1024,1,64]{2,4,1,3,0:T(8,128)(2,1)} fusion(f32[2,1024,1024]{1,2,0:T(8,128)} %fusion.112, bf16[3,2,1024,64]{2,3,0,1:T(8,128)(2,1)} %fusion.49, f32[2,1024,1024]{1,2,0:T(8,128)} %get-tuple-element.19, f32[2,1024]{1,0:T(2,128)S(1)} %get-tuple-element.18), kind=kOutput, calls=%fused_computation.51 | convolution fusion | flops 283249664 | bytes 34095104 | tf_op jit(solution)/shard_map/bhqk,bqhe->bkhe/dot_general | solution.py:113
  128.5 14.5 %fusion.96 = bf16[1,2,1024,1,64]{2,4,1,3,0:T(8,128)(2,1)} fusion(f32[2,1024,1024]{1,2,0:T(8,128)} %fusion.112, bf16[3,2,1024,64]{2,3,0,1:T(8,128)(2,1)} %fusion.49, f32[2,1024,1024]{1,2,0:T(8,128)} %get-tuple-element.19, f32[2,1024]{1,0:T(2,128)S(1)} %get-tuple-element.18), kind=kOutput, calls=%fused_computation.52 | convolution fusion | flops 283249664 | bytes 34095104 | tf_op jit(solution)/shard_map/bhqk,bkhe->bqhe/dot_general | solution.py:110
  143.1 3.4 fusion.52
  146.5 1.8 copy.110
  148.3 3.6 %reshape.137 = f32[1024,192]{1,0:T(8,128)} reshape(f32[1024,3,64]{2,1,0:T(4,128)} %bitcast.166) | data formatting | bytes 1572864
  151.9 4.3 %fusion.90 = bf16[2,1024,64]{1,2,0:T(8,128)(2,1)S(1)} fusion(bf16[3,2,1024,64]{2,3,0,1:T(8,128)(2,1)} %fusion.49, f32[2,1024,1024]{1,2,0:T(8,128)} %get-tuple-element.19, f32[2,1024]{1,0:T(2,128)S(1)} %get-tuple-element.18), kind=kOutput, calls=%fused_computation.50 | convolution fusion | flops 272760832 | bytes 8921088 | tf_op jit(solution)/shard_map/bhqk,bkhe->bqhe/dot_general | solution.py:86
  157.1 11.7 %all_to_all.43 = bf16[16,2,4096]{2,1,0:T(2,128)(2,1)} all-to-all(bf16[16,2,4096]{2,1,0:T(2,128)(2,1)S(1)} %reshape.141), channel_id=1, replica_groups=mesh['patch'=16,'var'=16] {'patch'}, dimensions={0} | all-to-all | bytes 524288 | tf_op jit(solution)/shard_map/all_to_all | solution.py:89
  168.8 1.3 reshape.142
  171.2 1.4 all_to_all.35
  172.7 1.2 fusion.84
  173.8 176.3 %reduce-scatter.4.cloned.1.call-done = f32[64,192]{1,0:T(8,128)} async-done(((f32[1024,192]{1,0:T(8,128)}), f32[64,192]{1,0:T(8,128)}) %reduce-scatter.4.cloned.1.call-update) | async-done | bytes 49168
  (38 shorter events, 11.0 us)
Async XLA Ops:
  7.2 45.9 %copy-start = (bf16[1024,1024]{1,0:T(8,128)(2,1)S(1)}, bf16[1024,1024]{1,0:T(8,128)(2,1)}, u32[]{:S(2)}) copy-start(bf16[1024,1024]{1,0:T(8,128)(2,1)} %param.28) | copy-start | bytes 6291460
  9.0 32.6 %all-to-all-start = ((bf16[16,2,768]{2,1,0:T(2,128)(2,1)}), bf16[16,2,768]{2,1,0:T(2,128)(2,1)S(1)}, u32[]{:S(2)}, u32[]{:S(2)}) async-start(bf16[16,2,768]{2,1,0:T(2,128)(2,1)} %reshape.139), calls=%async_computation | async-start | bytes 98304 | tf_op jit(solution)/shard_map/all_to_all | solution.py:35
  20.7 74.1 %all-gather.2.cloned.1.call-start = ((), (), s32[]{:S(2)}) async-start(), calls=%async_computation.4 | async-start | bytes 4456448 | tf_op jit(solution)/shard_map/all_gather | solution.py:72
  22.4 19.2 %copy-start.1 = (bf16[1024]{0:T(1024)(128)(2,1)S(1)}, bf16[1024]{0:T(1024)(128)(2,1)}, u32[]{:S(2)}) copy-start(bf16[1024]{0:T(1024)(128)(2,1)} %param.26) | copy-start | bytes 6148
  52.8 297.3 %reduce-scatter.4.cloned.1.call-start = ((), (), s32[]{:S(2)}) async-start(), calls=%async_computation.5 | async-start | bytes 1114112
  106.5 5.6 %copy-start.2 = (f32[2,1024,1024]{1,2,0:T(8,128)S(1)}, f32[2,1024,1024]{1,2,0:T(8,128)}, u32[]{:S(2)}) copy-start(f32[2,1024,1024]{1,2,0:T(8,128)} %get-tuple-element.19) | copy-start | bytes 25165828
Sparse Core Ops, SparseCore 0:
  52.9 41.9 all-gather.1
  152.0 198.0 reduce-scatter.3
where the time goes:
time: 364 us; the launch traced here: 359 us
  waiting for transfers between devices  199 us (55%)
  matrix products  77.5 us (21%)
  local copies, waits for them, and re-layouts  27.7 us (8%)
  blocking collectives  24.4 us (7%)
  between operations  14.2 us (4%)
  starting transfers between devices  12 us (3%)
  other arithmetic  3.7 us (1%)
    unnamed x3, waiting for transfers between devices  176 us
    all_gather x1, waiting for transfers between devices, on_device(): everyone = lax.all_gather(normed, 'patch', axis=1, tiled=True)  22.6 us
    unnamed x18, local copies, waits for them, and re-layouts  17.4 us
    dot_general x1, matrix products, on_device(): jnp.einsum('bhqk,bkhe->bqhe', grad_scores, key_rows, preferred_element_ty...  14.5 us
    dot_general x1, matrix products, on_device(): jnp.einsum('bhqk,bqhe->bkhe', grad_scores, queries, preferred_element_typ...  14.4 us
    all_to_all x1, blocking collectives, on_device(): lax.all_to_all(grad_context, 'patch', split_axis=2, concat_axis=1, tiled=...  12.7 us
    all_to_all x1, starting transfers between devices, on_device(): lax.all_to_all(fields, 'var', split_axis=0, concat_axis=1, tiled=True)  11.7 us
    all_to_all x1, blocking collectives, on_device(): lax.all_to_all(context.reshape(samples, length, columns), 'patch', split_...  11.7 us
  transfers between devices with their start and end apart: 3, of which 2 were waited for; matrix products, arithmetic and copies ran while one was open for 10% of the time, Pallas kernels for 0%

commit v1 on v0

v1 whole, which is shorter than its diff:
```python
import functools

import jax
import jax.numpy as jnp
from jax import lax
from jax.experimental import pallas as pl
from jax.experimental.pallas import tpu as pltpu
from jax.sharding import PartitionSpec as P

H = 16
HD = 64
V = 48
PIX = 4
D = 1024
ROWS = 64
BLOCK = 256
F32 = jnp.float32
BF16 = jnp.bfloat16
VMEM_LIMIT = 56 * 1024 * 1024

NN = (((1,), (0,)), ((), ()))
NT = (((1,), (1,)), ((), ()))
TN = (((0,), (0,)), ((), ()))


def mm(a, b, dims=NN):
    return lax.dot_general(a, b, dims, preferred_element_type=F32)


def split2(x):
    high = x.astype(BF16)
    return high, (x - high.astype(F32)).astype(BF16)


def prep_kernel(
    target_ref, query_ref, embed_ref, var_embed_ref, key_ref, value_ref, out_w_ref, cot_ref,
    place_ref, score_ref, table_ref, grad_ref,
):
    count = place_ref.shape[1]
    rows = lax.broadcasted_iota(jnp.int32, (V * PIX, count), 0)
    place_ref[...] = (target_ref[...] == rows).astype(F32).astype(BF16)
    row = lax.broadcasted_iota(jnp.int32, (V * PIX, V * PIX), 0)
    col = lax.broadcasted_iota(jnp.int32, (V * PIX, V * PIX), 1)
    order = ((row % V) * PIX + row // V == col).astype(F32).astype(BF16)
    table = jnp.concatenate(
        [mm(order, embed_ref[...]).astype(BF16), var_embed_ref[...]], axis=0
    )
    values = mm(table, value_ref[...]).T
    high, low = split2(values)
    for h in range(H):
        table_ref[h, :HD, :] = high[h * HD:(h + 1) * HD]
        table_ref[h, HD:, :] = low[h * HD:(h + 1) * HD]
    head = lax.broadcasted_iota(jnp.int32, (H, D), 0)
    feature = lax.broadcasted_iota(jnp.int32, (H, D), 1)
    query = jnp.where(feature // HD == head, query_ref[...].astype(F32) * HD ** (-0.5), 0.0)
    key_query = mm(query.astype(BF16), key_ref[...], NT)
    first = key_query.astype(BF16)
    rest = key_query - first.astype(F32)
    second = rest.astype(BF16)
    third = (rest - second.astype(F32)).astype(BF16)
    score_ref[...] = mm(table, first, NT) + (mm(table, second, NT) + mm(table, third, NT))
    grad = mm(cot_ref[...], out_w_ref[...], NT).astype(BF16)
    for j in range(H):
        r = (j % 2) * ROWS
        own = grad[r:r + ROWS, j * HD:(j + 1) * HD]
        other = grad[r:r + ROWS, (j ^ 1) * HD:((j ^ 1) + 1) * HD]
        grad_ref[j] = jnp.concatenate([own, other], axis=1)


def token_kernel(
    place_ref, fields_ref, score_ref, table_ref, agg_out_ref, pos_ref, lead_ref, lead_table_ref, gain_ref,
    core_ref, tokens_ref, keep_ref, send_ref, normed_ref,
):
    pixels = mm(place_ref[...], fields_ref[...])
    parts = [pixels[k * V:(k + 1) * V] for k in range(PIX)]
    pooled = []
    for h in range(H):
        column = lambda k: score_ref[k * V:(k + 1) * V, h:h + 1]
        scores = column(PIX) + parts[0] * column(0)
        for k in range(1, PIX):
            scores = scores + parts[k] * column(k)
        probs = jnp.exp(scores - jnp.max(scores, axis=0, keepdims=True))
        probs = probs / jnp.sum(probs, axis=0, keepdims=True)
        mixing = jnp.concatenate([probs * part for part in parts] + [probs], axis=0)
        high, low = split2(mixing)
        both = mm(table_ref[h], high)
        pooled.append((both[:HD] + (both[HD:] + mm(table_ref[h, :HD], low))).astype(BF16))
    pooled = jnp.concatenate(pooled, axis=0)
    tokens = mm(pooled, agg_out_ref[...], TN)
    row = lax.broadcasted_iota(jnp.int32, (2 * ROWS, 16), 0)
    col = lax.broadcasted_iota(jnp.int32, (2 * ROWS, 16), 1)
    lead = jnp.where(row < ROWS, lead_ref[0], lead_ref[1])
    lead_rows = mm((lead == col).astype(F32).astype(BF16), lead_table_ref[...])
    pos = pos_ref[...].astype(F32)
    tokens = tokens + jnp.concatenate([pos, pos], axis=0) + lead_rows
    tokens_ref[...] = tokens
    center = tokens - jnp.mean(tokens, axis=-1, keepdims=True)
    spread = jnp.mean(center * center, axis=-1, keepdims=True)
    normed_ref[...] = (center * lax.rsqrt(spread + 1e-05) * gain_ref[...].astype(F32)).astype(BF16)
    own = pl.multiple_of(core_ref[0] * ROWS, ROWS)
    other = pl.multiple_of((1 - core_ref[0]) * ROWS, ROWS)
    keep_ref[...] = normed_ref[pl.ds(own, ROWS), :]
    send_ref[...] = normed_ref[pl.ds(other, ROWS), :]


def attention_kernel(pieces, *refs):
    n = len(pieces)
    piece_refs = refs[:n]
    (offset_ref, weight_ref, grad_ctx_ref, context_ref, own_ref, other_ref,
     x_ref, q_ref, k_ref, v_ref, dq_ref, dk_ref, dv_ref, w_ref, sem) = refs[n:]
    copies = []
    for i, (ref, start) in enumerate(zip(piece_refs, pieces)):
        copies.append(pltpu.make_async_copy(ref, x_ref.at[pl.ds(start, ref.shape[0])], sem.at[i]))
        copies[-1].start()
    for copy in copies:
        copy.wait()
    offsets = [pl.multiple_of(offset_ref[i], ROWS) for i in range(H)]
    projected = mm(x_ref[...], weight_ref[...]).astype(BF16)
    for i in range(H):
        rows = pl.ds(offsets[i], ROWS)
        here = projected[i * ROWS:(i + 1) * ROWS]
        q_ref[rows, :] = here[:, :128] * jnp.asarray(HD ** (-0.5), BF16)
        k_ref[rows, :] = here[:, 128:256]
        v_ref[rows, :] = here[:, 256:]
    keys = k_ref[...]
    values = v_ref[...]
    keys_t = keys.T
    values_t = values.T
    dk_ref[...] = jnp.zeros_like(dk_ref)
    dv_ref[...] = jnp.zeros_like(dv_ref)
    lane = lax.broadcasted_iota(jnp.int32, (BLOCK, 128), 1)

    def step(i, carry):
        rows = pl.ds(pl.multiple_of(i * BLOCK, BLOCK), BLOCK)
        queries = q_ref[rows, :]
        grads = grad_ctx_ref[rows, :]
        context, dq, low, ds, gs, qs = [], [], [], [], [], []
        for h in range(2):
            mine = lane // HD == h
            q = jnp.where(mine, queries, jnp.zeros_like(queries))
            g = jnp.where(mine, grads, jnp.zeros_like(grads))
            scores = mm(keys, q, NT)
            e = jnp.exp(scores - jnp.max(scores, axis=0, keepdims=True))
            probs = e * (1.0 / jnp.sum(e, axis=0, keepdims=True))
            probs_low = probs.astype(BF16)
            context.append(mm(values_t[h * HD:(h + 1) * HD], probs_low))
            dp = mm(values, g, NT)
            dots = jnp.sum(probs * dp, axis=0, keepdims=True)
            d = (probs * (dp - dots)).astype(BF16)
            dq.append(mm(keys_t[h * HD:(h + 1) * HD], d))
            low.append(probs_low)
            ds.append(d)
            gs.append(g)
            qs.append(q)
        context_ref[rows, :] = jnp.concatenate(context, axis=0).T.astype(BF16)
        dq_ref[rows, :] = (jnp.concatenate(dq, axis=0).T * HD ** (-0.5)).astype(BF16)
        dv_ref[...] += mm(jnp.concatenate(low, axis=1), jnp.concatenate(gs, axis=0))
        dk_ref[...] += mm(jnp.concatenate(ds, axis=1), jnp.concatenate(qs, axis=0))
        return carry

    lax.fori_loop(0, D // BLOCK, step, 0)
    for i in range(H):
        rows = pl.ds(offsets[i], ROWS)
        here = slice(i * ROWS, (i + 1) * ROWS)
        dq = dq_ref[rows, :]
        dk = dk_ref[rows, :].astype(BF16)
        dv = dv_ref[rows, :].astype(BF16)
        w_ref[here, 0:128] = jnp.concatenate([dq[:, :HD], dk[:, :HD]], axis=1)
        w_ref[here, 128:256] = jnp.concatenate([dq[:, HD:], dk[:, HD:]], axis=1)
        w_ref[here, 256:384] = dv
    grad = mm(x_ref[...], w_ref[...], TN)
    for j in range(H):
        top = grad[j * ROWS:j * ROWS + ROWS // 2, 256:]
        bottom = grad[j * ROWS + ROWS // 2:(j + 1) * ROWS, 256:]
        own_ref[j, :ROWS] = grad[j * ROWS:(j + 1) * ROWS, :128]
        own_ref[j, ROWS:] = jnp.concatenate([top[:, :HD], bottom[:, :HD]], axis=1)
        other_ref[j, :ROWS] = grad[j * ROWS:(j + 1) * ROWS, 128:256]
        other_ref[j, ROWS:] = jnp.concatenate([top[:, HD:], bottom[:, HD:]], axis=1)


def output_kernel(context_ref, out_w_ref, tokens_ref, out_ref):
    rows = []
    for s in range(2):
        parts = []
        for m in range(H // 2):
            part = context_ref[2 * m + s]
            if s:
                part = jnp.concatenate([part[:, HD:], part[:, :HD]], axis=1)
            parts.append(part)
        rows.append(jnp.concatenate(parts, axis=1))
    context = jnp.concatenate(rows, axis=0)
    out_ref[...] = (tokens_ref[...] + mm(context, out_w_ref[...])).astype(BF16)


def sum_kernel(parts_ref, out_ref):
    total = parts_ref[0].astype(F32)
    for j in range(1, H):
        total = total + parts_ref[j].astype(F32)
    out_ref[0] = total[:ROWS, :HD]
    out_ref[1] = total[:ROWS, HD:]
    out_ref[2, :ROWS // 2] = total[ROWS:, :HD]
    out_ref[2, ROWS // 2:] = total[ROWS:, HD:]


VM = pl.BlockSpec(memory_space=pltpu.VMEM)
SM = pl.BlockSpec(memory_space=pltpu.SMEM)
ANY = pl.BlockSpec(memory_space=pl.ANY)


def call(kernel, out, in_specs, name, scratch=()):
    return pl.pallas_call(
        kernel,
        out_shape=out,
        in_specs=in_specs,
        out_specs=jax.tree.map(lambda _: VM, out),
        scratch_shapes=list(scratch),
        compiler_params=pltpu.CompilerParams(vmem_limit_bytes=VMEM_LIMIT),
        name=name,
    )


def shape(dims, dtype):
    return jax.ShapeDtypeStruct(dims, dtype)


def on_device(
    fields, var_ids, lead_index, embed_weight, var_embed, agg_query, agg_key, agg_value, agg_out,
    pos_embed, lead_table, norm_gain, qkv_weight, out_weight, cotangent,
):
    place = lax.axis_index("patch")
    core = place % 2
    chip = place // 2
    pair = [(i, i ^ 1) for i in range(16)]
    across = [(i, i ^ 2) for i in range(16)]
    up = [(i, (i + 4) % 16) for i in range(16)]
    down = [(i, (i - 4) % 16) for i in range(16)]
    move = lambda a, perm: lax.ppermute(a, "patch", perm)

    sent = fields.reshape(16, 2, 3, PIX, ROWS).transpose(0, 2, 3, 1, 4).reshape(16, 12, 128)
    sent = jnp.pad(sent, ((0, 0), (0, 4), (0, 0)))
    owned = lax.all_to_all(sent, "var", split_axis=0, concat_axis=0, tiled=True).reshape(256, 128)
    target = var_ids.reshape(16, 3, 1) + V * jnp.arange(PIX, dtype=jnp.int32)[None, None, :]
    target = jnp.pad(target.reshape(16, 12), ((0, 0), (0, 4)), constant_values=-1).reshape(1, 256)

    other_weight = move(qkv_weight, pair)
    weight = jnp.concatenate([qkv_weight, other_weight], axis=2)
    weight = weight.transpose(1, 0, 2).reshape(D, 384)

    placing, score, table, grad_parts = call(
        prep_kernel,
        (shape((V * PIX, 256), BF16), shape((V * (PIX + 1), H), F32),
         shape((H, 2 * HD, V * (PIX + 1)), BF16), shape((H, ROWS, 128), BF16)),
        [VM] * 8, "prep",
    )(target, agg_query.reshape(1, D), embed_weight.reshape(V * PIX, D), var_embed, agg_key, agg_value,
      out_weight, cotangent.reshape(2 * ROWS, D))

    tokens, keep, send = call(
        token_kernel,
        (shape((2 * ROWS, D), F32), shape((ROWS, D), BF16), shape((ROWS, D), BF16)),
        [VM] * 6 + [SM] + [VM] * 2 + [SM], "tokens", [pltpu.VMEM((2 * ROWS, D), BF16)],
    )(placing, owned, score, table, agg_out, pos_embed, lead_index, lead_table, norm_gain.reshape(1, D),
      core.reshape(1))

    here = jnp.concatenate([keep, move(send, pair)], axis=0)
    y = move(here, across)
    left = move(here, up)
    right = move(here, down)
    grad_ctx = lax.all_to_all(grad_parts, "patch", split_axis=0, concat_axis=0, tiled=True)
    far0 = move(left[:64], up)
    far1 = move(right[64:], down)
    y_left = move(y, up)
    y_right = move(y, down)
    y_far0 = move(far0, across)
    y_far1 = move(y_left[64:96], up)
    y_far2 = move(y_right[96:], down)
    pieces = [here, y, left, right, y_left, y_right, far0, far1, y_far0, y_far1, y_far2]
    starts, at = [], 0
    for piece in pieces:
        starts.append(at)
        at += piece.shape[0]
    cx, cy = chip // 2, chip % 2
    chips = []
    for dx, dy in [(0, 0), (0, 1), (-1, 0), (1, 0), (-1, 1), (1, 1), (2, 0), (2, 1)]:
        chips.append(((cx + dx) % 4) * 2 + (cy + dy) % 2)
    chips = jnp.stack(chips)
    offsets = (chips[:, None] * 128 + jnp.stack([core, 1 - core])[None, :] * ROWS).reshape(16)

    scratch = [pltpu.VMEM((D, D), BF16)] + [pltpu.VMEM((D, 128), BF16)] * 4
    scratch += [pltpu.VMEM((D, 128), F32)] * 2 + [pltpu.VMEM((D, 384), BF16)]
    scratch += [pltpu.SemaphoreType.DMA((len(pieces),))]
    context, own, other = call(
        functools.partial(attention_kernel, tuple(starts)),
        (shape((D, 128), BF16), shape((H, 96, 128), F32), shape((H, 96, 128), F32)),
        [ANY] * len(pieces) + [SM, VM, VM], "attention", scratch,
    )(*pieces, offsets.astype(jnp.int32), weight, grad_ctx.reshape(D, 128))

    partial_grad = (own + move(other, pair)).astype(BF16)
    parts = lax.all_to_all(partial_grad, "var", split_axis=0, concat_axis=0, tiled=True)
    merged = lax.all_to_all(context.reshape(H, ROWS, 128), "patch", split_axis=0, concat_axis=0, tiled=True)
    layer_out = call(output_kernel, shape((2 * ROWS, D), BF16), [VM] * 3, "out")(merged, out_weight, tokens)
    grad_qkv = call(sum_kernel, shape((3, ROWS, HD), F32), [VM], "sum")(parts)
    return layer_out.reshape(2, ROWS, D), grad_qkv


def solution(mesh):
    in_specs = (
        P(None, "var", None, "patch"), P(), P("var"), P(), P(), P(), P(), P(), P(), P("patch", None), P(), P(),
        P(None, None, "patch"), P(), P("var", "patch", None),
    )
    out_specs = (P("var", "patch", None), P(None, "var", "patch"))
    return jax.shard_map(on_device, mesh=mesh, in_specs=in_specs, out_specs=out_specs, check_vma=False)
```

time: 364 us -> 131 us (0.36); the launches traced: 359 us -> 131 us
  waiting for transfers between devices: 199 us -> 32.8 us
  matrix products: 77.5 us -> 0 us
  Pallas kernels: 0 us -> 37.1 us
  starting transfers between devices: 12 us -> 44.1 us
  blocking collectives: 24.4 us -> 0 us
  local copies, waits for them, and re-layouts: 27.7 us -> 13.3 us
  between operations: 14.2 us -> 0.83 us
    unnamed x3 -> x0, waiting for transfers between devices: 176 us -> none
    dot_general x17 -> x0, matrix products: 70.6 us -> none  [the longest x1 14.5 us: on_device(): jnp.einsum('bhqk,bkhe->bqhe', grad_scores, key_rows, preferred_element_ty...]
    pallas_call x0 -> x5, Pallas kernels: none -> 37.1 us  [the longest x1 21.6 us: on_device(): call(functools.partial(attention_kernel, tuple(starts)), (shape((D, 128),...]
    all_to_all x2 -> x0, blocking collectives: 24.4 us -> none  [the longest x1 12.7 us: on_device(): lax.all_to_all(grad_context, 'patch', split_axis=2, concat_axis=1, tiled=...]
    all_gather x1 -> x0, waiting for transfers between devices: 22.6 us -> none  [on_device(): everyone = lax.all_gather(normed, 'patch', axis=1, tiled=True)]
    all_to_all x1 -> x4, starting transfers between devices: 11.7 us -> 29.7 us  [the longest x1 11.7 us: on_device(): lax.all_to_all(sent, 'var', split_axis=0, concat_axis=0, tiled=True)]
    all_to_all x1 -> x4, waiting for transfers between devices: 0.01 us -> 17.4 us  [the longest x1 12 us: on_device(): lax.all_to_all(partial_grad, 'var', split_axis=0, concat_axis=0, tiled=True)]
    ppermute x0 -> x13, waiting for transfers between devices: none -> 15.4 us  [on_device(): move = lambda a, perm: lax.ppermute(a, 'patch', perm)]
  transfers between devices with their start and end apart: 3 -> 17, of which waited for: 2 -> 7; matrix products, arithmetic and copies ran while one was open for 10% -> 10% of each run, Pallas kernels for 0% -> 7%
where the time goes in v1:
time: 131 us
  starting transfers between devices  44.1 us (34%)
  Pallas kernels  37.1 us (28%)
  waiting for transfers between devices  32.8 us (25%)
  local copies, waits for them, and re-layouts  13.3 us (10%)
  other arithmetic  2.24 us (2%)
    pallas_call x1, Pallas kernels, on_device(): call(functools.partial(attention_kernel, tuple(starts)), (shape((D, 128),...  21.6 us
    ppermute x13, waiting for transfers between devices, on_device(): move = lambda a, perm: lax.ppermute(a, 'patch', perm)  15.4 us
    ppermute x13, starting transfers between devices, on_device(): move = lambda a, perm: lax.ppermute(a, 'patch', perm)  14.4 us
    all_to_all x1, waiting for transfers between devices, on_device(): lax.all_to_all(partial_grad, 'var', split_axis=0, concat_axis=0, tiled=True)  12 us
    all_to_all x1, starting transfers between devices, on_device(): lax.all_to_all(sent, 'var', split_axis=0, concat_axis=0, tiled=True)  11.7 us
    all_to_all x1, starting transfers between devices, on_device(): lax.all_to_all(partial_grad, 'var', split_axis=0, concat_axis=0, tiled=True)  9.33 us
    pallas_call x1, Pallas kernels, on_device(): call(prep_kernel, (shape((V * PIX, 256), BF16), shape((V * (PIX + 1), H),...  6.25 us
    all_to_all x1, waiting for transfers between devices, on_device(): lax.all_to_all(context.reshape(H, ROWS, 128), 'patch', split_axis=0, conc...  5.39 us
  transfers between devices with their start and end apart: 17, of which 7 were waited for; matrix products, arithmetic and copies ran while one was open for 10% of the time, Pallas kernels for 7%

profile of v1, /device:TPU:1, one launch (start us, length us, event | category | flops | bytes accessed | tf_op | source)
XLA Modules:
  0.0 130.5 jit_solution(3860190769902080975)
XLA Ops:
  0.6 1.0 copy.32
  2.4 11.7 %all-to-all-start = ((bf16[16,16,128]{2,1,0:T(8,128)(2,1)}), bf16[16,16,128]{2,1,0:T(8,128)(2,1)S(1)}, u32[]{:S(2)}, u32[]{:S(2)}) async-start(bf16[16,16,128]{2,1,0:T(8,128)(2,1)} %pad.9.clone), calls=%async_computation | async-start | bytes 131072 | tf_op jit(solution)/shard_map/all_to_all | solution.py:241
  14.3 1.3 reshape.142.query_ref
  15.5 1.3 reshape.148.gain_ref
  16.8 0.7 add.125
  17.8 0.7 reshape.141.target_ref
  18.5 1.8 %reshape.143.embed_ref = bf16[192,1024]{1,0:T(8,128)(2,1)} reshape(bf16[48,4,1024]{2,1,0:T(4,128)(2,1)} %param.18) | data formatting | bytes 786432 | tf_op jit(solution)/shard_map/reshape | solution.py:254
  20.3 6.3 %prep.1 = (bf16[192,256]{1,0:T(8,128)(2,1)}, f32[240,16]{1,0:T(8,128)}, bf16[16,128,240]{2,1,0:T(8,128)(2,1)}, bf16[16,64,128]{2,1,0:T(8,128)(2,1)}) custom-call(s32[1,256]{1,0:T(1,128)} %reshape.141.target_ref, bf16[1,1024]{1,0:T(2,128)(2,1)} %reshape.142.query_ref, bf16[192,1024]{1,0:T(8,128)(2,1)} %reshape.143.embed_ref, bf16[48,1024]{1,0:T(8,128)(2,1)} %var_embed_ref.1, ...), custom_call_target="tpu_custom_call" | custom-call | tf_op jit(solution)/shard_map/prep/pallas_call | solution.py:249
  27.2 4.5 %tokens.1 = (f32[128,1024]{1,0:T(8,128)}, bf16[64,1024]{1,0:T(8,128)(2,1)}, bf16[64,1024]{1,0:T(8,128)(2,1)}) custom-call(bf16[192,256]{1,0:T(8,128)(2,1)} %get-tuple-element.12.place_ref, bf16[256,128]{1,0:T(8,128)(2,1)} %bitcast.29, f32[240,16]{1,0:T(8,128)} %get-tuple-element.13.score_ref, bf16[16,128,240]{2,1,0:T(8,128)(2,1)} %get-tuple-element.14.table_ref, ...), custom_call_target="tpu_custom_call" | custom-call | tf_op jit(solution)/shard_map/tokens/pallas_call | solution.py:257
  31.7 1.0 collective-permute-start
  32.7 0.9 constant_dynamic-update-slice_fusion.1
  35.1 5.2 %all-to-all-start.1 = ((bf16[16,64,128]{2,1,0:T(8,128)(2,1)}), bf16[16,64,128]{2,1,0:T(8,128)(2,1)S(1)}, u32[]{:S(2)}, u32[]{:S(2)}) async-start(bf16[16,64,128]{2,1,0:T(8,128)(2,1)} %get-tuple-element.17), calls=%async_computation.1 | async-start | bytes 524288 | tf_op jit(solution)/shard_map/all_to_all | solution.py:268
  40.3 1.4 %collective-permute-start.2 = (bf16[128,1024]{1,0:T(8,128)(2,1)S(1)}, bf16[128,1024]{1,0:T(8,128)(2,1)S(1)}, u32[]{:S(2)}, u32[]{:S(2)}) collective-permute-start(bf16[128,1024]{1,0:T(8,128)(2,1)S(1)} %constant_dynamic-update-slice_fusion.refs_0_), channel_id=1, source_target_pairs={{0,64},{16,80},{32,96},{48,112},{64,128},{80,144},{96,160},{112,17... | collective-permute-start | bytes 786440 | tf_op jit(solution)/shard_map/ppermute | solution.py:237
  41.8 1.3 %collective-permute-start.3 = (bf16[128,1024]{1,0:T(8,128)(2,1)S(1)}, bf16[128,1024]{1,0:T(8,128)(2,1)S(1)}, u32[]{:S(2)}, u32[]{:S(2)}) collective-permute-start(bf16[128,1024]{1,0:T(8,128)(2,1)S(1)} %constant_dynamic-update-slice_fusion.refs_0_), channel_id=1, source_target_pairs={{0,192},{16,208},{32,224},{48,240},{64,0},{80,16},{96,32},{112,48}... | collective-permute-start | bytes 786440 | tf_op jit(solution)/shard_map/ppermute | solution.py:237
  43.1 1.4 %collective-permute-start.5 = (bf16[128,1024]{1,0:T(8,128)(2,1)S(1)}, bf16[128,1024]{1,0:T(8,128)(2,1)S(1)}, u32[]{:S(2)}, u32[]{:S(2)}) collective-permute-start(bf16[128,1024]{1,0:T(8,128)(2,1)S(1)} %collective-permute-done.1.refs_1_), channel_id=1, source_target_pairs={{0,192},{16,208},{32,224},{48,240},{64,0},{80,16},{96,32},{112,48}... | collective-permute-start | bytes 786440 | tf_op jit(solution)/shard_map/ppermute | solution.py:237
  44.6 7.6 %collective-permute-done.2.refs_2_ = bf16[128,1024]{1,0:T(8,128)(2,1)S(1)} collective-permute-done((bf16[128,1024]{1,0:T(8,128)(2,1)S(1)}, bf16[128,1024]{1,0:T(8,128)(2,1)S(1)}, u32[]{:S(2)}, u32[]{:S(2)}) %collective-permute-start.2) | collective-permute-done | bytes 262176 | tf_op jit(solution)/shard_map/ppermute | solution.py:237
  53.0 2.7 %collective-permute-start.7 = (bf16[64,1024]{1,0:T(8,128)(2,1)S(1)}, bf16[64,1024]{1,0:T(8,128)(2,1)}, u32[]{:S(2)}, u32[]{:S(2)}) collective-permute-start(bf16[64,1024]{1,0:T(8,128)(2,1)S(1)} %slice.17), channel_id=1, source_target_pairs={{0,192},{16,208},{32,224},{48,240},{64,0},{80,16},{96,32},{112,48}... | collective-permute-start | bytes 393224 | tf_op jit(solution)/shard_map/ppermute | solution.py:237
  55.8 5.0 %collective-permute-done.6.refs_6_ = bf16[64,1024]{1,0:T(8,128)(2,1)} collective-permute-done((bf16[64,1024]{1,0:T(8,128)(2,1)S(1)}, bf16[64,1024]{1,0:T(8,128)(2,1)}, u32[]{:S(2)}, u32[]{:S(2)}) %collective-permute-start.6) | collective-permute-done | bytes 131104 | tf_op jit(solution)/shard_map/ppermute | solution.py:237
  60.8 1.2 collective-permute-start.8
  63.9 0.9 collective-permute-start.9
  64.9 1.2 copy.28.refs_12_
  66.4 2.2 %collective-permute-done.9.refs_9_ = bf16[32,1024]{1,0:T(8,128)(2,1)} collective-permute-done((bf16[32,1024]{1,0:T(8,128)(2,1)}, bf16[32,1024]{1,0:T(8,128)(2,1)}, u32[]{:S(2)}, u32[]{:S(2)}) %collective-permute-start.9) | collective-permute-done | bytes 65568 | tf_op jit(solution)/shard_map/ppermute | solution.py:237
  68.6 21.6 %attention.1 = (bf16[1024,128]{1,0:T(8,128)(2,1)}, f32[16,96,128]{2,1,0:T(8,128)}, f32[16,96,128]{2,1,0:T(8,128)}) custom-call(bf16[128,1024]{1,0:T(8,128)(2,1)} %copy-done.5, bf16[128,1024]{1,0:T(8,128)(2,1)} %copy-done.10, bf16[128,1024]{1,0:T(8,128)(2,1)} %copy-done.3, bf16[128,1024]{1,0:T(8,128)(2,1)} %copy-done.4, bf16[128,1024]{1,0:T(8,128)(2,1)} %copy-done.7, ...), custom_call_target="tpu_custom_call" | custom-call | tf_op jit(solution)/shard_map/attention/pallas_call | solution.py:291
  90.2 2.7 %collective-permute-start.12 = (f32[16,96,128]{2,1,0:T(8,128)}, f32[16,96,128]{2,1,0:T(8,128)S(1)}, u32[]{:S(2)}, u32[]{:S(2)}) collective-permute-start(f32[16,96,128]{2,1,0:T(8,128)} %get-tuple-element.21), channel_id=1, source_target_pairs={{0,16},{16,0},{32,48},{48,32},{64,80},{80,64},{96,112},{112,96},{1... | collective-permute-start | bytes 2359304 | tf_op jit(solution)/shard_map/ppermute | solution.py:237
  92.9 3.4 %all-to-all-start.2 = ((bf16[16,64,128]{2,1,0:T(8,128)(2,1)}), bf16[16,64,128]{2,1,0:T(8,128)(2,1)S(1)}, u32[]{:S(2)}, u32[]{:S(2)}) async-start(bf16[16,64,128]{2,1,0:T(8,128)(2,1)} %bitcast.32), calls=%async_computation.2 | async-start | bytes 524288 | tf_op jit(solution)/shard_map/all_to_all | solution.py:299
  96.3 2.0 %add_convert_fusion = bf16[16,96,128]{2,1,0:T(8,128)(2,1)} fusion(f32[16,96,128]{2,1,0:T(8,128)} %get-tuple-element.20, f32[16,96,128]{2,1,0:T(8,128)S(1)} %collective-permute-done.12), kind=kLoop, calls=%fused_computation.1 | loop fusion | flops 393216 | bytes 1966080 | tf_op jit(solution)/shard_map/convert_element_type | solution.py:297
  98.3 5.4 %all-to-all-done.2.context_ref = bf16[16,64,128]{2,1,0:T(8,128)(2,1)S(1)} async-done(((bf16[16,64,128]{2,1,0:T(8,128)(2,1)}), bf16[16,64,128]{2,1,0:T(8,128)(2,1)S(1)}, u32[]{:S(2)}, u32[]{:S(2)}) %all-to-all-start.2) | async-done | bytes 262176 | tf_op jit(solution)/shard_map/all_to_all | solution.py:299
  103.7 9.3 %all-to-all-start.3 = ((bf16[16,96,128]{2,1,0:T(8,128)(2,1)}), bf16[16,96,128]{2,1,0:T(8,128)(2,1)S(1)}, u32[]{:S(2)}, u32[]{:S(2)}) async-start(bf16[16,96,128]{2,1,0:T(8,128)(2,1)} %add_convert_fusion), calls=%async_computation.3 | async-start | bytes 786432 | tf_op jit(solution)/shard_map/all_to_all | solution.py:298
  113.0 2.9 %out.1 = bf16[128,1024]{1,0:T(8,128)(2,1)} custom-call(bf16[16,64,128]{2,1,0:T(8,128)(2,1)} %copy-done.1, bf16[1024,1024]{1,0:T(8,128)(2,1)} %out_w_ref.3, f32[128,1024]{1,0:T(8,128)} %get-tuple-element.19.tokens_ref), custom_call_target="tpu_custom_call" | custom-call | tf_op jit(solution)/shard_map/out/pallas_call | solution.py:300
  116.0 12.0 %all-to-all-done.3.parts_ref = bf16[16,96,128]{2,1,0:T(8,128)(2,1)S(1)} async-done(((bf16[16,96,128]{2,1,0:T(8,128)(2,1)}), bf16[16,96,128]{2,1,0:T(8,128)(2,1)S(1)}, u32[]{:S(2)}, u32[]{:S(2)}) %all-to-all-start.3) | async-done | bytes 393248 | tf_op jit(solution)/shard_map/all_to_all | solution.py:298
  128.0 0.7 copy-done
  128.7 1.8 %sum.1 = f32[3,64,64]{2,1,0:T(8,128)} custom-call(bf16[16,96,128]{2,1,0:T(8,128)(2,1)} %copy-done), custom_call_target="tpu_custom_call" | custom-call | tf_op jit(solution)/shard_map/sum/pallas_call | solution.py:301
  (61 shorter events, 6.5 us)
Async XLA Ops:
  2.4 24.2 %all-to-all-start = ((bf16[16,16,128]{2,1,0:T(8,128)(2,1)}), bf16[16,16,128]{2,1,0:T(8,128)(2,1)S(1)}, u32[]{:S(2)}, u32[]{:S(2)}) async-start(bf16[16,16,128]{2,1,0:T(8,128)(2,1)} %pad.9.clone), calls=%async_computation | async-start | bytes 131072 | tf_op jit(solution)/shard_map/all_to_all | solution.py:241
  26.6 7.8 %copy-start.8 = (bf16[3,1024,64]{1,2,0:T(8,128)(2,1)S(1)}, bf16[3,1024,64]{1,2,0:T(8,128)(2,1)}, u32[]{:S(2)}) copy-start(bf16[3,1024,64]{1,2,0:T(8,128)(2,1)} %param.27) | copy-start | bytes 1179652
  26.6 0.6 copy-start.9
  31.7 2.1 %collective-permute-start = (bf16[64,1024]{1,0:T(8,128)(2,1)}, bf16[64,1024]{1,0:T(8,128)(2,1)S(1)}, u32[]{:S(2)}, u32[]{:S(2)}) collective-permute-start(bf16[64,1024]{1,0:T(8,128)(2,1)} %get-tuple-element.16), channel_id=1, source_target_pairs={{0,16},{16,0},{32,48},{48,32},{64,80},{80,64},{96,112},{112,96},{1... | collective-permute-start | bytes 393224 | tf_op jit(solution)/shard_map/ppermute | solution.py:237
  33.9 32.1 %copy-start.5 = (bf16[128,1024]{1,0:T(8,128)(2,1)}, bf16[128,1024]{1,0:T(8,128)(2,1)S(1)}, u32[]{:S(2)}) copy-start(bf16[128,1024]{1,0:T(8,128)(2,1)S(1)} %constant_dynamic-update-slice_fusion.refs_0_) | copy-start | bytes 786436
  33.9 9.2 %collective-permute-start.1 = (bf16[128,1024]{1,0:T(8,128)(2,1)S(1)}, bf16[128,1024]{1,0:T(8,128)(2,1)S(1)}, u32[]{:S(2)}, u32[]{:S(2)}) collective-permute-start(bf16[128,1024]{1,0:T(8,128)(2,1)S(1)} %constant_dynamic-update-slice_fusion.refs_0_), channel_id=1, source_target_pairs={{0,32},{16,48},{32,0},{48,16},{64,96},{80,112},{96,64},{112,80},{1... | collective-permute-start | bytes 786440 | tf_op jit(solution)/shard_map/ppermute | solution.py:237
  34.4 30.4 %collective-permute-start.11 = (bf16[3,1024,64]{1,2,0:T(8,128)(2,1)S(1)}, bf16[3,1024,64]{1,2,0:T(8,128)(2,1)S(1)}, u32[]{:S(2)}, u32[]{:S(2)}) collective-permute-start(bf16[3,1024,64]{1,2,0:T(8,128)(2,1)S(1)} %copy-done.8), channel_id=1, source_target_pairs={{0,16},{16,0},{32,48},{48,32},{64,80},{80,64},{96,112},{112,96},{1... | collective-permute-start | bytes 1179656 | tf_op jit(solution)/shard_map/ppermute | solution.py:237
  35.1 31.0 %all-to-all-start.1 = ((bf16[16,64,128]{2,1,0:T(8,128)(2,1)}), bf16[16,64,128]{2,1,0:T(8,128)(2,1)S(1)}, u32[]{:S(2)}, u32[]{:S(2)}) async-start(bf16[16,64,128]{2,1,0:T(8,128)(2,1)} %get-tuple-element.17), calls=%async_computation.1 | async-start | bytes 524288 | tf_op jit(solution)/shard_map/all_to_all | solution.py:268
  40.3 11.9 %collective-permute-start.2 = (bf16[128,1024]{1,0:T(8,128)(2,1)S(1)}, bf16[128,1024]{1,0:T(8,128)(2,1)S(1)}, u32[]{:S(2)}, u32[]{:S(2)}) collective-permute-start(bf16[128,1024]{1,0:T(8,128)(2,1)S(1)} %constant_dynamic-update-slice_fusion.refs_0_), channel_id=1, source_target_pairs={{0,64},{16,80},{32,96},{48,112},{64,128},{80,144},{96,160},{112,17... | collective-permute-start | bytes 786440 | tf_op jit(solution)/shard_map/ppermute | solution.py:237
  41.8 11.3 %collective-permute-start.3 = (bf16[128,1024]{1,0:T(8,128)(2,1)S(1)}, bf16[128,1024]{1,0:T(8,128)(2,1)S(1)}, u32[]{:S(2)}, u32[]{:S(2)}) collective-permute-start(bf16[128,1024]{1,0:T(8,128)(2,1)S(1)} %constant_dynamic-update-slice_fusion.refs_0_), channel_id=1, source_target_pairs={{0,192},{16,208},{32,224},{48,240},{64,0},{80,16},{96,32},{112,48}... | collective-permute-start | bytes 786440 | tf_op jit(solution)/shard_map/ppermute | solution.py:237
  43.1 25.5 %copy-start.10 = (bf16[128,1024]{1,0:T(8,128)(2,1)}, bf16[128,1024]{1,0:T(8,128)(2,1)S(1)}, u32[]{:S(2)}) copy-start(bf16[128,1024]{1,0:T(8,128)(2,1)S(1)} %collective-permute-done.1.refs_1_) | copy-start | bytes 786436
  43.1 18.9 %collective-permute-start.5 = (bf16[128,1024]{1,0:T(8,128)(2,1)S(1)}, bf16[128,1024]{1,0:T(8,128)(2,1)S(1)}, u32[]{:S(2)}, u32[]{:S(2)}) collective-permute-start(bf16[128,1024]{1,0:T(8,128)(2,1)S(1)} %collective-permute-done.1.refs_1_), channel_id=1, source_target_pairs={{0,192},{16,208},{32,224},{48,240},{64,0},{80,16},{96,32},{112,48}... | collective-permute-start | bytes 786440 | tf_op jit(solution)/shard_map/ppermute | solution.py:237
  44.4 18.8 %collective-permute-start.4 = (bf16[128,1024]{1,0:T(8,128)(2,1)S(1)}, bf16[128,1024]{1,0:T(8,128)(2,1)S(1)}, u32[]{:S(2)}, u32[]{:S(2)}) collective-permute-start(bf16[128,1024]{1,0:T(8,128)(2,1)S(1)} %collective-permute-done.1.refs_1_), channel_id=1, source_target_pairs={{0,64},{16,80},{32,96},{48,112},{64,128},{80,144},{96,160},{112,17... | collective-permute-start | bytes 786440 | tf_op jit(solution)/shard_map/ppermute | solution.py:237
  52.3 16.3 %copy-start.3 = (bf16[128,1024]{1,0:T(8,128)(2,1)}, bf16[128,1024]{1,0:T(8,128)(2,1)S(1)}, u32[]{:S(2)}) copy-start(bf16[128,1024]{1,0:T(8,128)(2,1)S(1)} %collective-permute-done.2.refs_2_) | copy-start | bytes 786436
  52.3 8.5 %collective-permute-start.6 = (bf16[64,1024]{1,0:T(8,128)(2,1)S(1)}, bf16[64,1024]{1,0:T(8,128)(2,1)}, u32[]{:S(2)}, u32[]{:S(2)}) collective-permute-start(bf16[64,1024]{1,0:T(8,128)(2,1)S(1)} %slice.16), channel_id=1, source_target_pairs={{0,64},{16,80},{32,96},{48,112},{64,128},{80,144},{96,160},{112,17... | collective-permute-start | bytes 393224 | tf_op jit(solution)/shard_map/ppermute | solution.py:237
  53.0 15.5 %copy-start.4 = (bf16[128,1024]{1,0:T(8,128)(2,1)}, bf16[128,1024]{1,0:T(8,128)(2,1)S(1)}, u32[]{:S(2)}) copy-start(bf16[128,1024]{1,0:T(8,128)(2,1)S(1)} %collective-permute-done.3.refs_3_) | copy-start | bytes 786436
  53.0 13.0 %collective-permute-start.7 = (bf16[64,1024]{1,0:T(8,128)(2,1)S(1)}, bf16[64,1024]{1,0:T(8,128)(2,1)}, u32[]{:S(2)}, u32[]{:S(2)}) collective-permute-start(bf16[64,1024]{1,0:T(8,128)(2,1)S(1)} %slice.17), channel_id=1, source_target_pairs={{0,192},{16,208},{32,224},{48,240},{64,0},{80,16},{96,32},{112,48}... | collective-permute-start | bytes 393224 | tf_op jit(solution)/shard_map/ppermute | solution.py:237
  60.8 5.3 %collective-permute-start.8 = (bf16[64,1024]{1,0:T(8,128)(2,1)}, bf16[64,1024]{1,0:T(8,128)(2,1)}, u32[]{:S(2)}, u32[]{:S(2)}) collective-permute-start(bf16[64,1024]{1,0:T(8,128)(2,1)} %collective-permute-done.6.refs_6_), channel_id=1, source_target_pairs={{0,32},{16,48},{32,0},{48,16},{64,96},{80,112},{96,64},{112,80},{1... | collective-permute-start | bytes 393224 | tf_op jit(solution)/shard_map/ppermute | solution.py:237
  62.0 6.6 %copy-start.6 = (bf16[128,1024]{1,0:T(8,128)(2,1)}, bf16[128,1024]{1,0:T(8,128)(2,1)S(1)}, u32[]{:S(2)}) copy-start(bf16[128,1024]{1,0:T(8,128)(2,1)S(1)} %collective-permute-done.5.refs_5_) | copy-start | bytes 786436
  62.7 3.7 %collective-permute-start.10 = (bf16[32,1024]{1,0:T(8,128)(2,1)}, bf16[32,1024]{1,0:T(8,128)(2,1)}, u32[]{:S(2)}, u32[]{:S(2)}) collective-permute-start(bf16[32,1024]{1,0:T(8,128)(2,1)} %slice.19), channel_id=1, source_target_pairs={{0,192},{16,208},{32,224},{48,240},{64,0},{80,16},{96,32},{112,48}... | collective-permute-start | bytes 196616 | tf_op jit(solution)/shard_map/ppermute | solution.py:237
  63.2 5.3 %copy-start.7 = (bf16[128,1024]{1,0:T(8,128)(2,1)}, bf16[128,1024]{1,0:T(8,128)(2,1)S(1)}, u32[]{:S(2)}) copy-start(bf16[128,1024]{1,0:T(8,128)(2,1)S(1)} %collective-permute-done.4.refs_4_) | copy-start | bytes 786436
  63.9 4.6 %collective-permute-start.9 = (bf16[32,1024]{1,0:T(8,128)(2,1)}, bf16[32,1024]{1,0:T(8,128)(2,1)}, u32[]{:S(2)}, u32[]{:S(2)}) collective-permute-start(bf16[32,1024]{1,0:T(8,128)(2,1)} %slice.18), channel_id=1, source_target_pairs={{0,64},{16,80},{32,96},{48,112},{64,128},{80,144},{96,160},{112,17... | collective-permute-start | bytes 196616 | tf_op jit(solution)/shard_map/ppermute | solution.py:237
  66.1 2.5 %copy-start.2 = (bf16[16,64,128]{2,1,0:T(8,128)(2,1)}, bf16[16,64,128]{2,1,0:T(8,128)(2,1)S(1)}, u32[]{:S(2)}) copy-start(bf16[16,64,128]{2,1,0:T(8,128)(2,1)S(1)} %all-to-all-done.1) | copy-start | bytes 786436
  90.2 6.1 %collective-permute-start.12 = (f32[16,96,128]{2,1,0:T(8,128)}, f32[16,96,128]{2,1,0:T(8,128)S(1)}, u32[]{:S(2)}, u32[]{:S(2)}) collective-permute-start(f32[16,96,128]{2,1,0:T(8,128)} %get-tuple-element.21), channel_id=1, source_target_pairs={{0,16},{16,0},{32,48},{48,32},{64,80},{80,64},{96,112},{112,96},{1... | collective-permute-start | bytes 2359304 | tf_op jit(solution)/shard_map/ppermute | solution.py:237
  92.9 10.8 %all-to-all-start.2 = ((bf16[16,64,128]{2,1,0:T(8,128)(2,1)}), bf16[16,64,128]{2,1,0:T(8,128)(2,1)S(1)}, u32[]{:S(2)}, u32[]{:S(2)}) async-start(bf16[16,64,128]{2,1,0:T(8,128)(2,1)} %bitcast.32), calls=%async_computation.2 | async-start | bytes 524288 | tf_op jit(solution)/shard_map/all_to_all | solution.py:299
  103.7 9.3 %copy-start.1 = (bf16[16,64,128]{2,1,0:T(8,128)(2,1)}, bf16[16,64,128]{2,1,0:T(8,128)(2,1)S(1)}, u32[]{:S(2)}) copy-start(bf16[16,64,128]{2,1,0:T(8,128)(2,1)S(1)} %all-to-all-done.2.context_ref) | copy-start | bytes 786436
  103.7 24.3 %all-to-all-start.3 = ((bf16[16,96,128]{2,1,0:T(8,128)(2,1)}), bf16[16,96,128]{2,1,0:T(8,128)(2,1)S(1)}, u32[]{:S(2)}, u32[]{:S(2)}) async-start(bf16[16,96,128]{2,1,0:T(8,128)(2,1)} %add_convert_fusion), calls=%async_computation.3 | async-start | bytes 786432 | tf_op jit(solution)/shard_map/all_to_all | solution.py:298
  128.0 0.7 copy-start

commit v2 on v1

v2 whole, which is shorter than its diff:
```python
import functools

import jax
import jax.numpy as jnp
from jax import lax
from jax.experimental import pallas as pl
from jax.experimental.pallas import tpu as pltpu
from jax.sharding import PartitionSpec as P

H = 16
HD = 64
V = 48
PIX = 4
D = 1024
ROWS = 64
F32 = jnp.float32
BF16 = jnp.bfloat16
PIECES = 10
MIB = 1024 * 1024
VMEM_MIB = 58

NN = (((1,), (0,)), ((), ()))
NT = (((1,), (1,)), ((), ()))
TN = (((0,), (0,)), ((), ()))


def mm(a, b, dims=NN):
    return lax.dot_general(a, b, dims, preferred_element_type=F32)


def split2(x):
    high = x.astype(BF16)
    return high, (x - high.astype(F32)).astype(BF16)


def fetch(pairs, sems, first=0):
    copies = [pltpu.make_async_copy(a, b, sems.at[first + i]) for i, (a, b) in enumerate(pairs)]
    for copy in copies:
        copy.start()
    return copies


def prep_kernel(
    ids_ref, query_ref, var_embed_ref, embed_hbm, value_hbm, key_hbm, cot_hbm, out_w_hbm,
    place_ref, score_ref, grad_ref, table_hbm,
    embed_ref, value_ref, key_ref, cot_ref, out_w_ref, table_ref, embed_rows_ref, sems,
):
    copies = fetch(
        [(embed_hbm, embed_ref), (value_hbm, value_ref), (key_hbm, key_ref), (cot_hbm, cot_ref), (out_w_hbm, out_w_ref)], sems
    )
    count = place_ref.shape[1]
    slot = lax.broadcasted_iota(jnp.int32, (V, count), 0)
    col = lax.broadcasted_iota(jnp.int32, (V, count), 1)
    here = ((col // 16) * 3 + (col % 16) // PIX == slot) & (col % 16 < 3 * PIX)
    ids = jnp.broadcast_to(ids_ref[...].reshape(1, V).astype(F32).astype(BF16), (8, V))
    variable = mm(ids, here.astype(F32).astype(BF16))[:1].astype(jnp.int32)
    row = lax.broadcasted_iota(jnp.int32, (V * PIX, count), 0)
    col = lax.broadcasted_iota(jnp.int32, (V * PIX, count), 1)
    match = (variable + V * (col % PIX) == row) & (col % 16 < 3 * PIX)
    place_ref[...] = match.astype(F32).astype(BF16)
    copies[0].wait()
    for n in range(V):
        embed_rows_ref[n * PIX:(n + 1) * PIX, :] = embed_ref[n].astype(F32)
    row = lax.broadcasted_iota(jnp.int32, (V * PIX, V * PIX), 0)
    col = lax.broadcasted_iota(jnp.int32, (V * PIX, V * PIX), 1)
    order = ((row % V) * PIX + row // V == col).astype(F32).astype(BF16)
    table = jnp.concatenate(
        [mm(order, embed_rows_ref[...].astype(BF16)).astype(BF16), var_embed_ref[...]], axis=0
    )
    copies[1].wait()
    values = mm(table, value_ref[...]).T
    high, low = split2(values)
    for h in range(H):
        table_ref[h, :HD, :] = high[h * HD:(h + 1) * HD]
        table_ref[h, HD:, :] = low[h * HD:(h + 1) * HD]
    saved = pltpu.make_async_copy(table_ref, table_hbm, sems.at[5])
    saved.start()
    head = lax.broadcasted_iota(jnp.int32, (H, D), 0)
    feature = lax.broadcasted_iota(jnp.int32, (H, D), 1)
    query = jnp.where(feature // HD == head, query_ref[...].astype(F32).reshape(1, D) * HD ** (-0.5), 0.0)
    copies[2].wait()
    key_query = mm(query.astype(BF16), key_ref[...], NT)
    first = key_query.astype(BF16)
    rest = key_query - first.astype(F32)
    second = rest.astype(BF16)
    third = (rest - second.astype(F32)).astype(BF16)
    score_ref[...] = mm(table, first, NT) + (mm(table, second, NT) + mm(table, third, NT))
    copies[3].wait()
    copies[4].wait()
    grad = mm(cot_ref[...].reshape(2 * ROWS, D), out_w_ref[...], NT).astype(BF16)
    for j in range(H):
        r = (j % 2) * ROWS
        own = grad[r:r + ROWS, j * HD:(j + 1) * HD]
        other = grad[r:r + ROWS, (j ^ 1) * HD:((j ^ 1) + 1) * HD]
        grad_ref[j] = jnp.concatenate([own, other], axis=1)
    saved.wait()


def token_kernel(
    place_ref, fields_ref, score_ref, table_hbm, agg_out_hbm, pos_ref, lead_ref, lead_table_ref, gain_ref,
    core_ref, tokens_ref, keep_ref, send_ref, normed_ref, rows_ref, table_ref, agg_out_ref, sems,
):
    copies = fetch([(table_hbm, table_ref), (agg_out_hbm, agg_out_ref)], sems)
    rows_ref[...] = jnp.zeros_like(rows_ref)
    for j in range(H):
        rows_ref[16 * j:16 * j + 3 * PIX, :] = fields_ref[j]
    pixels = mm(place_ref[...], rows_ref[...])
    parts = [pixels[k * V:(k + 1) * V] for k in range(PIX)]
    mixed = []
    for h in range(H):
        column = lambda k: score_ref[k * V:(k + 1) * V, h:h + 1]
        scores = column(PIX) + parts[0] * column(0)
        for k in range(1, PIX):
            scores = scores + parts[k] * column(k)
        probs = jnp.exp(scores - jnp.max(scores, axis=0, keepdims=True))
        probs = probs / jnp.sum(probs, axis=0, keepdims=True)
        mixing = jnp.concatenate([probs * part for part in parts] + [probs], axis=0)
        mixed.append(split2(mixing))
    copies[0].wait()
    pooled = []
    for h in range(H):
        high, low = mixed[h]
        both = mm(table_ref[h], high)
        pooled.append((both[:HD] + (both[HD:] + mm(table_ref[h, :HD], low))).astype(BF16))
    pooled = jnp.concatenate(pooled, axis=0)
    copies[1].wait()
    tokens = mm(pooled, agg_out_ref[...], TN)
    row = lax.broadcasted_iota(jnp.int32, (2 * ROWS, 16), 0)
    col = lax.broadcasted_iota(jnp.int32, (2 * ROWS, 16), 1)
    lead = jnp.where(row < ROWS, lead_ref[0], lead_ref[1])
    lead_rows = mm((lead == col).astype(F32).astype(BF16), lead_table_ref[...])
    pos = pos_ref[...].astype(F32)
    tokens = tokens + jnp.concatenate([pos, pos], axis=0) + lead_rows
    tokens_ref[...] = tokens
    center = tokens - jnp.mean(tokens, axis=-1, keepdims=True)
    spread = jnp.mean(center * center, axis=-1, keepdims=True)
    normed_ref[...] = (center * lax.rsqrt(spread + 1e-05) * gain_ref[...].astype(F32).reshape(1, D)).astype(BF16)
    own = pl.multiple_of(core_ref[0] * ROWS, ROWS)
    other = pl.multiple_of((1 - core_ref[0]) * ROWS, ROWS)
    keep_ref[...] = normed_ref[pl.ds(own, ROWS), :]
    send_ref[...] = normed_ref[pl.ds(other, ROWS), :]


def softmax_of(keys, queries):
    scores = mm(keys, queries, NT)
    e = jnp.exp(scores - jnp.max(scores, axis=0, keepdims=True))
    return e * (1.0 / jnp.sum(e, axis=0, keepdims=True))


def head_of(x, h):
    lane = lax.broadcasted_iota(jnp.int32, x.shape, 1)
    return jnp.where(lane // HD == h, x, jnp.zeros_like(x))


def gather_rows(pieces, x_ref):
    pairs, at = [], 0
    for piece in pieces:
        pairs.append((piece, x_ref.at[pl.ds(at, piece.shape[0])]))
        at += piece.shape[0]
    return pairs


def attention_kernel(*refs):
    pieces = refs[:PIECES]
    offset_ref, to_ref, own_w_ref, other_w_ref, grad_ctx_ref, own_ref, other_ref = refs[PIECES:PIECES + 7]
    part_refs = refs[PIECES + 7:PIECES + 11]
    x_ref, context_ref, q_ref, k_ref, v_ref, rows_ref, sems = refs[PIECES + 11:]
    copies = fetch(gather_rows(pieces, x_ref), sems)
    weight = jnp.concatenate([w for i in range(3) for w in (own_w_ref[i], other_w_ref[i])], axis=1)
    for copy in copies:
        copy.wait()
    projected = mm(x_ref[...], weight).astype(BF16)
    for i in range(H):
        rows = pl.ds(pl.multiple_of(offset_ref[i], ROWS), ROWS)
        here = projected[i * ROWS:(i + 1) * ROWS]
        q_ref[rows, :] = here[:, :128] * jnp.asarray(HD ** (-0.5), BF16)
        k_ref[rows, :] = here[:, 128:256]
        v_ref[rows, :] = here[:, 256:]
    keys, values = k_ref[...], v_ref[...]
    keys_t, values_t = keys.T, values.T
    context, dq, low, ds, gs, qs = [], [], [], [], [], []
    for h in range(2):
        queries = head_of(q_ref[...], h)
        grads = head_of(grad_ctx_ref[...], h)
        probs = softmax_of(keys, queries)
        probs_low = probs.astype(BF16)
        context.append(mm(values_t[h * HD:(h + 1) * HD], probs_low))
        dp = mm(values, grads, NT)
        dots = jnp.sum(probs * dp, axis=0, keepdims=True)
        d = (probs * (dp - dots)).astype(BF16)
        dq.append(mm(keys_t[h * HD:(h + 1) * HD], d))
        low.append(probs_low)
        ds.append(d)
        gs.append(grads)
        qs.append(queries)
    context_ref[...] = jnp.concatenate(context, axis=0).T.astype(BF16)
    for i in range(H):
        part_refs[i // 4][i % 4] = context_ref[pl.ds(pl.multiple_of(to_ref[i], ROWS), ROWS), :]
    dq = (jnp.concatenate(dq, axis=0).T * HD ** (-0.5)).astype(BF16)
    dv = mm(jnp.concatenate(low, axis=1), jnp.concatenate(gs, axis=0)).astype(BF16)
    dk = mm(jnp.concatenate(ds, axis=1), jnp.concatenate(qs, axis=0)).astype(BF16)
    rows_ref[:, :128] = jnp.concatenate([dq[:, :HD], dk[:, :HD]], axis=1)
    rows_ref[:, 128:256] = jnp.concatenate([dq[:, HD:], dk[:, HD:]], axis=1)
    rows_ref[:, 256:] = dv
    order = [rows_ref[pl.ds(pl.multiple_of(offset_ref[i], ROWS), ROWS), :] for i in range(H)]
    grad = mm(x_ref[...], jnp.concatenate(order, axis=0), TN).astype(BF16)
    for j in range(H):
        top = grad[j * ROWS:j * ROWS + ROWS // 2, 256:]
        bottom = grad[j * ROWS + ROWS // 2:(j + 1) * ROWS, 256:]
        own_ref[j, :ROWS] = grad[j * ROWS:(j + 1) * ROWS, :128]
        own_ref[j, ROWS:] = jnp.concatenate([top[:, :HD], bottom[:, :HD]], axis=1)
        other_ref[j, :ROWS] = grad[j * ROWS:(j + 1) * ROWS, 128:256]
        other_ref[j, ROWS:] = jnp.concatenate([top[:, HD:], bottom[:, HD:]], axis=1)


def output_kernel(from_ref, core_ref, *refs):
    near = refs[:4]
    along = refs[4:7]
    out_w_ref, tokens_ref, out_ref, context_ref = refs[7:]
    core = core_ref[0]
    for dx in range(4):
        for i in range(4):
            part = along[dx - 1][i] if dx else near[i][0]
            sample = core if i % 2 == 0 else 1 - core
            part = jnp.where(sample == 1, jnp.concatenate([part[:, HD:], part[:, :HD]], axis=1), part)
            context_ref[from_ref[dx * 2 + i // 2], pl.ds(pl.multiple_of(sample * ROWS, ROWS), ROWS), :] = part
    context = jnp.concatenate([context_ref[m] for m in range(H // 2)], axis=1)
    out_ref[...] = (tokens_ref[...] + mm(context, out_w_ref[...])).astype(BF16)


def sum_kernel(parts_ref, out_ref):
    total = parts_ref[0].astype(F32)
    for j in range(1, H):
        total = total + parts_ref[j].astype(F32)
    out_ref[0] = total[:ROWS, :HD]
    out_ref[1] = total[:ROWS, HD:]
    out_ref[2, :ROWS // 2] = total[ROWS:, :HD]
    out_ref[2, ROWS // 2:] = total[ROWS:, HD:]


VM = pl.BlockSpec(memory_space=pltpu.VMEM)
SM = pl.BlockSpec(memory_space=pltpu.SMEM)
ANY = pl.BlockSpec(memory_space=pl.ANY)


def call(kernel, out, in_specs, name, scratch=(), out_specs=None, mib=VMEM_MIB):
    return pl.pallas_call(
        kernel,
        out_shape=out,
        in_specs=in_specs,
        out_specs=out_specs or jax.tree.map(lambda _: VM, out),
        scratch_shapes=list(scratch),
        compiler_params=pltpu.CompilerParams(vmem_limit_bytes=mib * MIB),
        name=name,
    )


def shape(dims, dtype):
    return jax.ShapeDtypeStruct(dims, dtype)


def on_device(
    fields, var_ids, lead_index, embed_weight, var_embed, agg_query, agg_key, agg_value, agg_out,
    pos_embed, lead_table, norm_gain, qkv_weight, out_weight, cotangent,
):
    place = lax.axis_index("patch")
    core = place % 2
    chip = place // 2
    pair = [(i, i ^ 1) for i in range(16)]
    move = lambda a, perm: lax.ppermute(a, "patch", perm)

    sent = fields.reshape(16, 2, 3, PIX, ROWS).transpose(0, 2, 3, 1, 4).reshape(16, 12, 128)
    owned = lax.all_to_all(sent, "var", split_axis=0, concat_axis=0, tiled=True)
    other_weight = move(qkv_weight, pair)
    placing, score, grad_parts, table = call(
        prep_kernel,
        (shape((V * PIX, 256), BF16), shape((V * (PIX + 1), H), F32), shape((H, ROWS, 128), BF16),
         shape((H, 2 * HD, V * (PIX + 1)), BF16)),
        [VM] * 3 + [ANY] * 5, "prep",
        [pltpu.VMEM((V, PIX, D), BF16)] + [pltpu.VMEM((D, D), BF16)] * 2 + [pltpu.VMEM((2, ROWS, D), BF16)]
        + [pltpu.VMEM((D, D), BF16), pltpu.VMEM((H, 2 * HD, V * (PIX + 1)), BF16), pltpu.VMEM((V * PIX, D), F32)]
        + [pltpu.SemaphoreType.DMA((6,))],
        out_specs=(VM, VM, VM, ANY),
    )(var_ids, agg_query, var_embed, embed_weight, agg_value, agg_key, cotangent, out_weight)
    table, other_weight = lax.optimization_barrier((table, other_weight))
    tokens, keep, send = call(
        token_kernel,
        (shape((2 * ROWS, D), F32), shape((ROWS, D), BF16), shape((ROWS, D), BF16)),
        [VM] * 3 + [ANY] * 2 + [VM] + [SM] + [VM] * 2 + [SM], "tokens",
        [pltpu.VMEM((2 * ROWS, D), BF16), pltpu.VMEM((16 * H, 128), BF16), pltpu.VMEM((H, 2 * HD, V * (PIX + 1)), BF16),
         pltpu.VMEM((D, D), BF16), pltpu.SemaphoreType.DMA((2,))],
    )(placing, owned, score, table, agg_out, pos_embed, lead_index, lead_table, norm_gain,
      core.reshape(1))

    here = jnp.concatenate([keep, move(send, pair)], axis=0)
    grad_parts, _ = lax.optimization_barrier((grad_parts, here))
    grad_ctx = lax.all_to_all(grad_parts, "patch", split_axis=0, concat_axis=0, tiled=True)
    shift = lambda a, dx, dy: move(a, [(i, (i + 4 * dx) % 16 ^ (2 * dy)) for i in range(16)])
    left, right, across = shift(here, 1, 0), shift(here, 3, 0), shift(here, 0, 1)
    far0, far1 = shift(left[:64], 1, 0), shift(right[64:], 3, 0)
    left1, right1 = shift(across, 1, 0), shift(across, 3, 0)
    far2, far3 = shift(far0, 0, 1), shift(far1, 0, 1)
    steps = [(1, 0), (3, 0), (0, 1), (2, 0), (1, 1), (3, 1), (2, 1)]
    pieces = [here, left, right, across, far0, far1, left1, right1, far2, far3]
    cx, cy = chip // 2, chip % 2
    chips = []
    for dx, dy in [(0, 0)] + steps:
        chips.append(((cx + 4 - dx) % 4) * 2 + (cy + dy) % 2)
    chips = jnp.stack(chips)
    offsets = (chips[:, None] * 128 + jnp.stack([core, 1 - core])[None, :] * ROWS).reshape(16)

    offsets = offsets.astype(jnp.int32)
    grad_ctx = grad_ctx.reshape(D, 128)
    dest = jnp.stack([((cx + dx) % 4) * 2 + (cy + dy) % 2 for dy in range(2) for dx in range(4)]).reshape(2, 1, 4)
    to = (dest * 128 + jnp.stack([core, 1 - core]).reshape(1, 2, 1) * ROWS).reshape(H).astype(jnp.int32)
    source = jnp.stack([((cx + 4 - dx) % 4) * 2 + (cy + dy) % 2 for dx in range(4) for dy in range(2)]).astype(jnp.int32)
    tall, quarter = pltpu.VMEM((D, 128), BF16), shape((4, ROWS, 128), BF16)
    own, other, *parts = call(
        attention_kernel, (shape((H, 96, 128), BF16),) * 2 + (quarter,) * 4, [ANY] * PIECES + [SM] * 2 + [VM] * 3, "attention",
        [pltpu.VMEM((D, D), BF16)] + [tall] * 4 + [pltpu.VMEM((D, 384), BF16), pltpu.SemaphoreType.DMA((PIECES,))],
    )(*pieces, offsets, to, qkv_weight, other_weight, grad_ctx)
    partial_grad = (own.astype(F32) + move(other, pair).astype(F32)).astype(BF16)
    swap = lambda a, dy, dc: move(a, [(i, i ^ (2 * dy + dc)) for i in range(16)])
    near = [parts[0], swap(parts[1], 0, 1), swap(parts[2], 1, 0), swap(parts[3], 1, 1)]
    sums = lax.all_to_all(partial_grad, "var", split_axis=0, concat_axis=0, tiled=True)
    along = jnp.stack(near, axis=1)
    along = [shift(along[dx], dx, 0) for dx in (1, 2, 3)]
    layer_out = call(
        output_kernel, shape((2 * ROWS, D), BF16), [SM] * 2 + [VM] * 9, "out", [pltpu.VMEM((H // 2, 2 * ROWS, 128), BF16)], mib=8,
    )(source, core.reshape(1), *near, *along, out_weight, tokens)
    grad_qkv = call(sum_kernel, shape((3, ROWS, HD), F32), [VM], "sum", mib=4)(sums)
    return layer_out.reshape(2, ROWS, D), grad_qkv


def solution(mesh):
    in_specs = (
        P(None, "var", None, "patch"), P(), P("var"), P(), P(), P(), P(), P(), P(), P("patch", None), P(), P(),
        P(None, None, "patch"), P(), P("var", "patch", None),
    )
    out_specs = (P("var", "patch", None), P(None, "var", "patch"))
    return jax.shard_map(on_device, mesh=mesh, in_specs=in_specs, out_specs=out_specs, check_vma=False)
```

time: 131 us -> 105 us (0.80)
  waiting for transfers between devices: 32.8 us -> 18.1 us
  Pallas kernels: 37.1 us -> 29.3 us
  local copies, waits for them, and re-layouts: 13.3 us -> 7.92 us
    all_to_all x1, waiting for transfers between devices: 12 us -> 0.01 us  [on_device(): lax.all_to_all(partial_grad, 'var', split_axis=0, concat_axis=0, tiled=True)]
    ppermute x13 -> x18, starting transfers between devices: 14.4 us -> 23.4 us  [on_device(): move = lambda a, perm: lax.ppermute(a, 'patch', perm)]
    pallas_call x3, Pallas kernels: 26.3 us -> 17.7 us  [the longest x1 15.1 us: on_device(): call(attention_kernel, (shape((H, 96, 128), BF16),) * 2 + (quarter,) * 4,...]
    reshape x5 -> x0, local copies, waits for them, and re-layouts: 6.24 us -> none  [the longest x1 1.85 us: on_device(): embed_weight.reshape(V * PIX, D)]
    all_to_all x2 -> x1, starting transfers between devices: 15.2 us -> 9.18 us  [on_device(): owned = lax.all_to_all(sent, 'var', split_axis=0, concat_axis=0, tiled=True)]
    all_to_all x1, starting transfers between devices: 9.33 us -> 5.75 us  [on_device(): lax.all_to_all(partial_grad, 'var', split_axis=0, concat_axis=0, tiled=True)]
    all_to_all x2 -> x1, waiting for transfers between devices: 5.4 us -> 2.3 us  [on_device(): owned = lax.all_to_all(sent, 'var', split_axis=0, concat_axis=0, tiled=True)]
    squeeze x0 -> x1, other arithmetic: none -> 1.41 us  [on_device(): along = [shift(along[dx], dx, 0) for dx in (1, 2, 3)]]
  transfers between devices with their start and end apart: 17 -> 21, of which waited for: 7 -> 11; matrix products, arithmetic and copies ran while one was open for 10% -> 8% of each run, Pallas kernels for 7% -> 8%
where the time goes in v2:
time: 105 us; the launch traced here: 104 us
  starting transfers between devices  44.6 us (42%)
  Pallas kernels  29.3 us (28%)
  waiting for transfers between devices  18.1 us (17%)
  local copies, waits for them, and re-layouts  7.92 us (8%)
  other arithmetic  3.47 us (3%)
    ppermute x18, starting transfers between devices, on_device(): move = lambda a, perm: lax.ppermute(a, 'patch', perm)  23.4 us
    ppermute x18, waiting for transfers between devices, on_device(): move = lambda a, perm: lax.ppermute(a, 'patch', perm)  15.8 us
    pallas_call x1, Pallas kernels, on_device(): call(attention_kernel, (shape((H, 96, 128), BF16),) * 2 + (quarter,) * 4,...  15.1 us
    all_to_all x1, starting transfers between devices, on_device(): owned = lax.all_to_all(sent, 'var', split_axis=0, concat_axis=0, tiled=True)  9.18 us
    pallas_call x1, Pallas kernels, on_device(): call(prep_kernel, (shape((V * PIX, 256), BF16), shape((V * (PIX + 1), H),...  6.85 us
    all_to_all x1, starting transfers between devices, on_device(): lax.all_to_all(grad_parts, 'patch', split_axis=0, concat_axis=0, tiled=True)  6.23 us
    all_to_all x1, starting transfers between devices, on_device(): lax.all_to_all(partial_grad, 'var', split_axis=0, concat_axis=0, tiled=True)  5.75 us
    pallas_call x1, Pallas kernels, on_device(): call(token_kernel, (shape((2 * ROWS, D), F32), shape((ROWS, D), BF16), sh...  4.77 us
  transfers between devices with their start and end apart: 21, of which 11 were waited for; matrix products, arithmetic and copies ran while one was open for 8% of the time, Pallas kernels for 8%

profile of v2, /device:TPU:1, one launch (start us, length us, event | category | flops | bytes accessed | tf_op | source)
XLA Modules:
  0.0 104.4 jit_solution(5233670263221918680)
XLA Ops:
  0.6 3.3 %collective-permute-start = (bf16[3,1024,64]{1,2,0:T(8,128)(2,1)}, bf16[3,1024,64]{1,2,0:T(8,128)(2,1)S(1)}, u32[]{:S(2)}, u32[]{:S(2)}) collective-permute-start(bf16[3,1024,64]{1,2,0:T(8,128)(2,1)} %param.27), channel_id=1, source_target_pairs={{0,16},{16,0},{32,48},{48,32},{64,80},{80,64},{96,112},{112,96},{1... | collective-permute-start | bytes 1179656 | tf_op jit(solution)/shard_map/ppermute | solution.py:270
  4.0 1.0 copy.29
  5.7 9.2 %all-to-all-start = ((bf16[16,12,128]{2,1,0:T(8,128)(2,1)}), bf16[16,12,128]{2,1,0:T(8,128)(2,1)S(1)}, u32[]{:S(2)}, u32[]{:S(2)}) async-start(bf16[16,12,128]{2,1,0:T(8,128)(2,1)} %copy.25), calls=%async_computation | async-start | bytes 131072 | tf_op jit(solution)/shard_map/all_to_all | solution.py:273
  15.1 6.9 %prep.1 = (bf16[192,256]{1,0:T(8,128)(2,1)}, f32[240,16]{1,0:T(8,128)}, bf16[16,64,128]{2,1,0:T(8,128)(2,1)}, bf16[16,128,240]{2,1,0:T(8,128)(2,1)}) custom-call(s32[48]{0:T(128)} %ids_ref.1, bf16[1024]{0:T(1024)(128)(2,1)} %query_ref.1, bf16[48,1024]{1,0:T(8,128)(2,1)} %var_embed_ref.1, bf16[48,4,1024]{2,1,0:T(4,128)(2,1)} %embed_hbm.1, ...), custom_call_target="tpu_custom_call" | custom-call | tf_op jit(solution)/shard_map/prep/pallas_call | solution.py:275
  22.0 2.3 %all-to-all-done.fields_ref = bf16[16,12,128]{2,1,0:T(8,128)(2,1)S(1)} async-done(((bf16[16,12,128]{2,1,0:T(8,128)(2,1)}), bf16[16,12,128]{2,1,0:T(8,128)(2,1)S(1)}, u32[]{:S(2)}, u32[]{:S(2)}) %all-to-all-start) | async-done | bytes 49184 | tf_op jit(solution)/shard_map/all_to_all | solution.py:273
  24.9 4.8 %tokens.1 = (f32[128,1024]{1,0:T(8,128)}, bf16[64,1024]{1,0:T(8,128)(2,1)}, bf16[64,1024]{1,0:T(8,128)(2,1)}) custom-call(bf16[192,256]{1,0:T(8,128)(2,1)} %get-tuple-element.18.place_ref, bf16[16,12,128]{2,1,0:T(8,128)(2,1)} %copy-done.11, f32[240,16]{1,0:T(8,128)} %get-tuple-element.19.score_ref, bf16[16,128,240]{2,1,0:T(8,128)(2,1)} %get-tuple-element.21.table_hbm, ...), custom_call_target="tpu_custom_call" | custom-call | tf_op jit(solution)/shard_map/tokens/pallas_call | solution.py:286
  29.7 1.5 %collective-permute-start.1 = (bf16[64,1024]{1,0:T(8,128)(2,1)}, bf16[64,1024]{1,0:T(8,128)(2,1)S(1)}, u32[]{:S(2)}, u32[]{:S(2)}) collective-permute-start(bf16[64,1024]{1,0:T(8,128)(2,1)} %get-tuple-element.23), channel_id=1, source_target_pairs={{0,16},{16,0},{32,48},{48,32},{64,80},{80,64},{96,112},{112,96},{1... | collective-permute-start | bytes 393224 | tf_op jit(solution)/shard_map/ppermute | solution.py:270
  31.2 0.9 constant_dynamic-update-slice_fusion.1
  32.9 2.5 %collective-permute-start.3 = (bf16[128,1024]{1,0:T(8,128)(2,1)S(1)}, bf16[128,1024]{1,0:T(8,128)(2,1)S(1)}, u32[]{:S(2)}, u32[]{:S(2)}) collective-permute-start(bf16[128,1024]{1,0:T(8,128)(2,1)S(1)} %constant_dynamic-update-slice_fusion.refs_0_), channel_id=1, source_target_pairs={{0,192},{16,208},{32,224},{48,240},{64,0},{80,16},{96,32},{112,48}... | collective-permute-start | bytes 786440 | tf_op jit(solution)/shard_map/ppermute | solution.py:270
  35.7 6.2 %all-to-all-start.1 = ((bf16[16,64,128]{2,1,0:T(8,128)(2,1)}), bf16[16,64,128]{2,1,0:T(8,128)(2,1)S(1)}, u32[]{:S(2)}, u32[]{:S(2)}) async-start(bf16[16,64,128]{2,1,0:T(8,128)(2,1)} %get-tuple-element.26), calls=%async_computation.1 | async-start | bytes 524288 | tf_op jit(solution)/shard_map/all_to_all | solution.py:297
  42.0 2.7 %collective-permute-start.6 = (bf16[64,1024]{1,0:T(8,128)(2,1)S(1)}, bf16[64,1024]{1,0:T(8,128)(2,1)S(1)}, u32[]{:S(2)}, u32[]{:S(2)}) collective-permute-start(bf16[64,1024]{1,0:T(8,128)(2,1)S(1)} %slice.21), channel_id=1, source_target_pairs={{0,192},{16,208},{32,224},{48,240},{64,0},{80,16},{96,32},{112,48}... | collective-permute-start | bytes 393224 | tf_op jit(solution)/shard_map/ppermute | solution.py:270
  44.8 2.6 %collective-permute-start.8 = (bf16[128,1024]{1,0:T(8,128)(2,1)S(1)}, bf16[128,1024]{1,0:T(8,128)(2,1)S(1)}, u32[]{:S(2)}, u32[]{:S(2)}) collective-permute-start(bf16[128,1024]{1,0:T(8,128)(2,1)S(1)} %collective-permute-done.4.refs_3_), channel_id=1, source_target_pairs={{0,192},{16,208},{32,224},{48,240},{64,0},{80,16},{96,32},{112,48}... | collective-permute-start | bytes 786440 | tf_op jit(solution)/shard_map/ppermute | solution.py:270
  47.4 1.2 %copy.26.refs_12_ = bf16[3,1024,64]{2,1,0:T(8,128)(2,1)} copy(bf16[3,1024,64]{1,2,0:T(8,128)(2,1)S(1)} %copy-done.7) | data formatting | bytes 786432 | tf_op args[12]
  49.9 1.2 %collective-permute-start.10 = (bf16[64,1024]{1,0:T(8,128)(2,1)S(1)}, bf16[64,1024]{1,0:T(8,128)(2,1)S(1)}, u32[]{:S(2)}, u32[]{:S(2)}) collective-permute-start(bf16[64,1024]{1,0:T(8,128)(2,1)S(1)} %collective-permute-done.6.refs_5_), channel_id=1, source_target_pairs={{0,32},{16,48},{32,0},{48,16},{64,96},{80,112},{96,64},{112,80},{1... | collective-permute-start | bytes 393224 | tf_op jit(solution)/shard_map/ppermute | solution.py:270
  52.4 1.2 %copy.27.refs_13_ = bf16[3,1024,64]{2,1,0:T(8,128)(2,1)} copy(bf16[3,1024,64]{1,2,0:T(8,128)(2,1)S(1)} %collective-permute-done) | data formatting | bytes 786432 | tf_op jit(solution)/shard_map/optimization_barrier | solution.py:285
  54.0 2.3 %collective-permute-done.9.refs_8_ = bf16[64,1024]{1,0:T(8,128)(2,1)S(1)} collective-permute-done((bf16[64,1024]{1,0:T(8,128)(2,1)S(1)}, bf16[64,1024]{1,0:T(8,128)(2,1)S(1)}, u32[]{:S(2)}, u32[]{:S(2)}) %collective-permute-start.9) | collective-permute-done | bytes 131104 | tf_op jit(solution)/shard_map/ppermute | solution.py:270
  57.2 15.1 %attention.1 = (bf16[16,96,128]{2,1,0:T(8,128)(2,1)}, bf16[16,96,128]{2,1,0:T(8,128)(2,1)}, bf16[4,64,128]{2,1,0:T(8,128)(2,1)}, bf16[4,64,128]{2,1,0:T(8,128)(2...) custom-call(bf16[128,1024]{1,0:T(8,128)(2,1)} %copy-done.6, bf16[128,1024]{1,0:T(8,128)(2,1)} %copy-done.5, ...), custom_call_target="tpu_custom_call" | custom-call | tf_op jit(solution)/shard_map/attention/pallas_call | solution.py:318
  72.3 2.4 %collective-permute-start.17 = (bf16[16,96,128]{2,1,0:T(8,128)(2,1)}, bf16[16,96,128]{2,1,0:T(8,128)(2,1)S(1)}, u32[]{:S(2)}, u32[]{:S(2)}) collective-permute-start(bf16[16,96,128]{2,1,0:T(8,128)(2,1)} %get-tuple-element.33), channel_id=1, source_target_pairs={{0,16},{16,0},{32,48},{48,32},{64,80},{80,64},{96,112},{112,96},{1... | collective-permute-start | bytes 1179656 | tf_op jit(solution)/shard_map/ppermute | solution.py:270
  74.7 1.6 %collective-permute-done.17 = bf16[16,96,128]{2,1,0:T(8,128)(2,1)S(1)} collective-permute-done((bf16[16,96,128]{2,1,0:T(8,128)(2,1)}, bf16[16,96,128]{2,1,0:T(8,128)(2,1)S(1)}, u32[]{:S(2)}, u32[]{:S(2)}) %collective-permute-start.17) | collective-permute-done | bytes 393248 | tf_op jit(solution)/shard_map/ppermute | solution.py:270
  76.3 1.8 %add_convert_fusion = bf16[16,96,128]{2,1,0:T(8,128)(2,1)} fusion(bf16[16,96,128]{2,1,0:T(8,128)(2,1)S(1)} %collective-permute-done.17, bf16[16,96,128]{2,1,0:T(8,128)(2,1)} %get-tuple-element.32), kind=kLoop, calls=%fused_computation | loop fusion | flops 786432 | bytes 1179648 | tf_op jit(solution)/shard_map/convert_element_type | solution.py:322
  78.1 5.7 %all-to-all-start.2 = ((bf16[16,96,128]{2,1,0:T(8,128)(2,1)}), bf16[16,96,128]{2,1,0:T(8,128)(2,1)S(1)}, u32[]{:S(2)}, u32[]{:S(2)}) async-start(bf16[16,96,128]{2,1,0:T(8,128)(2,1)} %add_convert_fusion), calls=%async_computation.2 | async-start | bytes 786432 | tf_op jit(solution)/shard_map/all_to_all | solution.py:325
  83.9 0.7 collective-permute-start.11
  85.2 1.4 %collective-permute-start.13 = (bf16[4,64,128]{2,1,0:T(8,128)(2,1)}, bf16[4,64,128]{2,1,0:T(8,128)(2,1)S(1)}, u32[]{:S(2)}, u32[]{:S(2)}) collective-permute-start(bf16[4,64,128]{2,1,0:T(8,128)(2,1)} %get-tuple-element.30), channel_id=1, source_target_pairs={{0,48},{16,32},{32,16},{48,0},{64,112},{80,96},{96,80},{112,64},{1... | collective-permute-start | bytes 196616 | tf_op jit(solution)/shard_map/ppermute | solution.py:270
  86.5 1.4 %collective-permute-done.12.refs_2_ = bf16[4,64,128]{2,1,0:T(8,128)(2,1)S(1)} collective-permute-done((bf16[4,64,128]{2,1,0:T(8,128)(2,1)}, bf16[4,64,128]{2,1,0:T(8,128)(2,1)S(1)}, u32[]{:S(2)}, u32[]{:S(2)}) %collective-permute-start.12) | collective-permute-done | bytes 65568 | tf_op jit(solution)/shard_map/ppermute | solution.py:270
  87.9 3.1 %collective-permute-done.13.refs_3_ = bf16[4,64,128]{2,1,0:T(8,128)(2,1)S(1)} collective-permute-done((bf16[4,64,128]{2,1,0:T(8,128)(2,1)}, bf16[4,64,128]{2,1,0:T(8,128)(2,1)S(1)}, u32[]{:S(2)}, u32[]{:S(2)}) %collective-permute-start.13) | collective-permute-done | bytes 65568 | tf_op jit(solution)/shard_map/ppermute | solution.py:270
  91.0 1.4 %fusion = (bf16[4,64,128]{2,1,0:T(8,128)(2,1)}, bf16[4,64,128]{2,1,0:T(8,128)(2,1)}, bf16[4,64,128]{2,1,0:T(8,128)(2,1)S(1)}) fusion(bf16[4,1,64,128]{3,2,1,0:T(8,128)(2,1)S(1)} %bitcast.33, bf16[4,1,64,128]{3,2,1,0:T(8,128)(2,1)S(1)} %bitcast.32, bf16[4,1,64,128]{3,2,1,0:T(8,128)(2,1)S(1)} %bitcast.31, bf16[4,1,64,128]{3,2,1,0:T(8,128)(2,1)} %bitcast.30), kind=kLoop, calls=%fused_computation.3 | loop fusion | flops 294912 | bytes 458752 | tf_op jit(solution)/shard_map/squeeze | solution.py:327
  92.4 2.3 %collective-permute-start.16 = (bf16[4,64,128]{2,1,0:T(8,128)(2,1)}, bf16[4,64,128]{2,1,0:T(8,128)(2,1)S(1)}, u32[]{:S(2)}, u32[]{:S(2)}) collective-permute-start(bf16[4,64,128]{2,1,0:T(8,128)(2,1)} %get-tuple-element.34), channel_id=1, source_target_pairs={{0,192},{16,208},{32,224},{48,240},{64,0},{80,16},{96,32},{112,48}... | collective-permute-start | bytes 196616 | tf_op jit(solution)/shard_map/ppermute | solution.py:270
  95.8 2.4 %collective-permute-done.16.refs_6_ = bf16[4,64,128]{2,1,0:T(8,128)(2,1)S(1)} collective-permute-done((bf16[4,64,128]{2,1,0:T(8,128)(2,1)}, bf16[4,64,128]{2,1,0:T(8,128)(2,1)S(1)}, u32[]{:S(2)}, u32[]{:S(2)}) %collective-permute-start.16) | collective-permute-done | bytes 65568 | tf_op jit(solution)/shard_map/ppermute | solution.py:270
  98.2 2.2 %collective-permute-done.15.refs_5_ = bf16[4,64,128]{2,1,0:T(8,128)(2,1)S(1)} collective-permute-done((bf16[4,64,128]{2,1,0:T(8,128)(2,1)}, bf16[4,64,128]{2,1,0:T(8,128)(2,1)S(1)}, u32[]{:S(2)}, u32[]{:S(2)}) %collective-permute-start.15) | collective-permute-done | bytes 65568 | tf_op jit(solution)/shard_map/ppermute | solution.py:270
  100.4 1.5 %collective-permute-done.14.refs_4_ = bf16[4,64,128]{2,1,0:T(8,128)(2,1)S(1)} collective-permute-done((bf16[4,64,128]{2,1,0:T(8,128)(2,1)S(1)}, bf16[4,64,128]{2,1,0:T(8,128)(2,1)S(1)}, u32[]{:S(2)}, u32[]{:S(2)}) %collective-permute-start.14) | collective-permute-done | bytes 65568 | tf_op jit(solution)/shard_map/ppermute | solution.py:270
  101.8 1.8 %out.1 = bf16[128,1024]{1,0:T(8,128)(2,1)} custom-call(s32[8]{0:T(128)S(1)} %stack.86.from_ref, s32[1]{0:T(128)} %bitcast.8.core_ref, bf16[4,64,128]{2,1,0:T(8,128)(2,1)S(1)} %copy-done.2, bf16[4,64,128]{2,1,0:T(8,128)(2,1)S(1)} %collective-permute-done.11.refs_1_, bf16[4,64,128]{2,1,0:T(8,128)(2,1)S(1)} %collective-permute-done.12.refs_2_, ...), custom_call_target="tpu_custom_call" | custom-call | tf_op jit(solution)/shard_map/out/pallas_call | solution.py:328
  103.6 0.8 sum.1
  (69 shorter events, 8.2 us)
Async XLA Ops:
  0.6 21.3 %collective-permute-start = (bf16[3,1024,64]{1,2,0:T(8,128)(2,1)}, bf16[3,1024,64]{1,2,0:T(8,128)(2,1)S(1)}, u32[]{:S(2)}, u32[]{:S(2)}) collective-permute-start(bf16[3,1024,64]{1,2,0:T(8,128)(2,1)} %param.27), channel_id=1, source_target_pairs={{0,16},{16,0},{32,48},{48,32},{64,80},{80,64},{96,112},{112,96},{1... | collective-permute-start | bytes 1179656 | tf_op jit(solution)/shard_map/ppermute | solution.py:270
  5.7 18.6 %all-to-all-start = ((bf16[16,12,128]{2,1,0:T(8,128)(2,1)}), bf16[16,12,128]{2,1,0:T(8,128)(2,1)S(1)}, u32[]{:S(2)}, u32[]{:S(2)}) async-start(bf16[16,12,128]{2,1,0:T(8,128)(2,1)} %copy.25), calls=%async_computation | async-start | bytes 131072 | tf_op jit(solution)/shard_map/all_to_all | solution.py:273
  24.9 22.5 %copy-start.7 = (bf16[3,1024,64]{1,2,0:T(8,128)(2,1)S(1)}, bf16[3,1024,64]{1,2,0:T(8,128)(2,1)}, u32[]{:S(2)}) copy-start(bf16[3,1024,64]{1,2,0:T(8,128)(2,1)} %param.27) | copy-start | bytes 1179652
  29.7 2.7 %collective-permute-start.1 = (bf16[64,1024]{1,0:T(8,128)(2,1)}, bf16[64,1024]{1,0:T(8,128)(2,1)S(1)}, u32[]{:S(2)}, u32[]{:S(2)}) collective-permute-start(bf16[64,1024]{1,0:T(8,128)(2,1)} %get-tuple-element.23), channel_id=1, source_target_pairs={{0,16},{16,0},{32,48},{48,32},{64,80},{80,64},{96,112},{112,96},{1... | collective-permute-start | bytes 393224 | tf_op jit(solution)/shard_map/ppermute | solution.py:270
  32.4 24.0 %copy-start.6 = (bf16[128,1024]{1,0:T(8,128)(2,1)}, bf16[128,1024]{1,0:T(8,128)(2,1)S(1)}, u32[]{:S(2)}) copy-start(bf16[128,1024]{1,0:T(8,128)(2,1)S(1)} %constant_dynamic-update-slice_fusion.refs_0_) | copy-start | bytes 786436
  32.4 12.3 %collective-permute-start.4 = (bf16[128,1024]{1,0:T(8,128)(2,1)S(1)}, bf16[128,1024]{1,0:T(8,128)(2,1)S(1)}, u32[]{:S(2)}, u32[]{:S(2)}) collective-permute-start(bf16[128,1024]{1,0:T(8,128)(2,1)S(1)} %constant_dynamic-update-slice_fusion.refs_0_), channel_id=1, source_target_pairs={{0,32},{16,48},{32,0},{48,16},{64,96},{80,112},{96,64},{112,80},{1... | collective-permute-start | bytes 786440 | tf_op jit(solution)/shard_map/ppermute | solution.py:270
  32.9 9.0 %collective-permute-start.3 = (bf16[128,1024]{1,0:T(8,128)(2,1)S(1)}, bf16[128,1024]{1,0:T(8,128)(2,1)S(1)}, u32[]{:S(2)}, u32[]{:S(2)}) collective-permute-start(bf16[128,1024]{1,0:T(8,128)(2,1)S(1)} %constant_dynamic-update-slice_fusion.refs_0_), channel_id=1, source_target_pairs={{0,192},{16,208},{32,224},{48,240},{64,0},{80,16},{96,32},{112,48}... | collective-permute-start | bytes 786440 | tf_op jit(solution)/shard_map/ppermute | solution.py:270
  35.4 9.3 %collective-permute-start.2 = (bf16[128,1024]{1,0:T(8,128)(2,1)S(1)}, bf16[128,1024]{1,0:T(8,128)(2,1)S(1)}, u32[]{:S(2)}, u32[]{:S(2)}) collective-permute-start(bf16[128,1024]{1,0:T(8,128)(2,1)S(1)} %constant_dynamic-update-slice_fusion.refs_0_), channel_id=1, source_target_pairs={{0,64},{16,80},{32,96},{48,112},{64,128},{80,144},{96,160},{112,17... | collective-permute-start | bytes 786440 | tf_op jit(solution)/shard_map/ppermute | solution.py:270
  35.7 17.9 %all-to-all-start.1 = ((bf16[16,64,128]{2,1,0:T(8,128)(2,1)}), bf16[16,64,128]{2,1,0:T(8,128)(2,1)S(1)}, u32[]{:S(2)}, u32[]{:S(2)}) async-start(bf16[16,64,128]{2,1,0:T(8,128)(2,1)} %get-tuple-element.26), calls=%async_computation.1 | async-start | bytes 524288 | tf_op jit(solution)/shard_map/all_to_all | solution.py:297
  41.9 14.5 %copy-start.4 = (bf16[128,1024]{1,0:T(8,128)(2,1)}, bf16[128,1024]{1,0:T(8,128)(2,1)S(1)}, u32[]{:S(2)}) copy-start(bf16[128,1024]{1,0:T(8,128)(2,1)S(1)} %collective-permute-done.3.refs_2_) | copy-start | bytes 786436
  42.0 7.9 %collective-permute-start.6 = (bf16[64,1024]{1,0:T(8,128)(2,1)S(1)}, bf16[64,1024]{1,0:T(8,128)(2,1)S(1)}, u32[]{:S(2)}, u32[]{:S(2)}) collective-permute-start(bf16[64,1024]{1,0:T(8,128)(2,1)S(1)} %slice.21), channel_id=1, source_target_pairs={{0,192},{16,208},{32,224},{48,240},{64,0},{80,16},{96,32},{112,48}... | collective-permute-start | bytes 393224 | tf_op jit(solution)/shard_map/ppermute | solution.py:270
  44.6 11.8 %copy-start.5 = (bf16[128,1024]{1,0:T(8,128)(2,1)}, bf16[128,1024]{1,0:T(8,128)(2,1)S(1)}, u32[]{:S(2)}) copy-start(bf16[128,1024]{1,0:T(8,128)(2,1)S(1)} %collective-permute-done.2.refs_1_) | copy-start | bytes 786436
  44.7 6.4 %collective-permute-start.5 = (bf16[64,1024]{1,0:T(8,128)(2,1)S(1)}, bf16[64,1024]{1,0:T(8,128)(2,1)S(1)}, u32[]{:S(2)}, u32[]{:S(2)}) collective-permute-start(bf16[64,1024]{1,0:T(8,128)(2,1)S(1)} %slice.20), channel_id=1, source_target_pairs={{0,64},{16,80},{32,96},{48,112},{64,128},{80,144},{96,160},{112,17... | collective-permute-start | bytes 393224 | tf_op jit(solution)/shard_map/ppermute | solution.py:270
  44.8 11.7 %copy-start.8 = (bf16[128,1024]{1,0:T(8,128)(2,1)}, bf16[128,1024]{1,0:T(8,128)(2,1)S(1)}, u32[]{:S(2)}) copy-start(bf16[128,1024]{1,0:T(8,128)(2,1)S(1)} %collective-permute-done.4.refs_3_) | copy-start | bytes 786436
  44.8 11.6 %collective-permute-start.8 = (bf16[128,1024]{1,0:T(8,128)(2,1)S(1)}, bf16[128,1024]{1,0:T(8,128)(2,1)S(1)}, u32[]{:S(2)}, u32[]{:S(2)}) collective-permute-start(bf16[128,1024]{1,0:T(8,128)(2,1)S(1)} %collective-permute-done.4.refs_3_), channel_id=1, source_target_pairs={{0,192},{16,208},{32,224},{48,240},{64,0},{80,16},{96,32},{112,48}... | collective-permute-start | bytes 786440 | tf_op jit(solution)/shard_map/ppermute | solution.py:270
  47.4 8.9 %collective-permute-start.7 = (bf16[128,1024]{1,0:T(8,128)(2,1)S(1)}, bf16[128,1024]{1,0:T(8,128)(2,1)S(1)}, u32[]{:S(2)}, u32[]{:S(2)}) collective-permute-start(bf16[128,1024]{1,0:T(8,128)(2,1)S(1)} %collective-permute-done.4.refs_3_), channel_id=1, source_target_pairs={{0,64},{16,80},{32,96},{48,112},{64,128},{80,144},{96,160},{112,17... | collective-permute-start | bytes 786440 | tf_op jit(solution)/shard_map/ppermute | solution.py:270
  49.9 6.5 %copy-start.12 = (bf16[64,1024]{1,0:T(8,128)(2,1)}, bf16[64,1024]{1,0:T(8,128)(2,1)S(1)}, u32[]{:S(2)}) copy-start(bf16[64,1024]{1,0:T(8,128)(2,1)S(1)} %collective-permute-done.6.refs_5_) | copy-start | bytes 393220
  49.9 4.1 %collective-permute-start.10 = (bf16[64,1024]{1,0:T(8,128)(2,1)S(1)}, bf16[64,1024]{1,0:T(8,128)(2,1)S(1)}, u32[]{:S(2)}, u32[]{:S(2)}) collective-permute-start(bf16[64,1024]{1,0:T(8,128)(2,1)S(1)} %collective-permute-done.6.refs_5_), channel_id=1, source_target_pairs={{0,32},{16,48},{32,0},{48,16},{64,96},{80,112},{96,64},{112,80},{1... | collective-permute-start | bytes 393224 | tf_op jit(solution)/shard_map/ppermute | solution.py:270
  51.1 5.3 %copy-start.13 = (bf16[64,1024]{1,0:T(8,128)(2,1)}, bf16[64,1024]{1,0:T(8,128)(2,1)S(1)}, u32[]{:S(2)}) copy-start(bf16[64,1024]{1,0:T(8,128)(2,1)S(1)} %collective-permute-done.5.refs_4_) | copy-start | bytes 393220
  51.1 5.3 %collective-permute-start.9 = (bf16[64,1024]{1,0:T(8,128)(2,1)S(1)}, bf16[64,1024]{1,0:T(8,128)(2,1)S(1)}, u32[]{:S(2)}, u32[]{:S(2)}) collective-permute-start(bf16[64,1024]{1,0:T(8,128)(2,1)S(1)} %collective-permute-done.5.refs_4_), channel_id=1, source_target_pairs={{0,32},{16,48},{32,0},{48,16},{64,96},{80,112},{96,64},{112,80},{1... | collective-permute-start | bytes 393224 | tf_op jit(solution)/shard_map/ppermute | solution.py:270
  53.6 2.8 %copy-start.3 = (bf16[16,64,128]{2,1,0:T(8,128)(2,1)}, bf16[16,64,128]{2,1,0:T(8,128)(2,1)S(1)}, u32[]{:S(2)}) copy-start(bf16[16,64,128]{2,1,0:T(8,128)(2,1)S(1)} %all-to-all-done.1) | copy-start | bytes 786436
  57.2 44.6 %copy-start.1 = (f32[128,1024]{1,0:T(8,128)S(1)}, f32[128,1024]{1,0:T(8,128)}, u32[]{:S(2)}) copy-start(f32[128,1024]{1,0:T(8,128)} %get-tuple-element.31.refs_8_) | copy-start | bytes 1572868
  72.3 29.5 %copy-start = (bf16[1024,1024]{1,0:T(8,128)(2,1)S(1)}, bf16[1024,1024]{1,0:T(8,128)(2,1)}, u32[]{:S(2)}) copy-start(bf16[1024,1024]{1,0:T(8,128)(2,1)} %refs_7_.1) | copy-start | bytes 6291460
  72.3 29.5 %copy-start.2 = (bf16[4,64,128]{2,1,0:T(8,128)(2,1)S(1)}, bf16[4,64,128]{2,1,0:T(8,128)(2,1)}, u32[]{:S(2)}) copy-start(bf16[4,64,128]{2,1,0:T(8,128)(2,1)} %get-tuple-element.27.refs_0_) | copy-start | bytes 196612
  72.3 3.9 %collective-permute-start.17 = (bf16[16,96,128]{2,1,0:T(8,128)(2,1)}, bf16[16,96,128]{2,1,0:T(8,128)(2,1)S(1)}, u32[]{:S(2)}, u32[]{:S(2)}) collective-permute-start(bf16[16,96,128]{2,1,0:T(8,128)(2,1)} %get-tuple-element.33), channel_id=1, source_target_pairs={{0,16},{16,0},{32,48},{48,32},{64,80},{80,64},{96,112},{112,96},{1... | collective-permute-start | bytes 1179656 | tf_op jit(solution)/shard_map/ppermute | solution.py:270
  78.1 25.6 %all-to-all-start.2 = ((bf16[16,96,128]{2,1,0:T(8,128)(2,1)}), bf16[16,96,128]{2,1,0:T(8,128)(2,1)S(1)}, u32[]{:S(2)}, u32[]{:S(2)}) async-start(bf16[16,96,128]{2,1,0:T(8,128)(2,1)} %add_convert_fusion), calls=%async_computation.2 | async-start | bytes 786432 | tf_op jit(solution)/shard_map/all_to_all | solution.py:325
  83.9 2.7 %collective-permute-start.11 = (bf16[4,64,128]{2,1,0:T(8,128)(2,1)}, bf16[4,64,128]{2,1,0:T(8,128)(2,1)S(1)}, u32[]{:S(2)}, u32[]{:S(2)}) collective-permute-start(bf16[4,64,128]{2,1,0:T(8,128)(2,1)} %get-tuple-element.28), channel_id=1, source_target_pairs={{0,16},{16,0},{32,48},{48,32},{64,80},{80,64},{96,112},{112,96},{1... | collective-permute-start | bytes 196616 | tf_op jit(solution)/shard_map/ppermute | solution.py:270
  84.6 3.3 %collective-permute-start.12 = (bf16[4,64,128]{2,1,0:T(8,128)(2,1)}, bf16[4,64,128]{2,1,0:T(8,128)(2,1)S(1)}, u32[]{:S(2)}, u32[]{:S(2)}) collective-permute-start(bf16[4,64,128]{2,1,0:T(8,128)(2,1)} %get-tuple-element.29), channel_id=1, source_target_pairs={{0,32},{16,48},{32,0},{48,16},{64,96},{80,112},{96,64},{112,80},{1... | collective-permute-start | bytes 196616 | tf_op jit(solution)/shard_map/ppermute | solution.py:270
  85.2 5.8 %collective-permute-start.13 = (bf16[4,64,128]{2,1,0:T(8,128)(2,1)}, bf16[4,64,128]{2,1,0:T(8,128)(2,1)S(1)}, u32[]{:S(2)}, u32[]{:S(2)}) collective-permute-start(bf16[4,64,128]{2,1,0:T(8,128)(2,1)} %get-tuple-element.30), channel_id=1, source_target_pairs={{0,48},{16,32},{32,16},{48,0},{64,112},{80,96},{96,80},{112,64},{1... | collective-permute-start | bytes 196616 | tf_op jit(solution)/shard_map/ppermute | solution.py:270
  92.4 5.8 %collective-permute-start.16 = (bf16[4,64,128]{2,1,0:T(8,128)(2,1)}, bf16[4,64,128]{2,1,0:T(8,128)(2,1)S(1)}, u32[]{:S(2)}, u32[]{:S(2)}) collective-permute-start(bf16[4,64,128]{2,1,0:T(8,128)(2,1)} %get-tuple-element.34), channel_id=1, source_target_pairs={{0,192},{16,208},{32,224},{48,240},{64,0},{80,16},{96,32},{112,48}... | collective-permute-start | bytes 196616 | tf_op jit(solution)/shard_map/ppermute | solution.py:270
  94.7 5.7 %collective-permute-start.15 = (bf16[4,64,128]{2,1,0:T(8,128)(2,1)}, bf16[4,64,128]{2,1,0:T(8,128)(2,1)S(1)}, u32[]{:S(2)}, u32[]{:S(2)}) collective-permute-start(bf16[4,64,128]{2,1,0:T(8,128)(2,1)} %get-tuple-element.35), channel_id=1, source_target_pairs={{0,128},{16,144},{32,160},{48,176},{64,192},{80,208},{96,224},{112... | collective-permute-start | bytes 196616 | tf_op jit(solution)/shard_map/ppermute | solution.py:270
  95.4 6.4 %collective-permute-start.14 = (bf16[4,64,128]{2,1,0:T(8,128)(2,1)S(1)}, bf16[4,64,128]{2,1,0:T(8,128)(2,1)S(1)}, u32[]{:S(2)}, u32[]{:S(2)}) collective-permute-start(bf16[4,64,128]{2,1,0:T(8,128)(2,1)S(1)} %get-tuple-element.36), channel_id=1, source_target_pairs={{0,64},{16,80},{32,96},{48,112},{64,128},{80,144},{96,160},{112,17... | collective-permute-start | bytes 196616 | tf_op jit(solution)/shard_map/ppermute | solution.py:270
  (5 other events, 5.3 us)

commit v3 on v2

--- a/solution.py
+++ b/solution.py
@@ -135,8 +135,9 @@
     center = tokens - jnp.mean(tokens, axis=-1, keepdims=True)
     spread = jnp.mean(center * center, axis=-1, keepdims=True)
     normed_ref[...] = (center * lax.rsqrt(spread + 1e-05) * gain_ref[...].astype(F32).reshape(1, D)).astype(BF16)
-    own = pl.multiple_of(core_ref[0] * ROWS, ROWS)
-    other = pl.multiple_of((1 - core_ref[0]) * ROWS, ROWS)
+    core = core_ref[0] % 2
+    own = pl.multiple_of(core * ROWS, ROWS)
+    other = pl.multiple_of((1 - core) * ROWS, ROWS)
     keep_ref[...] = normed_ref[pl.ds(own, ROWS), :]
     send_ref[...] = normed_ref[pl.ds(other, ROWS), :]
 
@@ -150,6 +151,14 @@
 def head_of(x, h):
     lane = lax.broadcasted_iota(jnp.int32, x.shape, 1)
     return jnp.where(lane // HD == h, x, jnp.zeros_like(x))
+
+
+STEPS = [(0, 0), (1, 0), (3, 0), (0, 1), (2, 0), (1, 1), (3, 1), (2, 1)]
+
+
+def chip_at(place, dx, dy):
+    chip = place // 2
+    return (chip // 2 + dx) % 4 * 2 + (chip + dy) % 2
 
 
 def gather_rows(pieces, x_ref):
@@ -160,18 +169,35 @@
     return pairs
 
 
+def project_kernel(*refs):
+    pieces = refs[:PIECES - 2]
+    own_w_ref, other_w_ref, out_ref, x_ref, sems = refs[PIECES - 2:]
+    copies = fetch(gather_rows(pieces, x_ref), sems)
+    weight = jnp.concatenate([w for i in range(3) for w in (own_w_ref[i], other_w_ref[i])], axis=0)
+    for copy in copies:
+        copy.wait()
+    out_ref[...] = mm(x_ref[...], weight, NT).astype(BF16)
+
+
 def attention_kernel(*refs):
     pieces = refs[:PIECES]
-    offset_ref, to_ref, own_w_ref, other_w_ref, grad_ctx_ref, own_ref, other_ref = refs[PIECES:PIECES + 7]
+    place_ref, projected_hbm, own_w_ref, other_w_ref, grad_ctx_ref, own_ref, other_ref = refs[PIECES:PIECES + 7]
     part_refs = refs[PIECES + 7:PIECES + 11]
-    x_ref, context_ref, q_ref, k_ref, v_ref, rows_ref, sems = refs[PIECES + 11:]
-    copies = fetch(gather_rows(pieces, x_ref), sems)
-    weight = jnp.concatenate([w for i in range(3) for w in (own_w_ref[i], other_w_ref[i])], axis=1)
-    for copy in copies:
+    x_ref, projected_ref, context_ref, q_ref, k_ref, v_ref, rows_ref, sems = refs[PIECES + 11:]
+    place = place_ref[0]
+    core = place % 2
+    rows_at = lambda dx, dy, s: pl.ds(pl.multiple_of(chip_at(place, dx, dy) * 128 + jnp.abs(core - s) * ROWS, ROWS), ROWS)
+    offsets = [rows_at(4 - dx, dy, s) for dx, dy in STEPS for s in range(2)]
+    done = D - 2 * ROWS
+    pairs = gather_rows(pieces, x_ref)
+    copies = fetch([(projected_hbm, projected_ref.at[pl.ds(0, done)])] + pairs[-2:] + pairs[:-2], sems)
+    weight = jnp.concatenate([w for i in range(3) for w in (own_w_ref[i], other_w_ref[i])], axis=0)
+    for copy in copies[:3]:
         copy.wait()
-    projected = mm(x_ref[...], weight).astype(BF16)
+    projected_ref[done:, :] = mm(x_ref[done:, :], weight, NT).astype(BF16)
+    projected = projected_ref[...]
     for i in range(H):
-        rows = pl.ds(pl.multiple_of(offset_ref[i], ROWS), ROWS)
+        rows = offsets[i]
         here = projected[i * ROWS:(i + 1) * ROWS]
         q_ref[rows, :] = here[:, :128] * jnp.asarray(HD ** (-0.5), BF16)
         k_ref[rows, :] = here[:, 128:256]
@@ -195,15 +221,17 @@
         qs.append(queries)
     context_ref[...] = jnp.concatenate(context, axis=0).T.astype(BF16)
     for i in range(H):
-        part_refs[i // 4][i % 4] = context_ref[pl.ds(pl.multiple_of(to_ref[i], ROWS), ROWS), :]
+        part_refs[i // 4][i % 4] = context_ref[rows_at(i % 4, i // 8, i // 4 % 2), :]
     dq = (jnp.concatenate(dq, axis=0).T * HD ** (-0.5)).astype(BF16)
     dv = mm(jnp.concatenate(low, axis=1), jnp.concatenate(gs, axis=0)).astype(BF16)
     dk = mm(jnp.concatenate(ds, axis=1), jnp.concatenate(qs, axis=0)).astype(BF16)
     rows_ref[:, :128] = jnp.concatenate([dq[:, :HD], dk[:, :HD]], axis=1)
     rows_ref[:, 128:256] = jnp.concatenate([dq[:, HD:], dk[:, HD:]], axis=1)
     rows_ref[:, 256:] = dv
-    order = [rows_ref[pl.ds(pl.multiple_of(offset_ref[i], ROWS), ROWS), :] for i in range(H)]
-    grad = mm(x_ref[...], jnp.concatenate(order, axis=0), TN).astype(BF16)
+    order = jnp.concatenate([rows_ref[rows, :] for rows in offsets], axis=0)
+    for copy in copies[3:]:
+        copy.wait()
+    grad = mm(x_ref[...], order, TN).astype(BF16)
     for j in range(H):
         top = grad[j * ROWS:j * ROWS + ROWS // 2, 256:]
         bottom = grad[j * ROWS + ROWS // 2:(j + 1) * ROWS, 256:]
@@ -213,19 +241,24 @@
         other_ref[j, ROWS:] = jnp.concatenate([top[:, HD:], bottom[:, HD:]], axis=1)
 
 
-def output_kernel(from_ref, core_ref, *refs):
+def output_kernel(place_ref, *refs):
     near = refs[:4]
     along = refs[4:7]
     out_w_ref, tokens_ref, out_ref, context_ref = refs[7:]
-    core = core_ref[0]
+    place = place_ref[0]
+    core = place % 2
     for dx in range(4):
         for i in range(4):
             part = along[dx - 1][i] if dx else near[i][0]
             sample = core if i % 2 == 0 else 1 - core
             part = jnp.where(sample == 1, jnp.concatenate([part[:, HD:], part[:, :HD]], axis=1), part)
-            context_ref[from_ref[dx * 2 + i // 2], pl.ds(pl.multiple_of(sample * ROWS, ROWS), ROWS), :] = part
+            context_ref[chip_at(place, 4 - dx, i // 2), pl.ds(pl.multiple_of(sample * ROWS, ROWS), ROWS), :] = part
     context = jnp.concatenate([context_ref[m] for m in range(H // 2)], axis=1)
     out_ref[...] = (tokens_ref[...] + mm(context, out_w_ref[...])).astype(BF16)
+
+
+def add_kernel(a_ref, b_ref, out_ref):
+    out_ref[...] = (a_ref[...].astype(F32) + b_ref[...].astype(F32)).astype(BF16)
 
 
 def sum_kernel(parts_ref, out_ref):
@@ -264,14 +297,13 @@
     pos_embed, lead_table, norm_gain, qkv_weight, out_weight, cotangent,
 ):
     place = lax.axis_index("patch")
-    core = place % 2
-    chip = place // 2
     pair = [(i, i ^ 1) for i in range(16)]
     move = lambda a, perm: lax.ppermute(a, "patch", perm)
 
     sent = fields.reshape(16, 2, 3, PIX, ROWS).transpose(0, 2, 3, 1, 4).reshape(16, 12, 128)
     owned = lax.all_to_all(sent, "var", split_axis=0, concat_axis=0, tiled=True)
-    other_weight = move(qkv_weight, pair)
+    own_weight = qkv_weight.transpose(0, 2, 1)
+    other_weight = move(own_weight, pair)
     placing, score, grad_parts, table = call(
         prep_kernel,
         (shape((V * PIX, 256), BF16), shape((V * (PIX + 1), H), F32), shape((H, ROWS, 128), BF16),
@@ -290,7 +322,7 @@
         [pltpu.VMEM((2 * ROWS, D), BF16), pltpu.VMEM((16 * H, 128), BF16), pltpu.VMEM((H, 2 * HD, V * (PIX + 1)), BF16),
          pltpu.VMEM((D, D), BF16), pltpu.SemaphoreType.DMA((2,))],
     )(placing, owned, score, table, agg_out, pos_embed, lead_index, lead_table, norm_gain,
-      core.reshape(1))
+      place.reshape(1))
 
     here = jnp.concatenate([keep, move(send, pair)], axis=0)
     grad_parts, _ = lax.optimization_barrier((grad_parts, here))
@@ -299,35 +331,28 @@
     left, right, across = shift(here, 1, 0), shift(here, 3, 0), shift(here, 0, 1)
     far0, far1 = shift(left[:64], 1, 0), shift(right[64:], 3, 0)
     left1, right1 = shift(across, 1, 0), shift(across, 3, 0)
+    far0, far1, grad_ctx = lax.optimization_barrier((far0, far1, grad_ctx))
     far2, far3 = shift(far0, 0, 1), shift(far1, 0, 1)
-    steps = [(1, 0), (3, 0), (0, 1), (2, 0), (1, 1), (3, 1), (2, 1)]
     pieces = [here, left, right, across, far0, far1, left1, right1, far2, far3]
-    cx, cy = chip // 2, chip % 2
-    chips = []
-    for dx, dy in [(0, 0)] + steps:
-        chips.append(((cx + 4 - dx) % 4) * 2 + (cy + dy) % 2)
-    chips = jnp.stack(chips)
-    offsets = (chips[:, None] * 128 + jnp.stack([core, 1 - core])[None, :] * ROWS).reshape(16)
-
-    offsets = offsets.astype(jnp.int32)
     grad_ctx = grad_ctx.reshape(D, 128)
-    dest = jnp.stack([((cx + dx) % 4) * 2 + (cy + dy) % 2 for dy in range(2) for dx in range(4)]).reshape(2, 1, 4)
-    to = (dest * 128 + jnp.stack([core, 1 - core]).reshape(1, 2, 1) * ROWS).reshape(H).astype(jnp.int32)
-    source = jnp.stack([((cx + 4 - dx) % 4) * 2 + (cy + dy) % 2 for dx in range(4) for dy in range(2)]).astype(jnp.int32)
     tall, quarter = pltpu.VMEM((D, 128), BF16), shape((4, ROWS, 128), BF16)
+    projected = call(
+        project_kernel, shape((D - 2 * ROWS, 384), BF16), [ANY] * (PIECES - 2) + [VM] * 2, "project",
+        [pltpu.VMEM((D - 2 * ROWS, D), BF16), pltpu.SemaphoreType.DMA((PIECES - 2,))],
+    )(*pieces[:-2], own_weight, other_weight)
     own, other, *parts = call(
-        attention_kernel, (shape((H, 96, 128), BF16),) * 2 + (quarter,) * 4, [ANY] * PIECES + [SM] * 2 + [VM] * 3, "attention",
-        [pltpu.VMEM((D, D), BF16)] + [tall] * 4 + [pltpu.VMEM((D, 384), BF16), pltpu.SemaphoreType.DMA((PIECES,))],
-    )(*pieces, offsets, to, qkv_weight, other_weight, grad_ctx)
-    partial_grad = (own.astype(F32) + move(other, pair).astype(F32)).astype(BF16)
+        attention_kernel, (shape((H, 96, 128), BF16),) * 2 + (quarter,) * 4, [ANY] * PIECES + [SM, ANY] + [VM] * 3, "attention",
+        [pltpu.VMEM((D, D), BF16), pltpu.VMEM((D, 384), BF16)] + [tall] * 4 + [pltpu.VMEM((D, 384), BF16), pltpu.SemaphoreType.DMA((PIECES + 1,))],
+    )(*pieces, place.reshape(1), projected, own_weight, other_weight, grad_ctx)
+    partial_grad = call(add_kernel, shape((H, 96, 128), BF16), [VM] * 2, "add", mib=4)(own, move(other, pair))
     swap = lambda a, dy, dc: move(a, [(i, i ^ (2 * dy + dc)) for i in range(16)])
     near = [parts[0], swap(parts[1], 0, 1), swap(parts[2], 1, 0), swap(parts[3], 1, 1)]
     sums = lax.all_to_all(partial_grad, "var", split_axis=0, concat_axis=0, tiled=True)
     along = jnp.stack(near, axis=1)
     along = [shift(along[dx], dx, 0) for dx in (1, 2, 3)]
     layer_out = call(
-        output_kernel, shape((2 * ROWS, D), BF16), [SM] * 2 + [VM] * 9, "out", [pltpu.VMEM((H // 2, 2 * ROWS, 128), BF16)], mib=8,
-    )(source, core.reshape(1), *near, *along, out_weight, tokens)
+        output_kernel, shape((2 * ROWS, D), BF16), [SM] + [VM] * 9, "out", [pltpu.VMEM((H // 2, 2 * ROWS, 128), BF16)], mib=8,
+    )(place.reshape(1), *near, *along, out_weight, tokens)
     grad_qkv = call(sum_kernel, shape((3, ROWS, HD), F32), [VM], "sum", mib=4)(sums)
     return layer_out.reshape(2, ROWS, D), grad_qkv
 

time: 105 us -> 105 us (level)
  Pallas kernels: 29.3 us -> 32.9 us
  other arithmetic: 3.47 us -> 0.78 us
  waiting for transfers between devices: 18.1 us -> 20.7 us
  starting transfers between devices: 44.6 us -> 42.6 us
  local copies, waits for them, and re-layouts: 7.92 us -> 5.99 us
    pallas_call x1 -> x3, Pallas kernels: 1.8 us -> 6.7 us  [the longest x1 4.58 us: on_device(): call(project_kernel, shape((D - 2 * ROWS, 384), BF16), [ANY] * (PIECES -...]
    all_to_all x1, waiting for transfers between devices: 0.01 us -> 2.03 us  [on_device(): lax.all_to_all(grad_parts, 'patch', split_axis=0, concat_axis=0, tiled=True)]
    ppermute x18, starting transfers between devices: 23.4 us -> 21.4 us  [on_device(): move = lambda a, perm: lax.ppermute(a, 'patch', perm)]
    convert_element_type x1 -> x0, other arithmetic: 1.84 us -> none  [on_device(): (own.astype(F32) + move(other, pair).astype(F32)).astype(BF16)]
    pallas_call x1, Pallas kernels: 15.1 us -> 13.8 us  [on_device(): call(attention_kernel, (shape((H, 96, 128), BF16),) * 2 + (quarter,) * 4,...]
    add x2 -> x0, local copies, waits for them, and re-layouts: 1.2 us -> none  [the longest x1 0.62 us: on_device(): chips[:, None] * 128 + jnp.stack([core, 1 - core])[None, :] * ROWS]
    optimization_barrier x1 -> x0, local copies, waits for them, and re-layouts: 1.16 us -> none  [on_device(): table, other_weight = lax.optimization_barrier((table, other_weight))]
    unnamed x34 -> x35, local copies, waits for them, and re-layouts: 3.49 us -> 4.25 us
  transfers between devices with their start and end apart: 21 -> 21, of which waited for: 11 -> 13; matrix products, arithmetic and copies ran while one was open for 8% -> 3% of each run, Pallas kernels for 8% -> 12%
where the time goes in v3:
time: 105 us; the launch traced here: 104 us
  starting transfers between devices  42.6 us (41%)
  Pallas kernels  32.9 us (31%)
  waiting for transfers between devices  20.7 us (20%)
  local copies, waits for them, and re-layouts  5.99 us (6%)
    ppermute x18, starting transfers between devices, on_device(): move = lambda a, perm: lax.ppermute(a, 'patch', perm)  21.4 us
    ppermute x18, waiting for transfers between devices, on_device(): move = lambda a, perm: lax.ppermute(a, 'patch', perm)  16.2 us
    pallas_call x1, Pallas kernels, on_device(): call(attention_kernel, (shape((H, 96, 128), BF16),) * 2 + (quarter,) * 4,...  13.8 us
    all_to_all x1, starting transfers between devices, on_device(): owned = lax.all_to_all(sent, 'var', split_axis=0, concat_axis=0, tiled=True)  9.18 us
    pallas_call x1, Pallas kernels, on_device(): call(prep_kernel, (shape((V * PIX, 256), BF16), shape((V * (PIX + 1), H),...  6.86 us
    all_to_all x1, starting transfers between devices, on_device(): lax.all_to_all(grad_parts, 'patch', split_axis=0, concat_axis=0, tiled=True)  6.23 us
    all_to_all x1, starting transfers between devices, on_device(): lax.all_to_all(partial_grad, 'var', split_axis=0, concat_axis=0, tiled=True)  5.72 us
    pallas_call x1, Pallas kernels, on_device(): call(token_kernel, (shape((2 * ROWS, D), F32), shape((ROWS, D), BF16), sh...  4.75 us
  transfers between devices with their start and end apart: 21, of which 13 were waited for; matrix products, arithmetic and copies ran while one was open for 3% of the time, Pallas kernels for 12%

profile of v3, /device:TPU:1, one launch (start us, length us, event | category | flops | bytes accessed | tf_op | source)
XLA Modules:
  0.0 103.8 jit_solution(12655667331858698480)
XLA Ops:
  0.6 3.3 %collective-permute-start = (bf16[3,64,1024]{2,1,0:T(8,128)(2,1)}, bf16[3,64,1024]{2,1,0:T(8,128)(2,1)S(1)}, u32[]{:S(2)}, u32[]{:S(2)}) collective-permute-start(bf16[3,64,1024]{2,1,0:T(8,128)(2,1)} %bitcast.24), channel_id=1, source_target_pairs={{0,16},{16,0},{32,48},{48,32},{64,80},{80,64},{96,112},{112,96},{1... | collective-permute-start | bytes 1179656 | tf_op jit(solution)/shard_map/ppermute | solution.py:301
  4.0 1.0 copy.21
  5.7 9.2 %all-to-all-start = ((bf16[16,12,128]{2,1,0:T(8,128)(2,1)}), bf16[16,12,128]{2,1,0:T(8,128)(2,1)S(1)}, u32[]{:S(2)}, u32[]{:S(2)}) async-start(bf16[16,12,128]{2,1,0:T(8,128)(2,1)} %copy.19), calls=%async_computation | async-start | bytes 131072 | tf_op jit(solution)/shard_map/all_to_all | solution.py:304
  14.9 6.9 %prep.1 = (bf16[192,256]{1,0:T(8,128)(2,1)}, f32[240,16]{1,0:T(8,128)}, bf16[16,64,128]{2,1,0:T(8,128)(2,1)}, bf16[16,128,240]{2,1,0:T(8,128)(2,1)}) custom-call(s32[48]{0:T(128)} %ids_ref.1, bf16[1024]{0:T(1024)(128)(2,1)} %query_ref.1, bf16[48,1024]{1,0:T(8,128)(2,1)} %var_embed_ref.1, bf16[48,4,1024]{2,1,0:T(4,128)(2,1)} %embed_hbm.1, ...), custom_call_target="tpu_custom_call" | custom-call | tf_op jit(solution)/shard_map/prep/pallas_call | solution.py:307
  21.8 2.5 %all-to-all-done.fields_ref = bf16[16,12,128]{2,1,0:T(8,128)(2,1)S(1)} async-done(((bf16[16,12,128]{2,1,0:T(8,128)(2,1)}), bf16[16,12,128]{2,1,0:T(8,128)(2,1)S(1)}, u32[]{:S(2)}, u32[]{:S(2)}) %all-to-all-start) | async-done | bytes 49184 | tf_op jit(solution)/shard_map/all_to_all | solution.py:304
  24.9 4.8 %tokens.1 = (f32[128,1024]{1,0:T(8,128)}, bf16[64,1024]{1,0:T(8,128)(2,1)}, bf16[64,1024]{1,0:T(8,128)(2,1)}) custom-call(bf16[192,256]{1,0:T(8,128)(2,1)} %get-tuple-element.21.place_ref, bf16[16,12,128]{2,1,0:T(8,128)(2,1)} %copy-done.14, f32[240,16]{1,0:T(8,128)} %get-tuple-element.22.score_ref, bf16[16,128,240]{2,1,0:T(8,128)(2,1)} %get-tuple-element.24.table_hbm, ...), custom_call_target="tpu_custom_call" | custom-call | tf_op jit(solution)/shard_map/tokens/pallas_call | solution.py:318
  29.6 1.5 %collective-permute-start.1 = (bf16[64,1024]{1,0:T(8,128)(2,1)}, bf16[64,1024]{1,0:T(8,128)(2,1)S(1)}, u32[]{:S(2)}, u32[]{:S(2)}) collective-permute-start(bf16[64,1024]{1,0:T(8,128)(2,1)} %get-tuple-element.26), channel_id=1, source_target_pairs={{0,16},{16,0},{32,48},{48,32},{64,80},{80,64},{96,112},{112,96},{1... | collective-permute-start | bytes 393224 | tf_op jit(solution)/shard_map/ppermute | solution.py:301
  31.2 0.9 constant_dynamic-update-slice_fusion.1
  32.4 2.6 %collective-permute-start.3 = (bf16[128,1024]{1,0:T(8,128)(2,1)S(1)}, bf16[128,1024]{1,0:T(8,128)(2,1)S(1)}, u32[]{:S(2)}, u32[]{:S(2)}) collective-permute-start(bf16[128,1024]{1,0:T(8,128)(2,1)S(1)} %constant_dynamic-update-slice_fusion.refs_0_), channel_id=1, source_target_pairs={{0,192},{16,208},{32,224},{48,240},{64,0},{80,16},{96,32},{112,48}... | collective-permute-start | bytes 786440 | tf_op jit(solution)/shard_map/ppermute | solution.py:301
  35.3 6.2 %all-to-all-start.1 = ((bf16[16,64,128]{2,1,0:T(8,128)(2,1)}), bf16[16,64,128]{2,1,0:T(8,128)(2,1)S(1)}, u32[]{:S(2)}, u32[]{:S(2)}) async-start(bf16[16,64,128]{2,1,0:T(8,128)(2,1)} %get-tuple-element.28), calls=%async_computation.1 | async-start | bytes 524288 | tf_op jit(solution)/shard_map/all_to_all | solution.py:329
  41.6 2.7 %collective-permute-start.6 = (bf16[64,1024]{1,0:T(8,128)(2,1)S(1)}, bf16[64,1024]{1,0:T(8,128)(2,1)S(1)}, u32[]{:S(2)}, u32[]{:S(2)}) collective-permute-start(bf16[64,1024]{1,0:T(8,128)(2,1)S(1)} %slice.21), channel_id=1, source_target_pairs={{0,192},{16,208},{32,224},{48,240},{64,0},{80,16},{96,32},{112,48}... | collective-permute-start | bytes 393224 | tf_op jit(solution)/shard_map/ppermute | solution.py:301
  44.4 2.6 %collective-permute-start.8 = (bf16[128,1024]{1,0:T(8,128)(2,1)S(1)}, bf16[128,1024]{1,0:T(8,128)(2,1)S(1)}, u32[]{:S(2)}, u32[]{:S(2)}) collective-permute-start(bf16[128,1024]{1,0:T(8,128)(2,1)S(1)} %collective-permute-done.4.refs_3_), channel_id=1, source_target_pairs={{0,192},{16,208},{32,224},{48,240},{64,0},{80,16},{96,32},{112,48}... | collective-permute-start | bytes 786440 | tf_op jit(solution)/shard_map/ppermute | solution.py:301
  47.1 2.0 %all-to-all-done.1 = bf16[16,64,128]{2,1,0:T(8,128)(2,1)S(1)} async-done(((bf16[16,64,128]{2,1,0:T(8,128)(2,1)}), bf16[16,64,128]{2,1,0:T(8,128)(2,1)S(1)}, u32[]{:S(2)}, u32[]{:S(2)}) %all-to-all-start.1) | async-done | bytes 262176 | tf_op jit(solution)/shard_map/all_to_all | solution.py:329
  49.6 0.8 collective-permute-done.5.refs_4_
  50.3 1.4 %collective-permute-start.9 = (bf16[64,1024]{1,0:T(8,128)(2,1)S(1)}, bf16[64,1024]{1,0:T(8,128)(2,1)S(1)}, u32[]{:S(2)}, u32[]{:S(2)}) collective-permute-start(bf16[64,1024]{1,0:T(8,128)(2,1)S(1)} %collective-permute-done.5.refs_4_), channel_id=1, source_target_pairs={{0,32},{16,48},{32,0},{48,16},{64,96},{80,112},{96,64},{112,80},{1... | collective-permute-start | bytes 393224 | tf_op jit(solution)/shard_map/ppermute | solution.py:301
  51.8 3.4 %collective-permute-done.8.refs_7_ = bf16[128,1024]{1,0:T(8,128)(2,1)S(1)} collective-permute-done((bf16[128,1024]{1,0:T(8,128)(2,1)S(1)}, bf16[128,1024]{1,0:T(8,128)(2,1)S(1)}, u32[]{:S(2)}, u32[]{:S(2)}) %collective-permute-start.8) | collective-permute-done | bytes 262176 | tf_op jit(solution)/shard_map/ppermute | solution.py:301
  56.6 4.6 %project.1.refs_11_ = bf16[896,384]{1,0:T(8,128)(2,1)} custom-call(bf16[128,1024]{1,0:T(8,128)(2,1)} %copy-done.6, bf16[128,1024]{1,0:T(8,128)(2,1)} %copy-done.5, bf16[128,1024]{1,0:T(8,128)(2,1)} %copy-done.4, bf16[128,1024]{1,0:T(8,128)(2,1)} %copy-done.8, bf16[64,1024]{1,0:T(8,128)(2,1)} %copy-done.13, bf16[64,1024]{1,0:T(8,128)(2,1)} %copy-done.12, ...), custom_call_target="tpu_custom_call" | custom-call | tf_op jit(solution)/shard_map/project/pallas_call | solution.py:339
  61.9 13.8 %attention.1 = (bf16[16,96,128]{2,1,0:T(8,128)(2,1)}, bf16[16,96,128]{2,1,0:T(8,128)(2,1)}, bf16[4,64,128]{2,1,0:T(8,128)(2,1)}, bf16[4,64,128]{2,1,0:T(8,128)(2...) custom-call(bf16[128,1024]{1,0:T(8,128)(2,1)} %copy-done.6, bf16[128,1024]{1,0:T(8,128)(2,1)} %copy-done.5, ...), custom_call_target="tpu_custom_call" | custom-call | tf_op jit(solution)/shard_map/attention/pallas_call | solution.py:343
  75.7 1.7 %collective-permute-start.17 = (bf16[16,96,128]{2,1,0:T(8,128)(2,1)}, bf16[16,96,128]{2,1,0:T(8,128)(2,1)S(1)}, u32[]{:S(2)}, u32[]{:S(2)}) collective-permute-start(bf16[16,96,128]{2,1,0:T(8,128)(2,1)} %get-tuple-element.39), channel_id=1, source_target_pairs={{0,16},{16,0},{32,48},{48,32},{64,80},{80,64},{96,112},{112,96},{1... | collective-permute-start | bytes 1179656 | tf_op jit(solution)/shard_map/ppermute | solution.py:301
  77.4 1.6 %collective-permute-done.17.b_ref = bf16[16,96,128]{2,1,0:T(8,128)(2,1)S(1)} collective-permute-done((bf16[16,96,128]{2,1,0:T(8,128)(2,1)}, bf16[16,96,128]{2,1,0:T(8,128)(2,1)S(1)}, u32[]{:S(2)}, u32[]{:S(2)}) %collective-permute-start.17) | collective-permute-done | bytes 393248 | tf_op jit(solution)/shard_map/ppermute | solution.py:301
  79.0 1.0 copy-done.2
  80.0 0.8 add.1
  80.8 5.7 %all-to-all-start.2 = ((bf16[16,96,128]{2,1,0:T(8,128)(2,1)}), bf16[16,96,128]{2,1,0:T(8,128)(2,1)S(1)}, u32[]{:S(2)}, u32[]{:S(2)}) async-start(bf16[16,96,128]{2,1,0:T(8,128)(2,1)} %add.1), calls=%async_computation.2 | async-start | bytes 786432 | tf_op jit(solution)/shard_map/all_to_all | solution.py:350
  87.8 1.2 %collective-permute-start.13 = (bf16[4,64,128]{2,1,0:T(8,128)(2,1)}, bf16[4,64,128]{2,1,0:T(8,128)(2,1)S(1)}, u32[]{:S(2)}, u32[]{:S(2)}) collective-permute-start(bf16[4,64,128]{2,1,0:T(8,128)(2,1)} %get-tuple-element.36), channel_id=1, source_target_pairs={{0,48},{16,32},{32,16},{48,0},{64,112},{80,96},{96,80},{112,64},{1... | collective-permute-start | bytes 196616 | tf_op jit(solution)/shard_map/ppermute | solution.py:301
  89.1 2.1 %collective-permute-done.12.refs_2_ = bf16[4,64,128]{2,1,0:T(8,128)(2,1)S(1)} collective-permute-done((bf16[4,64,128]{2,1,0:T(8,128)(2,1)}, bf16[4,64,128]{2,1,0:T(8,128)(2,1)S(1)}, u32[]{:S(2)}, u32[]{:S(2)}) %collective-permute-start.12) | collective-permute-done | bytes 65568 | tf_op jit(solution)/shard_map/ppermute | solution.py:301
  91.2 2.5 %collective-permute-done.13.refs_3_ = bf16[4,64,128]{2,1,0:T(8,128)(2,1)S(1)} collective-permute-done((bf16[4,64,128]{2,1,0:T(8,128)(2,1)}, bf16[4,64,128]{2,1,0:T(8,128)(2,1)S(1)}, u32[]{:S(2)}, u32[]{:S(2)}) %collective-permute-start.13) | collective-permute-done | bytes 65568 | tf_op jit(solution)/shard_map/ppermute | solution.py:301
  93.7 0.8 fusion
  95.2 1.5 %collective-permute-start.15 = (bf16[4,64,128]{2,1,0:T(8,128)(2,1)S(1)}, bf16[4,64,128]{2,1,0:T(8,128)(2,1)S(1)}, u32[]{:S(2)}, u32[]{:S(2)}) collective-permute-start(bf16[4,64,128]{2,1,0:T(8,128)(2,1)S(1)} %get-tuple-element.41), channel_id=1, source_target_pairs={{0,128},{16,144},{32,160},{48,176},{64,192},{80,208},{96,224},{112... | collective-permute-start | bytes 196616 | tf_op jit(solution)/shard_map/ppermute | solution.py:301
  97.0 1.6 %collective-permute-done.16.refs_6_ = bf16[4,64,128]{2,1,0:T(8,128)(2,1)S(1)} collective-permute-done((bf16[4,64,128]{2,1,0:T(8,128)(2,1)S(1)}, bf16[4,64,128]{2,1,0:T(8,128)(2,1)S(1)}, u32[]{:S(2)}, u32[]{:S(2)}) %collective-permute-start.16) | collective-permute-done | bytes 65568 | tf_op jit(solution)/shard_map/ppermute | solution.py:301
  98.6 1.9 %collective-permute-done.15.refs_5_ = bf16[4,64,128]{2,1,0:T(8,128)(2,1)S(1)} collective-permute-done((bf16[4,64,128]{2,1,0:T(8,128)(2,1)S(1)}, bf16[4,64,128]{2,1,0:T(8,128)(2,1)S(1)}, u32[]{:S(2)}, u32[]{:S(2)}) %collective-permute-start.15) | collective-permute-done | bytes 65568 | tf_op jit(solution)/shard_map/ppermute | solution.py:301
  100.5 1.3 %collective-permute-done.14.refs_4_ = bf16[4,64,128]{2,1,0:T(8,128)(2,1)S(1)} collective-permute-done((bf16[4,64,128]{2,1,0:T(8,128)(2,1)S(1)}, bf16[4,64,128]{2,1,0:T(8,128)(2,1)S(1)}, u32[]{:S(2)}, u32[]{:S(2)}) %collective-permute-start.14) | collective-permute-done | bytes 65568 | tf_op jit(solution)/shard_map/ppermute | solution.py:301
  101.8 1.3 %out.1 = bf16[128,1024]{1,0:T(8,128)(2,1)} custom-call(s32[1]{0:T(128)} %bitcast.core_ref.refs_10_.place_ref, bf16[4,64,128]{2,1,0:T(8,128)(2,1)S(1)} %copy-done.3, bf16[4,64,128]{2,1,0:T(8,128)(2,1)S(1)} %collective-permute-done.11.refs_1_, bf16[4,64,128]{2,1,0:T(8,128)(2,1)S(1)} %collective-permute-done.12.refs_2_, ...), custom_call_target="tpu_custom_call" | custom-call | tf_op jit(solution)/shard_map/out/pallas_call | solution.py:353
  (59 shorter events, 7.8 us)
Async XLA Ops:
  0.6 21.1 %collective-permute-start = (bf16[3,64,1024]{2,1,0:T(8,128)(2,1)}, bf16[3,64,1024]{2,1,0:T(8,128)(2,1)S(1)}, u32[]{:S(2)}, u32[]{:S(2)}) collective-permute-start(bf16[3,64,1024]{2,1,0:T(8,128)(2,1)} %bitcast.24), channel_id=1, source_target_pairs={{0,16},{16,0},{32,48},{48,32},{64,80},{80,64},{96,112},{112,96},{1... | collective-permute-start | bytes 1179656 | tf_op jit(solution)/shard_map/ppermute | solution.py:301
  5.7 18.6 %all-to-all-start = ((bf16[16,12,128]{2,1,0:T(8,128)(2,1)}), bf16[16,12,128]{2,1,0:T(8,128)(2,1)S(1)}, u32[]{:S(2)}, u32[]{:S(2)}) async-start(bf16[16,12,128]{2,1,0:T(8,128)(2,1)} %copy.19), calls=%async_computation | async-start | bytes 131072 | tf_op jit(solution)/shard_map/all_to_all | solution.py:304
  21.7 13.6 %copy-start.7 = (bf16[3,64,1024]{2,1,0:T(8,128)(2,1)}, bf16[3,64,1024]{2,1,0:T(8,128)(2,1)S(1)}, u32[]{:S(2)}) copy-start(bf16[3,64,1024]{2,1,0:T(8,128)(2,1)S(1)} %collective-permute-done.refs_9_.refs_13_) | copy-start | bytes 1179652
  29.6 2.7 %collective-permute-start.1 = (bf16[64,1024]{1,0:T(8,128)(2,1)}, bf16[64,1024]{1,0:T(8,128)(2,1)S(1)}, u32[]{:S(2)}, u32[]{:S(2)}) collective-permute-start(bf16[64,1024]{1,0:T(8,128)(2,1)} %get-tuple-element.26), channel_id=1, source_target_pairs={{0,16},{16,0},{32,48},{48,32},{64,80},{80,64},{96,112},{112,96},{1... | collective-permute-start | bytes 393224 | tf_op jit(solution)/shard_map/ppermute | solution.py:301
  32.4 23.1 %copy-start.6 = (bf16[128,1024]{1,0:T(8,128)(2,1)}, bf16[128,1024]{1,0:T(8,128)(2,1)S(1)}, u32[]{:S(2)}) copy-start(bf16[128,1024]{1,0:T(8,128)(2,1)S(1)} %constant_dynamic-update-slice_fusion.refs_0_) | copy-start | bytes 786436
  32.4 9.2 %collective-permute-start.3 = (bf16[128,1024]{1,0:T(8,128)(2,1)S(1)}, bf16[128,1024]{1,0:T(8,128)(2,1)S(1)}, u32[]{:S(2)}, u32[]{:S(2)}) collective-permute-start(bf16[128,1024]{1,0:T(8,128)(2,1)S(1)} %constant_dynamic-update-slice_fusion.refs_0_), channel_id=1, source_target_pairs={{0,192},{16,208},{32,224},{48,240},{64,0},{80,16},{96,32},{112,48}... | collective-permute-start | bytes 786440 | tf_op jit(solution)/shard_map/ppermute | solution.py:301
  34.9 9.3 %collective-permute-start.2 = (bf16[128,1024]{1,0:T(8,128)(2,1)S(1)}, bf16[128,1024]{1,0:T(8,128)(2,1)S(1)}, u32[]{:S(2)}, u32[]{:S(2)}) collective-permute-start(bf16[128,1024]{1,0:T(8,128)(2,1)S(1)} %constant_dynamic-update-slice_fusion.refs_0_), channel_id=1, source_target_pairs={{0,64},{16,80},{32,96},{48,112},{64,128},{80,144},{96,160},{112,17... | collective-permute-start | bytes 786440 | tf_op jit(solution)/shard_map/ppermute | solution.py:301
  34.9 9.5 %collective-permute-start.4 = (bf16[128,1024]{1,0:T(8,128)(2,1)S(1)}, bf16[128,1024]{1,0:T(8,128)(2,1)S(1)}, u32[]{:S(2)}, u32[]{:S(2)}) collective-permute-start(bf16[128,1024]{1,0:T(8,128)(2,1)S(1)} %constant_dynamic-update-slice_fusion.refs_0_), channel_id=1, source_target_pairs={{0,32},{16,48},{32,0},{48,16},{64,96},{80,112},{96,64},{112,80},{1... | collective-permute-start | bytes 786440 | tf_op jit(solution)/shard_map/ppermute | solution.py:301
  35.3 13.8 %all-to-all-start.1 = ((bf16[16,64,128]{2,1,0:T(8,128)(2,1)}), bf16[16,64,128]{2,1,0:T(8,128)(2,1)S(1)}, u32[]{:S(2)}, u32[]{:S(2)}) async-start(bf16[16,64,128]{2,1,0:T(8,128)(2,1)} %get-tuple-element.28), calls=%async_computation.1 | async-start | bytes 524288 | tf_op jit(solution)/shard_map/all_to_all | solution.py:329
  41.6 13.9 %copy-start.4 = (bf16[128,1024]{1,0:T(8,128)(2,1)}, bf16[128,1024]{1,0:T(8,128)(2,1)S(1)}, u32[]{:S(2)}) copy-start(bf16[128,1024]{1,0:T(8,128)(2,1)S(1)} %collective-permute-done.3.refs_2_) | copy-start | bytes 786436
  41.6 7.9 %collective-permute-start.6 = (bf16[64,1024]{1,0:T(8,128)(2,1)S(1)}, bf16[64,1024]{1,0:T(8,128)(2,1)S(1)}, u32[]{:S(2)}, u32[]{:S(2)}) collective-permute-start(bf16[64,1024]{1,0:T(8,128)(2,1)S(1)} %slice.21), channel_id=1, source_target_pairs={{0,192},{16,208},{32,224},{48,240},{64,0},{80,16},{96,32},{112,48}... | collective-permute-start | bytes 393224 | tf_op jit(solution)/shard_map/ppermute | solution.py:301
  44.3 11.2 %copy-start.5 = (bf16[128,1024]{1,0:T(8,128)(2,1)}, bf16[128,1024]{1,0:T(8,128)(2,1)S(1)}, u32[]{:S(2)}) copy-start(bf16[128,1024]{1,0:T(8,128)(2,1)S(1)} %collective-permute-done.2.refs_1_) | copy-start | bytes 786436
  44.3 6.0 %collective-permute-start.5 = (bf16[64,1024]{1,0:T(8,128)(2,1)S(1)}, bf16[64,1024]{1,0:T(8,128)(2,1)S(1)}, u32[]{:S(2)}, u32[]{:S(2)}) collective-permute-start(bf16[64,1024]{1,0:T(8,128)(2,1)S(1)} %slice.20), channel_id=1, source_target_pairs={{0,64},{16,80},{32,96},{48,112},{64,128},{80,144},{96,160},{112,17... | collective-permute-start | bytes 393224 | tf_op jit(solution)/shard_map/ppermute | solution.py:301
  44.4 11.1 %copy-start.8 = (bf16[128,1024]{1,0:T(8,128)(2,1)}, bf16[128,1024]{1,0:T(8,128)(2,1)S(1)}, u32[]{:S(2)}) copy-start(bf16[128,1024]{1,0:T(8,128)(2,1)S(1)} %collective-permute-done.4.refs_3_) | copy-start | bytes 786436
  44.4 10.7 %collective-permute-start.8 = (bf16[128,1024]{1,0:T(8,128)(2,1)S(1)}, bf16[128,1024]{1,0:T(8,128)(2,1)S(1)}, u32[]{:S(2)}, u32[]{:S(2)}) collective-permute-start(bf16[128,1024]{1,0:T(8,128)(2,1)S(1)} %collective-permute-done.4.refs_3_), channel_id=1, source_target_pairs={{0,192},{16,208},{32,224},{48,240},{64,0},{80,16},{96,32},{112,48}... | collective-permute-start | bytes 786440 | tf_op jit(solution)/shard_map/ppermute | solution.py:301
  47.1 8.4 %collective-permute-start.7 = (bf16[128,1024]{1,0:T(8,128)(2,1)S(1)}, bf16[128,1024]{1,0:T(8,128)(2,1)S(1)}, u32[]{:S(2)}, u32[]{:S(2)}) collective-permute-start(bf16[128,1024]{1,0:T(8,128)(2,1)S(1)} %collective-permute-done.4.refs_3_), channel_id=1, source_target_pairs={{0,64},{16,80},{32,96},{48,112},{64,128},{80,144},{96,160},{112,17... | collective-permute-start | bytes 786440 | tf_op jit(solution)/shard_map/ppermute | solution.py:301
  49.1 12.1 %copy-start.11 = (bf16[16,64,128]{2,1,0:T(8,128)(2,1)}, bf16[16,64,128]{2,1,0:T(8,128)(2,1)S(1)}, u32[]{:S(2)}) copy-start(bf16[16,64,128]{2,1,0:T(8,128)(2,1)S(1)} %all-to-all-done.1) | copy-start | bytes 786436
  49.6 6.0 %copy-start.12 = (bf16[64,1024]{1,0:T(8,128)(2,1)}, bf16[64,1024]{1,0:T(8,128)(2,1)S(1)}, u32[]{:S(2)}) copy-start(bf16[64,1024]{1,0:T(8,128)(2,1)S(1)} %collective-permute-done.6.refs_5_) | copy-start | bytes 393220
  50.3 5.2 %copy-start.13 = (bf16[64,1024]{1,0:T(8,128)(2,1)}, bf16[64,1024]{1,0:T(8,128)(2,1)S(1)}, u32[]{:S(2)}) copy-start(bf16[64,1024]{1,0:T(8,128)(2,1)S(1)} %collective-permute-done.5.refs_4_) | copy-start | bytes 393220
  50.3 10.8 %collective-permute-start.9 = (bf16[64,1024]{1,0:T(8,128)(2,1)S(1)}, bf16[64,1024]{1,0:T(8,128)(2,1)S(1)}, u32[]{:S(2)}, u32[]{:S(2)}) collective-permute-start(bf16[64,1024]{1,0:T(8,128)(2,1)S(1)} %collective-permute-done.5.refs_4_), channel_id=1, source_target_pairs={{0,32},{16,48},{32,0},{48,16},{64,96},{80,112},{96,64},{112,80},{1... | collective-permute-start | bytes 393224 | tf_op jit(solution)/shard_map/ppermute | solution.py:301
  51.7 9.5 %collective-permute-start.10 = (bf16[64,1024]{1,0:T(8,128)(2,1)S(1)}, bf16[64,1024]{1,0:T(8,128)(2,1)S(1)}, u32[]{:S(2)}, u32[]{:S(2)}) collective-permute-start(bf16[64,1024]{1,0:T(8,128)(2,1)S(1)} %collective-permute-done.6.refs_5_), channel_id=1, source_target_pairs={{0,32},{16,48},{32,0},{48,16},{64,96},{80,112},{96,64},{112,80},{1... | collective-permute-start | bytes 393224 | tf_op jit(solution)/shard_map/ppermute | solution.py:301
  61.9 39.9 %copy-start.1 = (f32[128,1024]{1,0:T(8,128)S(1)}, f32[128,1024]{1,0:T(8,128)}, u32[]{:S(2)}) copy-start(f32[128,1024]{1,0:T(8,128)} %get-tuple-element.37.refs_8_) | copy-start | bytes 1572868
  75.7 26.1 %copy-start = (bf16[1024,1024]{1,0:T(8,128)(2,1)S(1)}, bf16[1024,1024]{1,0:T(8,128)(2,1)}, u32[]{:S(2)}) copy-start(bf16[1024,1024]{1,0:T(8,128)(2,1)} %refs_7_.1) | copy-start | bytes 6291460
  75.7 3.3 %collective-permute-start.17 = (bf16[16,96,128]{2,1,0:T(8,128)(2,1)}, bf16[16,96,128]{2,1,0:T(8,128)(2,1)S(1)}, u32[]{:S(2)}, u32[]{:S(2)}) collective-permute-start(bf16[16,96,128]{2,1,0:T(8,128)(2,1)} %get-tuple-element.39), channel_id=1, source_target_pairs={{0,16},{16,0},{32,48},{48,32},{64,80},{80,64},{96,112},{112,96},{1... | collective-permute-start | bytes 1179656 | tf_op jit(solution)/shard_map/ppermute | solution.py:301
  80.0 21.8 %copy-start.3 = (bf16[4,64,128]{2,1,0:T(8,128)(2,1)S(1)}, bf16[4,64,128]{2,1,0:T(8,128)(2,1)}, u32[]{:S(2)}) copy-start(bf16[4,64,128]{2,1,0:T(8,128)(2,1)} %get-tuple-element.33.refs_0_) | copy-start | bytes 196612
  80.8 22.2 %all-to-all-start.2 = ((bf16[16,96,128]{2,1,0:T(8,128)(2,1)}), bf16[16,96,128]{2,1,0:T(8,128)(2,1)S(1)}, u32[]{:S(2)}, u32[]{:S(2)}) async-start(bf16[16,96,128]{2,1,0:T(8,128)(2,1)} %add.1), calls=%async_computation.2 | async-start | bytes 786432 | tf_op jit(solution)/shard_map/all_to_all | solution.py:350
  86.6 2.5 %collective-permute-start.11 = (bf16[4,64,128]{2,1,0:T(8,128)(2,1)}, bf16[4,64,128]{2,1,0:T(8,128)(2,1)S(1)}, u32[]{:S(2)}, u32[]{:S(2)}) collective-permute-start(bf16[4,64,128]{2,1,0:T(8,128)(2,1)} %get-tuple-element.34), channel_id=1, source_target_pairs={{0,16},{16,0},{32,48},{48,32},{64,80},{80,64},{96,112},{112,96},{1... | collective-permute-start | bytes 196616 | tf_op jit(solution)/shard_map/ppermute | solution.py:301
  87.3 3.9 %collective-permute-start.12 = (bf16[4,64,128]{2,1,0:T(8,128)(2,1)}, bf16[4,64,128]{2,1,0:T(8,128)(2,1)S(1)}, u32[]{:S(2)}, u32[]{:S(2)}) collective-permute-start(bf16[4,64,128]{2,1,0:T(8,128)(2,1)} %get-tuple-element.35), channel_id=1, source_target_pairs={{0,32},{16,48},{32,0},{48,16},{64,96},{80,112},{96,64},{112,80},{1... | collective-permute-start | bytes 196616 | tf_op jit(solution)/shard_map/ppermute | solution.py:301
  87.8 5.8 %collective-permute-start.13 = (bf16[4,64,128]{2,1,0:T(8,128)(2,1)}, bf16[4,64,128]{2,1,0:T(8,128)(2,1)S(1)}, u32[]{:S(2)}, u32[]{:S(2)}) collective-permute-start(bf16[4,64,128]{2,1,0:T(8,128)(2,1)} %get-tuple-element.36), channel_id=1, source_target_pairs={{0,48},{16,32},{32,16},{48,0},{64,112},{80,96},{96,80},{112,64},{1... | collective-permute-start | bytes 196616 | tf_op jit(solution)/shard_map/ppermute | solution.py:301
  94.4 4.1 %collective-permute-start.16 = (bf16[4,64,128]{2,1,0:T(8,128)(2,1)S(1)}, bf16[4,64,128]{2,1,0:T(8,128)(2,1)S(1)}, u32[]{:S(2)}, u32[]{:S(2)}) collective-permute-start(bf16[4,64,128]{2,1,0:T(8,128)(2,1)S(1)} %get-tuple-element.40), channel_id=1, source_target_pairs={{0,192},{16,208},{32,224},{48,240},{64,0},{80,16},{96,32},{112,48}... | collective-permute-start | bytes 196616 | tf_op jit(solution)/shard_map/ppermute | solution.py:301
  95.2 5.3 %collective-permute-start.15 = (bf16[4,64,128]{2,1,0:T(8,128)(2,1)S(1)}, bf16[4,64,128]{2,1,0:T(8,128)(2,1)S(1)}, u32[]{:S(2)}, u32[]{:S(2)}) collective-permute-start(bf16[4,64,128]{2,1,0:T(8,128)(2,1)S(1)} %get-tuple-element.41), channel_id=1, source_target_pairs={{0,128},{16,144},{32,160},{48,176},{64,192},{80,208},{96,224},{112... | collective-permute-start | bytes 196616 | tf_op jit(solution)/shard_map/ppermute | solution.py:301
  96.7 5.1 %collective-permute-start.14 = (bf16[4,64,128]{2,1,0:T(8,128)(2,1)S(1)}, bf16[4,64,128]{2,1,0:T(8,128)(2,1)S(1)}, u32[]{:S(2)}, u32[]{:S(2)}) collective-permute-start(bf16[4,64,128]{2,1,0:T(8,128)(2,1)S(1)} %get-tuple-element.42), channel_id=1, source_target_pairs={{0,64},{16,80},{32,96},{48,112},{64,128},{80,144},{96,160},{112,17... | collective-permute-start | bytes 196616 | tf_op jit(solution)/shard_map/ppermute | solution.py:301
  (6 other events, 4.4 us)

commit v4 on v3

--- a/solution.py
+++ b/solution.py
@@ -169,33 +169,20 @@
     return pairs
 
 
-def project_kernel(*refs):
-    pieces = refs[:PIECES - 2]
-    own_w_ref, other_w_ref, out_ref, x_ref, sems = refs[PIECES - 2:]
+def attention_kernel(*refs):
+    pieces = refs[:PIECES]
+    place_ref, own_w_ref, other_w_ref, grad_ctx_ref, own_ref, other_ref = refs[PIECES:PIECES + 6]
+    part_refs = refs[PIECES + 6:PIECES + 10]
+    x_ref, context_ref, q_ref, k_ref, v_ref, rows_ref, sems = refs[PIECES + 10:]
+    place = place_ref[0]
+    core = place % 2
+    rows_at = lambda dx, dy, s: pl.ds(pl.multiple_of(chip_at(place, dx, dy) * 128 + jnp.abs(core - s) * ROWS, ROWS), ROWS)
+    offsets = [rows_at(4 - dx, dy, s) for dx, dy in STEPS for s in range(2)]
     copies = fetch(gather_rows(pieces, x_ref), sems)
     weight = jnp.concatenate([w for i in range(3) for w in (own_w_ref[i], other_w_ref[i])], axis=0)
     for copy in copies:
         copy.wait()
-    out_ref[...] = mm(x_ref[...], weight, NT).astype(BF16)
-
-
-def attention_kernel(*refs):
-    pieces = refs[:PIECES]
-    place_ref, projected_hbm, own_w_ref, other_w_ref, grad_ctx_ref, own_ref, other_ref = refs[PIECES:PIECES + 7]
-    part_refs = refs[PIECES + 7:PIECES + 11]
-    x_ref, projected_ref, context_ref, q_ref, k_ref, v_ref, rows_ref, sems = refs[PIECES + 11:]
-    place = place_ref[0]
-    core = place % 2
-    rows_at = lambda dx, dy, s: pl.ds(pl.multiple_of(chip_at(place, dx, dy) * 128 + jnp.abs(core - s) * ROWS, ROWS), ROWS)
-    offsets = [rows_at(4 - dx, dy, s) for dx, dy in STEPS for s in range(2)]
-    done = D - 2 * ROWS
-    pairs = gather_rows(pieces, x_ref)
-    copies = fetch([(projected_hbm, projected_ref.at[pl.ds(0, done)])] + pairs[-2:] + pairs[:-2], sems)
-    weight = jnp.concatenate([w for i in range(3) for w in (own_w_ref[i], other_w_ref[i])], axis=0)
-    for copy in copies[:3]:
-        copy.wait()
-    projected_ref[done:, :] = mm(x_ref[done:, :], weight, NT).astype(BF16)
-    projected = projected_ref[...]
+    projected = mm(x_ref[...], weight, NT).astype(BF16)
     for i in range(H):
         rows = offsets[i]
         here = projected[i * ROWS:(i + 1) * ROWS]
@@ -229,8 +216,6 @@
     rows_ref[:, 128:256] = jnp.concatenate([dq[:, HD:], dk[:, HD:]], axis=1)
     rows_ref[:, 256:] = dv
     order = jnp.concatenate([rows_ref[rows, :] for rows in offsets], axis=0)
-    for copy in copies[3:]:
-        copy.wait()
     grad = mm(x_ref[...], order, TN).astype(BF16)
     for j in range(H):
         top = grad[j * ROWS:j * ROWS + ROWS // 2, 256:]
@@ -336,14 +321,10 @@
     pieces = [here, left, right, across, far0, far1, left1, right1, far2, far3]
     grad_ctx = grad_ctx.reshape(D, 128)
     tall, quarter = pltpu.VMEM((D, 128), BF16), shape((4, ROWS, 128), BF16)
-    projected = call(
-        project_kernel, shape((D - 2 * ROWS, 384), BF16), [ANY] * (PIECES - 2) + [VM] * 2, "project",
-        [pltpu.VMEM((D - 2 * ROWS, D), BF16), pltpu.SemaphoreType.DMA((PIECES - 2,))],
-    )(*pieces[:-2], own_weight, other_weight)
     own, other, *parts = call(
-        attention_kernel, (shape((H, 96, 128), BF16),) * 2 + (quarter,) * 4, [ANY] * PIECES + [SM, ANY] + [VM] * 3, "attention",
-        [pltpu.VMEM((D, D), BF16), pltpu.VMEM((D, 384), BF16)] + [tall] * 4 + [pltpu.VMEM((D, 384), BF16), pltpu.SemaphoreType.DMA((PIECES + 1,))],
-    )(*pieces, place.reshape(1), projected, own_weight, other_weight, grad_ctx)
+        attention_kernel, (shape((H, 96, 128), BF16),) * 2 + (quarter,) * 4, [ANY] * PIECES + [SM] + [VM] * 3, "attention",
+        [pltpu.VMEM((D, D), BF16)] + [tall] * 4 + [pltpu.VMEM((D, 384), BF16), pltpu.SemaphoreType.DMA((PIECES,))],
+    )(*pieces, place.reshape(1), own_weight, other_weight, grad_ctx)
     partial_grad = call(add_kernel, shape((H, 96, 128), BF16), [VM] * 2, "add", mib=4)(own, move(other, pair))
     swap = lambda a, dy, dc: move(a, [(i, i ^ (2 * dy + dc)) for i in range(16)])
     near = [parts[0], swap(parts[1], 0, 1), swap(parts[2], 1, 0), swap(parts[3], 1, 1)]

time: 105 us -> 103 us (0.981)
  Pallas kernels: 32.9 us -> 29.5 us
  starting transfers between devices: 42.6 us -> 43.9 us
  waiting for transfers between devices: 20.7 us -> 21.8 us
    pallas_call x1 -> x0, Pallas kernels: 4.58 us -> none  [on_device(): call(project_kernel, shape((D - 2 * ROWS, 384), BF16), [ANY] * (PIECES -...]
    ppermute x18, starting transfers between devices: 21.4 us -> 22.8 us  [on_device(): move = lambda a, perm: lax.ppermute(a, 'patch', perm)]
    pallas_call x1, Pallas kernels: 13.8 us -> 15 us  [on_device(): call(attention_kernel, (shape((H, 96, 128), BF16),) * 2 + (quarter,) * 4,...]
    ppermute x18, waiting for transfers between devices: 16.2 us -> 17.3 us  [on_device(): move = lambda a, perm: lax.ppermute(a, 'patch', perm)]
  transfers between devices with their start and end apart: 21 -> 21, of which waited for: 13 -> 13; matrix products, arithmetic and copies ran while one was open for 3% -> 3% of each run, Pallas kernels for 12% -> 8%
where the time goes in v4:
time: 103 us
  starting transfers between devices  43.9 us (43%)
  Pallas kernels  29.5 us (29%)
  waiting for transfers between devices  21.8 us (21%)
  local copies, waits for them, and re-layouts  5.73 us (6%)
    ppermute x18, starting transfers between devices, on_device(): move = lambda a, perm: lax.ppermute(a, 'patch', perm)  22.8 us
    ppermute x18, waiting for transfers between devices, on_device(): move = lambda a, perm: lax.ppermute(a, 'patch', perm)  17.3 us
    pallas_call x1, Pallas kernels, on_device(): call(attention_kernel, (shape((H, 96, 128), BF16),) * 2 + (quarter,) * 4,...  15 us
    all_to_all x1, starting transfers between devices, on_device(): owned = lax.all_to_all(sent, 'var', split_axis=0, concat_axis=0, tiled=True)  9.18 us
    pallas_call x1, Pallas kernels, on_device(): call(prep_kernel, (shape((V * PIX, 256), BF16), shape((V * (PIX + 1), H),...  6.86 us
    all_to_all x1, starting transfers between devices, on_device(): lax.all_to_all(grad_parts, 'patch', split_axis=0, concat_axis=0, tiled=True)  6.23 us
    all_to_all x1, starting transfers between devices, on_device(): lax.all_to_all(partial_grad, 'var', split_axis=0, concat_axis=0, tiled=True)  5.74 us
    pallas_call x1, Pallas kernels, on_device(): call(token_kernel, (shape((2 * ROWS, D), F32), shape((ROWS, D), BF16), sh...  4.73 us
  transfers between devices with their start and end apart: 21, of which 13 were waited for; matrix products, arithmetic and copies ran while one was open for 3% of the time, Pallas kernels for 8%

profile of v4, /device:TPU:1, one launch (start us, length us, event | category | flops | bytes accessed | tf_op | source)
XLA Modules:
  0.0 102.6 jit_solution(16968225302043137068)
XLA Ops:
  0.6 3.3 %collective-permute-start = (bf16[3,64,1024]{2,1,0:T(8,128)(2,1)}, bf16[3,64,1024]{2,1,0:T(8,128)(2,1)S(1)}, u32[]{:S(2)}, u32[]{:S(2)}) collective-permute-start(bf16[3,64,1024]{2,1,0:T(8,128)(2,1)} %bitcast.26), channel_id=1, source_target_pairs={{0,16},{16,0},{32,48},{48,32},{64,80},{80,64},{96,112},{112,96},{1... | collective-permute-start | bytes 1179656 | tf_op jit(solution)/shard_map/ppermute | solution.py:286
  4.0 1.0 copy.21
  5.7 9.2 %all-to-all-start = ((bf16[16,12,128]{2,1,0:T(8,128)(2,1)}), bf16[16,12,128]{2,1,0:T(8,128)(2,1)S(1)}, u32[]{:S(2)}, u32[]{:S(2)}) async-start(bf16[16,12,128]{2,1,0:T(8,128)(2,1)} %copy.19), calls=%async_computation | async-start | bytes 131072 | tf_op jit(solution)/shard_map/all_to_all | solution.py:289
  14.9 6.9 %prep.1 = (bf16[192,256]{1,0:T(8,128)(2,1)}, f32[240,16]{1,0:T(8,128)}, bf16[16,64,128]{2,1,0:T(8,128)(2,1)}, bf16[16,128,240]{2,1,0:T(8,128)(2,1)}) custom-call(s32[48]{0:T(128)} %ids_ref.1, bf16[1024]{0:T(1024)(128)(2,1)} %query_ref.1, bf16[48,1024]{1,0:T(8,128)(2,1)} %var_embed_ref.1, bf16[48,4,1024]{2,1,0:T(4,128)(2,1)} %embed_hbm.1, ...), custom_call_target="tpu_custom_call" | custom-call | tf_op jit(solution)/shard_map/prep/pallas_call | solution.py:292
  21.8 2.5 %all-to-all-done.fields_ref = bf16[16,12,128]{2,1,0:T(8,128)(2,1)S(1)} async-done(((bf16[16,12,128]{2,1,0:T(8,128)(2,1)}), bf16[16,12,128]{2,1,0:T(8,128)(2,1)S(1)}, u32[]{:S(2)}, u32[]{:S(2)}) %all-to-all-start) | async-done | bytes 49184 | tf_op jit(solution)/shard_map/all_to_all | solution.py:289
  24.9 4.7 %tokens.1 = (f32[128,1024]{1,0:T(8,128)}, bf16[64,1024]{1,0:T(8,128)(2,1)}, bf16[64,1024]{1,0:T(8,128)(2,1)}) custom-call(bf16[192,256]{1,0:T(8,128)(2,1)} %get-tuple-element.21.place_ref, bf16[16,12,128]{2,1,0:T(8,128)(2,1)} %copy-done.12, f32[240,16]{1,0:T(8,128)} %get-tuple-element.22.score_ref, bf16[16,128,240]{2,1,0:T(8,128)(2,1)} %get-tuple-element.24.table_hbm, ...), custom_call_target="tpu_custom_call" | custom-call | tf_op jit(solution)/shard_map/tokens/pallas_call | solution.py:303
  29.6 1.5 %collective-permute-start.1 = (bf16[64,1024]{1,0:T(8,128)(2,1)}, bf16[64,1024]{1,0:T(8,128)(2,1)S(1)}, u32[]{:S(2)}, u32[]{:S(2)}) collective-permute-start(bf16[64,1024]{1,0:T(8,128)(2,1)} %get-tuple-element.26), channel_id=1, source_target_pairs={{0,16},{16,0},{32,48},{48,32},{64,80},{80,64},{96,112},{112,96},{1... | collective-permute-start | bytes 393224 | tf_op jit(solution)/shard_map/ppermute | solution.py:286
  31.2 0.9 constant_dynamic-update-slice_fusion.1
  32.4 2.6 %collective-permute-start.3 = (bf16[128,1024]{1,0:T(8,128)(2,1)S(1)}, bf16[128,1024]{1,0:T(8,128)(2,1)S(1)}, u32[]{:S(2)}, u32[]{:S(2)}) collective-permute-start(bf16[128,1024]{1,0:T(8,128)(2,1)S(1)} %constant_dynamic-update-slice_fusion.refs_0_), channel_id=1, source_target_pairs={{0,192},{16,208},{32,224},{48,240},{64,0},{80,16},{96,32},{112,48}... | collective-permute-start | bytes 786440 | tf_op jit(solution)/shard_map/ppermute | solution.py:286
  35.4 6.2 %all-to-all-start.1 = ((bf16[16,64,128]{2,1,0:T(8,128)(2,1)}), bf16[16,64,128]{2,1,0:T(8,128)(2,1)S(1)}, u32[]{:S(2)}, u32[]{:S(2)}) async-start(bf16[16,64,128]{2,1,0:T(8,128)(2,1)} %get-tuple-element.28), calls=%async_computation.1 | async-start | bytes 524288 | tf_op jit(solution)/shard_map/all_to_all | solution.py:314
  41.6 2.7 %collective-permute-start.6 = (bf16[64,1024]{1,0:T(8,128)(2,1)S(1)}, bf16[64,1024]{1,0:T(8,128)(2,1)S(1)}, u32[]{:S(2)}, u32[]{:S(2)}) collective-permute-start(bf16[64,1024]{1,0:T(8,128)(2,1)S(1)} %slice.21), channel_id=1, source_target_pairs={{0,192},{16,208},{32,224},{48,240},{64,0},{80,16},{96,32},{112,48}... | collective-permute-start | bytes 393224 | tf_op jit(solution)/shard_map/ppermute | solution.py:286
  44.4 2.6 %collective-permute-start.8 = (bf16[128,1024]{1,0:T(8,128)(2,1)S(1)}, bf16[128,1024]{1,0:T(8,128)(2,1)S(1)}, u32[]{:S(2)}, u32[]{:S(2)}) collective-permute-start(bf16[128,1024]{1,0:T(8,128)(2,1)S(1)} %collective-permute-done.4.refs_3_), channel_id=1, source_target_pairs={{0,192},{16,208},{32,224},{48,240},{64,0},{80,16},{96,32},{112,48}... | collective-permute-start | bytes 786440 | tf_op jit(solution)/shard_map/ppermute | solution.py:286
  47.1 2.0 %all-to-all-done.1 = bf16[16,64,128]{2,1,0:T(8,128)(2,1)S(1)} async-done(((bf16[16,64,128]{2,1,0:T(8,128)(2,1)}), bf16[16,64,128]{2,1,0:T(8,128)(2,1)S(1)}, u32[]{:S(2)}, u32[]{:S(2)}) %all-to-all-start.1) | async-done | bytes 262176 | tf_op jit(solution)/shard_map/all_to_all | solution.py:314
  49.6 0.8 collective-permute-done.5.refs_4_
  50.4 1.4 %collective-permute-start.9 = (bf16[64,1024]{1,0:T(8,128)(2,1)S(1)}, bf16[64,1024]{1,0:T(8,128)(2,1)S(1)}, u32[]{:S(2)}, u32[]{:S(2)}) collective-permute-start(bf16[64,1024]{1,0:T(8,128)(2,1)S(1)} %collective-permute-done.5.refs_4_), channel_id=1, source_target_pairs={{0,32},{16,48},{32,0},{48,16},{64,96},{80,112},{96,64},{112,80},{1... | collective-permute-start | bytes 393224 | tf_op jit(solution)/shard_map/ppermute | solution.py:286
  51.8 2.6 %collective-permute-done.9.refs_8_ = bf16[64,1024]{1,0:T(8,128)(2,1)S(1)} collective-permute-done((bf16[64,1024]{1,0:T(8,128)(2,1)S(1)}, bf16[64,1024]{1,0:T(8,128)(2,1)S(1)}, u32[]{:S(2)}, u32[]{:S(2)}) %collective-permute-start.9) | collective-permute-done | bytes 131104 | tf_op jit(solution)/shard_map/ppermute | solution.py:286
  54.5 1.7 %collective-permute-done.10.refs_9_ = bf16[64,1024]{1,0:T(8,128)(2,1)S(1)} collective-permute-done((bf16[64,1024]{1,0:T(8,128)(2,1)S(1)}, bf16[64,1024]{1,0:T(8,128)(2,1)S(1)}, u32[]{:S(2)}, u32[]{:S(2)}) %collective-permute-start.10) | collective-permute-done | bytes 131104 | tf_op jit(solution)/shard_map/ppermute | solution.py:286
  57.7 15.0 %attention.1 = (bf16[16,96,128]{2,1,0:T(8,128)(2,1)}, bf16[16,96,128]{2,1,0:T(8,128)(2,1)}, bf16[4,64,128]{2,1,0:T(8,128)(2,1)}, bf16[4,64,128]{2,1,0:T(8,128)(2...) custom-call(bf16[128,1024]{1,0:T(8,128)(2,1)} %copy-done.7, bf16[128,1024]{1,0:T(8,128)(2,1)} %copy-done.6, ...), custom_call_target="tpu_custom_call" | custom-call | tf_op jit(solution)/shard_map/attention/pallas_call | solution.py:324
  72.7 3.0 %collective-permute-start.17 = (bf16[16,96,128]{2,1,0:T(8,128)(2,1)}, bf16[16,96,128]{2,1,0:T(8,128)(2,1)S(1)}, u32[]{:S(2)}, u32[]{:S(2)}) collective-permute-start(bf16[16,96,128]{2,1,0:T(8,128)(2,1)} %get-tuple-element.39), channel_id=1, source_target_pairs={{0,16},{16,0},{32,48},{48,32},{64,80},{80,64},{96,112},{112,96},{1... | collective-permute-start | bytes 1179656 | tf_op jit(solution)/shard_map/ppermute | solution.py:286
  75.7 1.6 %collective-permute-done.17.b_ref = bf16[16,96,128]{2,1,0:T(8,128)(2,1)S(1)} collective-permute-done((bf16[16,96,128]{2,1,0:T(8,128)(2,1)}, bf16[16,96,128]{2,1,0:T(8,128)(2,1)S(1)}, u32[]{:S(2)}, u32[]{:S(2)}) %collective-permute-start.17) | collective-permute-done | bytes 393248 | tf_op jit(solution)/shard_map/ppermute | solution.py:286
  77.3 1.0 copy-done.2
  78.2 0.8 add.1
  79.1 5.7 %all-to-all-start.2 = ((bf16[16,96,128]{2,1,0:T(8,128)(2,1)}), bf16[16,96,128]{2,1,0:T(8,128)(2,1)S(1)}, u32[]{:S(2)}, u32[]{:S(2)}) async-start(bf16[16,96,128]{2,1,0:T(8,128)(2,1)} %add.1), calls=%async_computation.2 | async-start | bytes 786432 | tf_op jit(solution)/shard_map/all_to_all | solution.py:331
  86.2 1.1 %collective-permute-start.13 = (bf16[4,64,128]{2,1,0:T(8,128)(2,1)}, bf16[4,64,128]{2,1,0:T(8,128)(2,1)S(1)}, u32[]{:S(2)}, u32[]{:S(2)}) collective-permute-start(bf16[4,64,128]{2,1,0:T(8,128)(2,1)} %get-tuple-element.36), channel_id=1, source_target_pairs={{0,48},{16,32},{32,16},{48,0},{64,112},{80,96},{96,80},{112,64},{1... | collective-permute-start | bytes 196616 | tf_op jit(solution)/shard_map/ppermute | solution.py:286
  87.3 2.1 %collective-permute-done.12.refs_2_ = bf16[4,64,128]{2,1,0:T(8,128)(2,1)S(1)} collective-permute-done((bf16[4,64,128]{2,1,0:T(8,128)(2,1)}, bf16[4,64,128]{2,1,0:T(8,128)(2,1)S(1)}, u32[]{:S(2)}, u32[]{:S(2)}) %collective-permute-start.12) | collective-permute-done | bytes 65568 | tf_op jit(solution)/shard_map/ppermute | solution.py:286
  89.4 2.5 %collective-permute-done.13.refs_3_ = bf16[4,64,128]{2,1,0:T(8,128)(2,1)S(1)} collective-permute-done((bf16[4,64,128]{2,1,0:T(8,128)(2,1)}, bf16[4,64,128]{2,1,0:T(8,128)(2,1)S(1)}, u32[]{:S(2)}, u32[]{:S(2)}) %collective-permute-start.13) | collective-permute-done | bytes 65568 | tf_op jit(solution)/shard_map/ppermute | solution.py:286
  92.7 1.1 %collective-permute-start.16 = (bf16[4,64,128]{2,1,0:T(8,128)(2,1)S(1)}, bf16[4,64,128]{2,1,0:T(8,128)(2,1)S(1)}, u32[]{:S(2)}, u32[]{:S(2)}) collective-permute-start(bf16[4,64,128]{2,1,0:T(8,128)(2,1)S(1)} %get-tuple-element.40), channel_id=1, source_target_pairs={{0,192},{16,208},{32,224},{48,240},{64,0},{80,16},{96,32},{112,48}... | collective-permute-start | bytes 196616 | tf_op jit(solution)/shard_map/ppermute | solution.py:286
  93.8 1.3 %collective-permute-start.15 = (bf16[4,64,128]{2,1,0:T(8,128)(2,1)S(1)}, bf16[4,64,128]{2,1,0:T(8,128)(2,1)S(1)}, u32[]{:S(2)}, u32[]{:S(2)}) collective-permute-start(bf16[4,64,128]{2,1,0:T(8,128)(2,1)S(1)} %get-tuple-element.41), channel_id=1, source_target_pairs={{0,128},{16,144},{32,160},{48,176},{64,192},{80,208},{96,224},{112... | collective-permute-start | bytes 196616 | tf_op jit(solution)/shard_map/ppermute | solution.py:286
  95.3 1.5 %collective-permute-done.16.refs_6_ = bf16[4,64,128]{2,1,0:T(8,128)(2,1)S(1)} collective-permute-done((bf16[4,64,128]{2,1,0:T(8,128)(2,1)S(1)}, bf16[4,64,128]{2,1,0:T(8,128)(2,1)S(1)}, u32[]{:S(2)}, u32[]{:S(2)}) %collective-permute-start.16) | collective-permute-done | bytes 65568 | tf_op jit(solution)/shard_map/ppermute | solution.py:286
  96.8 2.3 %collective-permute-done.15.refs_5_ = bf16[4,64,128]{2,1,0:T(8,128)(2,1)S(1)} collective-permute-done((bf16[4,64,128]{2,1,0:T(8,128)(2,1)S(1)}, bf16[4,64,128]{2,1,0:T(8,128)(2,1)S(1)}, u32[]{:S(2)}, u32[]{:S(2)}) %collective-permute-start.15) | collective-permute-done | bytes 65568 | tf_op jit(solution)/shard_map/ppermute | solution.py:286
  99.1 1.4 %collective-permute-done.14.refs_4_ = bf16[4,64,128]{2,1,0:T(8,128)(2,1)S(1)} collective-permute-done((bf16[4,64,128]{2,1,0:T(8,128)(2,1)S(1)}, bf16[4,64,128]{2,1,0:T(8,128)(2,1)S(1)}, u32[]{:S(2)}, u32[]{:S(2)}) %collective-permute-start.14) | collective-permute-done | bytes 65568 | tf_op jit(solution)/shard_map/ppermute | solution.py:286
  100.6 1.3 %out.1 = bf16[128,1024]{1,0:T(8,128)(2,1)} custom-call(s32[1]{0:T(128)} %bitcast.core_ref.refs_10_.place_ref, bf16[4,64,128]{2,1,0:T(8,128)(2,1)S(1)} %copy-done.3, bf16[4,64,128]{2,1,0:T(8,128)(2,1)S(1)} %collective-permute-done.11.refs_1_, bf16[4,64,128]{2,1,0:T(8,128)(2,1)S(1)} %collective-permute-done.12.refs_2_, ...), custom_call_target="tpu_custom_call" | custom-call | tf_op jit(solution)/shard_map/out/pallas_call | solution.py:334
  (58 shorter events, 7.4 us)
Async XLA Ops:
  0.6 21.1 %collective-permute-start = (bf16[3,64,1024]{2,1,0:T(8,128)(2,1)}, bf16[3,64,1024]{2,1,0:T(8,128)(2,1)S(1)}, u32[]{:S(2)}, u32[]{:S(2)}) collective-permute-start(bf16[3,64,1024]{2,1,0:T(8,128)(2,1)} %bitcast.26), channel_id=1, source_target_pairs={{0,16},{16,0},{32,48},{48,32},{64,80},{80,64},{96,112},{112,96},{1... | collective-permute-start | bytes 1179656 | tf_op jit(solution)/shard_map/ppermute | solution.py:286
  5.7 18.6 %all-to-all-start = ((bf16[16,12,128]{2,1,0:T(8,128)(2,1)}), bf16[16,12,128]{2,1,0:T(8,128)(2,1)S(1)}, u32[]{:S(2)}, u32[]{:S(2)}) async-start(bf16[16,12,128]{2,1,0:T(8,128)(2,1)} %copy.19), calls=%async_computation | async-start | bytes 131072 | tf_op jit(solution)/shard_map/all_to_all | solution.py:289
  21.7 13.6 %copy-start.8 = (bf16[3,64,1024]{2,1,0:T(8,128)(2,1)}, bf16[3,64,1024]{2,1,0:T(8,128)(2,1)S(1)}, u32[]{:S(2)}) copy-start(bf16[3,64,1024]{2,1,0:T(8,128)(2,1)S(1)} %collective-permute-done.refs_12_) | copy-start | bytes 1179652
  29.6 2.7 %collective-permute-start.1 = (bf16[64,1024]{1,0:T(8,128)(2,1)}, bf16[64,1024]{1,0:T(8,128)(2,1)S(1)}, u32[]{:S(2)}, u32[]{:S(2)}) collective-permute-start(bf16[64,1024]{1,0:T(8,128)(2,1)} %get-tuple-element.26), channel_id=1, source_target_pairs={{0,16},{16,0},{32,48},{48,32},{64,80},{80,64},{96,112},{112,96},{1... | collective-permute-start | bytes 393224 | tf_op jit(solution)/shard_map/ppermute | solution.py:286
  32.4 23.8 %copy-start.7 = (bf16[128,1024]{1,0:T(8,128)(2,1)}, bf16[128,1024]{1,0:T(8,128)(2,1)S(1)}, u32[]{:S(2)}) copy-start(bf16[128,1024]{1,0:T(8,128)(2,1)S(1)} %constant_dynamic-update-slice_fusion.refs_0_) | copy-start | bytes 786436
  32.4 9.2 %collective-permute-start.3 = (bf16[128,1024]{1,0:T(8,128)(2,1)S(1)}, bf16[128,1024]{1,0:T(8,128)(2,1)S(1)}, u32[]{:S(2)}, u32[]{:S(2)}) collective-permute-start(bf16[128,1024]{1,0:T(8,128)(2,1)S(1)} %constant_dynamic-update-slice_fusion.refs_0_), channel_id=1, source_target_pairs={{0,192},{16,208},{32,224},{48,240},{64,0},{80,16},{96,32},{112,48}... | collective-permute-start | bytes 786440 | tf_op jit(solution)/shard_map/ppermute | solution.py:286
  35.0 9.3 %collective-permute-start.2 = (bf16[128,1024]{1,0:T(8,128)(2,1)S(1)}, bf16[128,1024]{1,0:T(8,128)(2,1)S(1)}, u32[]{:S(2)}, u32[]{:S(2)}) collective-permute-start(bf16[128,1024]{1,0:T(8,128)(2,1)S(1)} %constant_dynamic-update-slice_fusion.refs_0_), channel_id=1, source_target_pairs={{0,64},{16,80},{32,96},{48,112},{64,128},{80,144},{96,160},{112,17... | collective-permute-start | bytes 786440 | tf_op jit(solution)/shard_map/ppermute | solution.py:286
  35.0 9.5 %collective-permute-start.4 = (bf16[128,1024]{1,0:T(8,128)(2,1)S(1)}, bf16[128,1024]{1,0:T(8,128)(2,1)S(1)}, u32[]{:S(2)}, u32[]{:S(2)}) collective-permute-start(bf16[128,1024]{1,0:T(8,128)(2,1)S(1)} %constant_dynamic-update-slice_fusion.refs_0_), channel_id=1, source_target_pairs={{0,32},{16,48},{32,0},{48,16},{64,96},{80,112},{96,64},{112,80},{1... | collective-permute-start | bytes 786440 | tf_op jit(solution)/shard_map/ppermute | solution.py:286
  35.4 13.8 %all-to-all-start.1 = ((bf16[16,64,128]{2,1,0:T(8,128)(2,1)}), bf16[16,64,128]{2,1,0:T(8,128)(2,1)S(1)}, u32[]{:S(2)}, u32[]{:S(2)}) async-start(bf16[16,64,128]{2,1,0:T(8,128)(2,1)} %get-tuple-element.28), calls=%async_computation.1 | async-start | bytes 524288 | tf_op jit(solution)/shard_map/all_to_all | solution.py:314
  41.6 16.1 %copy-start.5 = (bf16[128,1024]{1,0:T(8,128)(2,1)}, bf16[128,1024]{1,0:T(8,128)(2,1)S(1)}, u32[]{:S(2)}) copy-start(bf16[128,1024]{1,0:T(8,128)(2,1)S(1)} %collective-permute-done.3.refs_2_) | copy-start | bytes 786436
  41.6 7.9 %collective-permute-start.6 = (bf16[64,1024]{1,0:T(8,128)(2,1)S(1)}, bf16[64,1024]{1,0:T(8,128)(2,1)S(1)}, u32[]{:S(2)}, u32[]{:S(2)}) collective-permute-start(bf16[64,1024]{1,0:T(8,128)(2,1)S(1)} %slice.21), channel_id=1, source_target_pairs={{0,192},{16,208},{32,224},{48,240},{64,0},{80,16},{96,32},{112,48}... | collective-permute-start | bytes 393224 | tf_op jit(solution)/shard_map/ppermute | solution.py:286
  44.3 13.3 %copy-start.6 = (bf16[128,1024]{1,0:T(8,128)(2,1)}, bf16[128,1024]{1,0:T(8,128)(2,1)S(1)}, u32[]{:S(2)}) copy-start(bf16[128,1024]{1,0:T(8,128)(2,1)S(1)} %collective-permute-done.2.refs_1_) | copy-start | bytes 786436
  44.3 6.0 %collective-permute-start.5 = (bf16[64,1024]{1,0:T(8,128)(2,1)S(1)}, bf16[64,1024]{1,0:T(8,128)(2,1)S(1)}, u32[]{:S(2)}, u32[]{:S(2)}) collective-permute-start(bf16[64,1024]{1,0:T(8,128)(2,1)S(1)} %slice.20), channel_id=1, source_target_pairs={{0,64},{16,80},{32,96},{48,112},{64,128},{80,144},{96,160},{112,17... | collective-permute-start | bytes 393224 | tf_op jit(solution)/shard_map/ppermute | solution.py:286
  44.4 11.8 %copy-start.9 = (bf16[128,1024]{1,0:T(8,128)(2,1)}, bf16[128,1024]{1,0:T(8,128)(2,1)S(1)}, u32[]{:S(2)}) copy-start(bf16[128,1024]{1,0:T(8,128)(2,1)S(1)} %collective-permute-done.4.refs_3_) | copy-start | bytes 786436
  44.4 11.8 %collective-permute-start.8 = (bf16[128,1024]{1,0:T(8,128)(2,1)S(1)}, bf16[128,1024]{1,0:T(8,128)(2,1)S(1)}, u32[]{:S(2)}, u32[]{:S(2)}) collective-permute-start(bf16[128,1024]{1,0:T(8,128)(2,1)S(1)} %collective-permute-done.4.refs_3_), channel_id=1, source_target_pairs={{0,192},{16,208},{32,224},{48,240},{64,0},{80,16},{96,32},{112,48}... | collective-permute-start | bytes 786440 | tf_op jit(solution)/shard_map/ppermute | solution.py:286
  47.1 9.1 %collective-permute-start.7 = (bf16[128,1024]{1,0:T(8,128)(2,1)S(1)}, bf16[128,1024]{1,0:T(8,128)(2,1)S(1)}, u32[]{:S(2)}, u32[]{:S(2)}) collective-permute-start(bf16[128,1024]{1,0:T(8,128)(2,1)S(1)} %collective-permute-done.4.refs_3_), channel_id=1, source_target_pairs={{0,64},{16,80},{32,96},{48,112},{64,128},{80,144},{96,160},{112,17... | collective-permute-start | bytes 786440 | tf_op jit(solution)/shard_map/ppermute | solution.py:286
  49.1 8.5 %copy-start.4 = (bf16[16,64,128]{2,1,0:T(8,128)(2,1)}, bf16[16,64,128]{2,1,0:T(8,128)(2,1)S(1)}, u32[]{:S(2)}) copy-start(bf16[16,64,128]{2,1,0:T(8,128)(2,1)S(1)} %all-to-all-done.1) | copy-start | bytes 786436
  49.6 6.7 %copy-start.13 = (bf16[64,1024]{1,0:T(8,128)(2,1)}, bf16[64,1024]{1,0:T(8,128)(2,1)S(1)}, u32[]{:S(2)}) copy-start(bf16[64,1024]{1,0:T(8,128)(2,1)S(1)} %collective-permute-done.6.refs_5_) | copy-start | bytes 393220
  50.4 5.9 %copy-start.14 = (bf16[64,1024]{1,0:T(8,128)(2,1)}, bf16[64,1024]{1,0:T(8,128)(2,1)S(1)}, u32[]{:S(2)}) copy-start(bf16[64,1024]{1,0:T(8,128)(2,1)S(1)} %collective-permute-done.5.refs_4_) | copy-start | bytes 393220
  50.4 4.1 %collective-permute-start.9 = (bf16[64,1024]{1,0:T(8,128)(2,1)S(1)}, bf16[64,1024]{1,0:T(8,128)(2,1)S(1)}, u32[]{:S(2)}, u32[]{:S(2)}) collective-permute-start(bf16[64,1024]{1,0:T(8,128)(2,1)S(1)} %collective-permute-done.5.refs_4_), channel_id=1, source_target_pairs={{0,32},{16,48},{32,0},{48,16},{64,96},{80,112},{96,64},{112,80},{1... | collective-permute-start | bytes 393224 | tf_op jit(solution)/shard_map/ppermute | solution.py:286
  51.7 4.5 %collective-permute-start.10 = (bf16[64,1024]{1,0:T(8,128)(2,1)S(1)}, bf16[64,1024]{1,0:T(8,128)(2,1)S(1)}, u32[]{:S(2)}, u32[]{:S(2)}) collective-permute-start(bf16[64,1024]{1,0:T(8,128)(2,1)S(1)} %collective-permute-done.6.refs_5_), channel_id=1, source_target_pairs={{0,32},{16,48},{32,0},{48,16},{64,96},{80,112},{96,64},{112,80},{1... | collective-permute-start | bytes 393224 | tf_op jit(solution)/shard_map/ppermute | solution.py:286
  57.7 42.9 %copy-start = (bf16[1024,1024]{1,0:T(8,128)(2,1)S(1)}, bf16[1024,1024]{1,0:T(8,128)(2,1)}, u32[]{:S(2)}) copy-start(bf16[1024,1024]{1,0:T(8,128)(2,1)} %refs_7_.1) | copy-start | bytes 6291460
  57.7 42.9 %copy-start.1 = (f32[128,1024]{1,0:T(8,128)S(1)}, f32[128,1024]{1,0:T(8,128)}, u32[]{:S(2)}) copy-start(f32[128,1024]{1,0:T(8,128)} %get-tuple-element.37.refs_8_) | copy-start | bytes 1572868
  72.7 4.5 %collective-permute-start.17 = (bf16[16,96,128]{2,1,0:T(8,128)(2,1)}, bf16[16,96,128]{2,1,0:T(8,128)(2,1)S(1)}, u32[]{:S(2)}, u32[]{:S(2)}) collective-permute-start(bf16[16,96,128]{2,1,0:T(8,128)(2,1)} %get-tuple-element.39), channel_id=1, source_target_pairs={{0,16},{16,0},{32,48},{48,32},{64,80},{80,64},{96,112},{112,96},{1... | collective-permute-start | bytes 1179656 | tf_op jit(solution)/shard_map/ppermute | solution.py:286
  78.2 22.3 %copy-start.3 = (bf16[4,64,128]{2,1,0:T(8,128)(2,1)S(1)}, bf16[4,64,128]{2,1,0:T(8,128)(2,1)}, u32[]{:S(2)}) copy-start(bf16[4,64,128]{2,1,0:T(8,128)(2,1)} %get-tuple-element.33.refs_0_) | copy-start | bytes 196612
  79.1 22.7 %all-to-all-start.2 = ((bf16[16,96,128]{2,1,0:T(8,128)(2,1)}), bf16[16,96,128]{2,1,0:T(8,128)(2,1)S(1)}, u32[]{:S(2)}, u32[]{:S(2)}) async-start(bf16[16,96,128]{2,1,0:T(8,128)(2,1)} %add.1), calls=%async_computation.2 | async-start | bytes 786432 | tf_op jit(solution)/shard_map/all_to_all | solution.py:331
  84.8 2.5 %collective-permute-start.11 = (bf16[4,64,128]{2,1,0:T(8,128)(2,1)}, bf16[4,64,128]{2,1,0:T(8,128)(2,1)S(1)}, u32[]{:S(2)}, u32[]{:S(2)}) collective-permute-start(bf16[4,64,128]{2,1,0:T(8,128)(2,1)} %get-tuple-element.34), channel_id=1, source_target_pairs={{0,16},{16,0},{32,48},{48,32},{64,80},{80,64},{96,112},{112,96},{1... | collective-permute-start | bytes 196616 | tf_op jit(solution)/shard_map/ppermute | solution.py:286
  85.6 3.9 %collective-permute-start.12 = (bf16[4,64,128]{2,1,0:T(8,128)(2,1)}, bf16[4,64,128]{2,1,0:T(8,128)(2,1)S(1)}, u32[]{:S(2)}, u32[]{:S(2)}) collective-permute-start(bf16[4,64,128]{2,1,0:T(8,128)(2,1)} %get-tuple-element.35), channel_id=1, source_target_pairs={{0,32},{16,48},{32,0},{48,16},{64,96},{80,112},{96,64},{112,80},{1... | collective-permute-start | bytes 196616 | tf_op jit(solution)/shard_map/ppermute | solution.py:286
  86.2 5.7 %collective-permute-start.13 = (bf16[4,64,128]{2,1,0:T(8,128)(2,1)}, bf16[4,64,128]{2,1,0:T(8,128)(2,1)S(1)}, u32[]{:S(2)}, u32[]{:S(2)}) collective-permute-start(bf16[4,64,128]{2,1,0:T(8,128)(2,1)} %get-tuple-element.36), channel_id=1, source_target_pairs={{0,48},{16,32},{32,16},{48,0},{64,112},{80,96},{96,80},{112,64},{1... | collective-permute-start | bytes 196616 | tf_op jit(solution)/shard_map/ppermute | solution.py:286
  92.7 4.1 %collective-permute-start.16 = (bf16[4,64,128]{2,1,0:T(8,128)(2,1)S(1)}, bf16[4,64,128]{2,1,0:T(8,128)(2,1)S(1)}, u32[]{:S(2)}, u32[]{:S(2)}) collective-permute-start(bf16[4,64,128]{2,1,0:T(8,128)(2,1)S(1)} %get-tuple-element.40), channel_id=1, source_target_pairs={{0,192},{16,208},{32,224},{48,240},{64,0},{80,16},{96,32},{112,48}... | collective-permute-start | bytes 196616 | tf_op jit(solution)/shard_map/ppermute | solution.py:286
  93.8 5.3 %collective-permute-start.15 = (bf16[4,64,128]{2,1,0:T(8,128)(2,1)S(1)}, bf16[4,64,128]{2,1,0:T(8,128)(2,1)S(1)}, u32[]{:S(2)}, u32[]{:S(2)}) collective-permute-start(bf16[4,64,128]{2,1,0:T(8,128)(2,1)S(1)} %get-tuple-element.41), channel_id=1, source_target_pairs={{0,128},{16,144},{32,160},{48,176},{64,192},{80,208},{96,224},{112... | collective-permute-start | bytes 196616 | tf_op jit(solution)/shard_map/ppermute | solution.py:286
  95.0 5.5 %collective-permute-start.14 = (bf16[4,64,128]{2,1,0:T(8,128)(2,1)S(1)}, bf16[4,64,128]{2,1,0:T(8,128)(2,1)S(1)}, u32[]{:S(2)}, u32[]{:S(2)}) collective-permute-start(bf16[4,64,128]{2,1,0:T(8,128)(2,1)S(1)} %get-tuple-element.42), channel_id=1, source_target_pairs={{0,64},{16,80},{32,96},{48,112},{64,128},{80,144},{96,160},{112,17... | collective-permute-start | bytes 196616 | tf_op jit(solution)/shard_map/ppermute | solution.py:286
  (6 other events, 7.7 us)
